TPU v7x, 128 devices: a whole 4x4x4 slice. The times are simulated.
128 devices in a mesh: fsdp: 8 (over y, z_lo), seq: 16 (over x, z_hi, core).
Axes of the slice: x: 4, y: 4, z: 4 (z_hi: 2, z_lo: 2; z = z_hi * 2 + z_lo), core: 2. Of those that a mesh axis runs over, the one named last changes fastest.
Arguments:
- inputs: bfloat16 [32768, 1024], P(('fsdp', 'seq')), may hold values from -6 to 6
- cotangent: bfloat16 [32768, 1024], P(('fsdp', 'seq')), may hold values from -6 to 6
- ln_attn_gain: bfloat16 [1024], P('fsdp'), may hold values from 0.099609375 to 1.8984375
- ln_attn_bias: bfloat16 [1024], P('fsdp'), may hold values from -3 to 3
- ln_mlp_gain: bfloat16 [1024], P('fsdp'), may hold values from 0.099609375 to 1.8984375
- ln_mlp_bias: bfloat16 [1024], P('fsdp'), may hold values from -3 to 3
- qkv_weight: bfloat16 [1024, 3072], P('fsdp'), may hold values from -0.25 to 0.25
- qkv_bias: bfloat16 [3072], P('fsdp'), may hold values from -3 to 3
- dense_weight: bfloat16 [1024, 1024], P('fsdp'), may hold values from -1.5 to 1.5
- dense_bias: bfloat16 [1024], P('fsdp'), may hold values from -3 to 3
- hidden_weight: bfloat16 [1024, 4096], P('fsdp'), may hold values from -0.1875 to 0.1875
- hidden_bias: bfloat16 [4096], P('fsdp'), may hold values from -3 to 3
- output_weight: bfloat16 [4096, 1024], P('fsdp'), may hold values from -0.09375 to 0.09375
- output_bias: bfloat16 [1024], P('fsdp'), may hold values from -3 to 3
Outputs:
- outputs: bfloat16 [32768, 1024], P(('fsdp', 'seq'))
- input_grad: float32 [32768, 1024], P(('fsdp', 'seq'))
- ln_attn_gain_grad: float32 [1024], P('fsdp')
- ln_attn_bias_grad: float32 [1024], P('fsdp')
- ln_mlp_gain_grad: float32 [1024], P('fsdp')
- ln_mlp_bias_grad: float32 [1024], P('fsdp')
- qkv_weight_grad: float32 [1024, 3072], P('fsdp')
- qkv_bias_grad: float32 [3072], P('fsdp')
- dense_weight_grad: float32 [1024, 1024], P('fsdp')
- dense_bias_grad: float32 [1024], P('fsdp')
- hidden_weight_grad: float32 [1024, 4096], P('fsdp')
- hidden_bias_grad: float32 [4096], P('fsdp')
- output_weight_grad: float32 [4096, 1024], P('fsdp')
- output_bias_grad: float32 [1024], P('fsdp')
All inputs are finite; a program needn't handle non-finite values.
Results may differ from a plain program's by a relative error of at most 0.023.
Values may be sent and summed in bfloat16 or wider, within the bound.
A program may use at most 256 MiB of HBM per device.

v0:
```python
import functools
import math

import jax
import jax.numpy as jnp
from jax import lax
from jax.experimental import pallas as pl
from jax.experimental.pallas import tpu as pltpu
from jax.sharding import PartitionSpec as P

D = 1024
FF = 4096
HEADS = 16
HEAD = 64
ROT = 16
CHIP_TOKENS = 512
FSDP = 8
CHIPS = 8

epsilon = 1e-05
F32 = jnp.float32
BF16 = jnp.bfloat16
NT = (((1,), (1,)), ((), ()))
TN = (((0,), (0,)), ((), ()))
MIB = 2**20
HBM = pl.BlockSpec(memory_space=pl.ANY)
VMEM = pl.BlockSpec(memory_space=pltpu.VMEM)


def place():
    f = lax.axis_index("fsdp")
    s = lax.axis_index("seq")
    return f, s, (f // 2, f % 2, s // 4, (s // 2) % 2, s % 2)


def device(y, z, x, core):
    return {"fsdp": y * 2 + z % 2, "seq": x * 4 + (z // 2) * 2 + core}


def barrier(devices):
    sem = pltpu.get_barrier_semaphore()
    for d in devices:
        pl.semaphore_signal(sem, inc=1, device_id=d, device_id_type=pl.DeviceIdType.MESH)
    pl.semaphore_wait(sem, len(devices))


def remote(src, dst, send, recv, target):
    return pltpu.make_async_remote_copy(
        src_ref=src,
        dst_ref=dst,
        send_sem=send,
        recv_sem=recv,
        device_id=target,
        device_id_type=pl.DeviceIdType.MESH,
    )


class Gather:
    def __init__(self, own, full, send, recv):
        f, s, (y, zl, px, zh, core) = place()
        z = zh * 2 + zl
        self.own, self.full, self.send, self.recv = own, full, send, recv
        self.yp = device((y + 1) % 4, z, px, core)
        self.ym = device((y + 3) % 4, z, px, core)
        self.zp = device(y, (z + 1) % 4, px, core)
        self.zm = device(y, (z + 3) % 4, px, core)
        self.f = f
        self.slots = [f, (f + 6) % 8, (f + 2) % 8, (f + 4) % 8]
        flip = f + 1 - 2 * zl
        self.far = [flip, (flip + 6) % 8, (flip + 2) % 8, (flip + 4) % 8]
        self.sends = []

    def neighbours(self):
        return [self.yp, self.ym, self.zp, self.zm]

    def started(self, src, dst, k, target):
        copy = remote(src, dst, self.send.at[k], self.recv.at[k], target)
        copy.start()
        self.sends.append(copy)

    def arrived(self, ref, k):
        remote(ref, ref, self.send.at[k], self.recv.at[k], self.yp).wait_recv()

    @staticmethod
    def part(ref, h):
        rows = ref.shape[0] // 2
        return ref.at[pl.ds(h * rows, rows)]

    def own_y(self):
        for n, (o, g) in enumerate(zip(self.own, self.full)):
            for k, h, target in ((0, 0, self.yp), (3, 1, self.ym), (2, 0, self.ym), (1, 1, self.yp)):
                self.started(self.part(o, h), self.part(g.at[self.f], h), 14 * n + k, target)

    def own_z(self):
        for n, (o, g) in enumerate(zip(self.own, self.full)):
            for k, h, target in ((6, 0, self.zp), (10, 1, self.zm)):
                self.started(self.part(o, h), self.part(g.at[self.f], h), 14 * n + k, target)

    def pass_on(self, n, k, slot, h, targets):
        ref = self.part(self.full[n].at[slot], h)
        self.arrived(ref, 14 * n + k)
        for kk, target in targets:
            self.started(ref, ref, 14 * n + kk, target)

    def near(self):
        for n in range(len(self.full)):
            self.pass_on(n, 0, self.slots[1], 0, [(4, self.yp), (7, self.zp)])
            self.pass_on(n, 3, self.slots[2], 1, [(5, self.ym), (12, self.zm)])
            self.pass_on(n, 2, self.slots[2], 0, [(8, self.zp)])
            self.pass_on(n, 1, self.slots[1], 1, [(11, self.zm)])

    def opposite(self):
        for n in range(len(self.full)):
            self.pass_on(n, 4, self.slots[3], 0, [(9, self.zp)])
            self.pass_on(n, 5, self.slots[3], 1, [(13, self.zm)])

    def finish(self):
        for n, g in enumerate(self.full):
            for j in range(4):
                self.arrived(self.part(g.at[self.far[j]], 0), 14 * n + 6 + j)
                self.arrived(self.part(g.at[self.far[j]], 1), 14 * n + 10 + j)
        for copy in self.sends:
            copy.wait_send()


def gather_kernel(wq, wd, small, x, ct, gq, gd, gs, gx, gc, send, recv, local_sem):
    f, s, (y, zl, px, zh, core) = place()
    sibling = device(y, zh * 2 + zl, px, 1 - core)
    others = [{"fsdp": (f + k) % 8, "seq": s} for k in range(1, 8)]
    zother = device(y, 2 * (1 - zh) + 1 - zl, px, core)
    own = [wq, wd.at[pl.ds(pl.multiple_of(core * 64, 64), 64)]]
    weights = Gather(own, [gq, gd], send, recv)
    barrier(others + [sibling, zother])
    base = 28
    weights.own_y()
    weights.started(x, gx.at[core], base, sibling)
    weights.started(ct, gc.at[core], base + 1, sibling)
    for k in range(1, 8):
        weights.started(small, gs.at[f], base + 1 + k, others[k - 1])
    weights.own_z()
    pairs = [(gx.at[core], x), (gc.at[core], ct), (gs.at[f], small), (gq.at[f], own[0]), (gd.at[f], own[1])]
    keeps = []
    for k, (b, a) in enumerate(pairs):
        copy = pltpu.make_async_copy(a, b, local_sem.at[k])
        copy.start()
        keeps.append(copy)
    weights.near()
    weights.opposite()
    weights.arrived(gx.at[1 - core], base)
    weights.arrived(gc.at[1 - core], base + 1)
    for k in range(1, 8):
        weights.arrived(gs.at[(f + 8 - k) % 8], base + 1 + k)
    weights.finish()
    for copy in keeps:
        copy.wait()


def gather(wq, wd, small, x, ct):
    def shape(*dims):
        return jax.ShapeDtypeStruct(dims, BF16)

    return pl.pallas_call(
        gather_kernel,
        out_shape=(
            shape(8, 128, 1536),
            shape(8, 64, 1024),
            shape(8, 16, 128),
            shape(2, 256, 1024),
            shape(2, 256, 1024),
        ),
        in_specs=[HBM] * 5,
        out_specs=(HBM,) * 5,
        scratch_shapes=[
            pltpu.SemaphoreType.DMA((37,)),
            pltpu.SemaphoreType.DMA((37,)),
            pltpu.SemaphoreType.DMA((5,)),
        ],
        compiler_params=pltpu.CompilerParams(collective_id=0, has_side_effects=True),
    )(wq, wd, small, x, ct)


def fold(op, a):
    result = a[:, :128]
    for j in range(128, a.shape[1], 128):
        result = op(result, a[:, j : j + 128])
    return result


def attention_kernel(
    packed, wh, wo, result, gh, go,
    hd, out, q_s, k_s, v_s, d_s, s_s, p_s, dk_s, dv_s, mx_s, l_s, o_s, dq_s,
    in_send, in_recv, out_send, out_recv, g_send, g_recv, local_sem,
):
    f, s, (y, zl, px, zh, core) = place()
    me = s // 2
    B = CHIP_TOKENS
    n = CHIPS
    scale = 1.0 / math.sqrt(HEAD)
    own = [wh, wo.at[pl.ds(pl.multiple_of(core * 256, 256), 256)]]
    weights = Gather(own, [gh, go], g_send, g_recv)

    def chip(j):
        return {"fsdp": f, "seq": j * 2 + core}

    barrier([chip((me + k) % n) for k in range(1, n)] + weights.neighbours())
    given = []
    for k in range(1, n):
        j = (me + k) % n
        copy = remote(packed.at[j], hd.at[me], in_send.at[k], in_recv.at[k], chip(j))
        copy.start()
        given.append(copy)
    weights.own_y()
    keeps = []
    for k, (a, b) in enumerate([(packed.at[me], hd.at[me]), (own[0], gh.at[f]), (own[1], go.at[f])]):
        copy = pltpu.make_async_copy(a, b, local_sem.at[k])
        copy.start()
        keeps.append(copy)
    keeps[0].wait()
    for k in range(1, n):
        ref = hd.at[(me + n - k) % n]
        remote(ref, ref, in_send.at[k], in_recv.at[k], chip(me)).wait_recv()
    weights.own_z()

    def block(i):
        return pl.ds(pl.multiple_of(i * B, B), B)

    def prepare(i, _):
        rows = block(i)
        piece = hd[i]
        q_s[rows, :] = piece[:, 0:64] * jnp.asarray(scale, BF16)
        k_s[rows, :] = piece[:, 64:128]
        v_s[rows, :] = piece[:, 128:192]
        d_s[rows, :] = piece[:, 192:256]
        return 0

    lax.fori_loop(0, n, prepare, 0)
    dk_s[...] = jnp.zeros_like(dk_s)
    dv_s[...] = jnp.zeros_like(dv_s)
    keep = lax.broadcasted_iota(jnp.int32, (B, B), 1) <= lax.broadcasted_iota(
        jnp.int32, (B, B), 0
    )

    def back_to(i):
        return remote(out.at[i], result.at[me], out_send.at[i], out_recv.at[me], chip(i))

    def query_block(t, _):
        i = n - 1 - t
        rows = block(i)
        qi = q_s[rows, :]
        mx_s[...] = jnp.full(mx_s.shape, -1e30, F32)

        def score(kb):
            return lax.dot_general(qi, k_s[block(kb), :], NT, preferred_element_type=F32)

        def first(kb, _):
            scores = score(kb)
            s_s[kb] = scores
            mx_s[...] = jnp.maximum(mx_s[...], fold(jnp.maximum, scores))
            return 0

        lax.fori_loop(0, i, first, 0)
        scores = jnp.where(keep, score(i), -1e30)
        s_s[i] = scores
        row_max = jnp.max(
            jnp.maximum(mx_s[...], fold(jnp.maximum, scores)), axis=1, keepdims=True
        )
        l_s[...] = jnp.zeros_like(l_s)
        o_s[...] = jnp.zeros_like(o_s)
        dq_s[...] = jnp.zeros_like(dq_s)

        def second(kb, _):
            p = jnp.exp(s_s[kb] - row_max)
            l_s[...] += fold(jnp.add, p)
            pb = p.astype(BF16)
            p_s[kb] = pb
            o_s[...] += jnp.dot(pb, v_s[block(kb), :], preferred_element_type=F32)
            return 0

        lax.fori_loop(0, i + 1, second, 0)
        inverse = 1.0 / jnp.sum(l_s[...], axis=1, keepdims=True)
        o = o_s[...] * inverse
        d = (d_s[rows, :].astype(F32) * inverse).astype(BF16)
        delta = jnp.sum(o * d.astype(F32), axis=1, keepdims=True)
        q_t = qi.T
        d_t = d.T

        def third(kb, _):
            cols = block(kb)
            pb = p_s[kb]
            dp = lax.dot_general(d, v_s[cols, :], NT, preferred_element_type=F32)
            ds = (pb.astype(F32) * (dp - delta)).astype(BF16)
            dq_s[...] += jnp.dot(ds, k_s[cols, :], preferred_element_type=F32)
            dk_s[:, cols] += jnp.dot(q_t, ds, preferred_element_type=F32)
            dv_s[:, cols] += jnp.dot(d_t, pb, preferred_element_type=F32)
            return 0

        lax.fori_loop(0, i + 1, third, 0)
        out[i, :, 0:64] = (dq_s[...] * scale).astype(BF16)
        out[i, :, 64:128] = dk_s[:, rows].T.astype(BF16)
        out[i, :, 128:192] = dv_s[:, rows].T.astype(BF16)
        out[i, :, 192:256] = o.astype(BF16)

        @pl.when(i != me)
        def _():
            back_to(i).start()

        @pl.when(i == me)
        def _():
            pltpu.make_async_copy(out.at[i], result.at[i], local_sem.at[3]).start()

        return 0

    lax.fori_loop(0, 1, query_block, 0)
    weights.near()
    lax.fori_loop(1, 2, query_block, 0)
    weights.opposite()
    lax.fori_loop(2, n, query_block, 0)

    for copy in given:
        copy.wait_send()
    keeps[1].wait()
    keeps[2].wait()
    weights.finish()
    for k in range(1, n):
        back_to((me + k) % n).wait_send()
    pltpu.make_async_copy(out.at[me], result.at[me], local_sem.at[3]).wait()
    for k in range(1, n):
        j = (me + k) % n
        ref = result.at[j]
        remote(ref, ref, out_send.at[j], out_recv.at[j], chip(me)).wait_recv()


def attention(packed, wh, wo):
    B = CHIP_TOKENS
    L = CHIPS * B
    return pl.pallas_call(
        attention_kernel,
        out_shape=(
            jax.ShapeDtypeStruct((CHIPS, B, 4 * HEAD), BF16),
            jax.ShapeDtypeStruct((8, 128, 2048), BF16),
            jax.ShapeDtypeStruct((8, 256, 1024), BF16),
        ),
        in_specs=[HBM] * 3,
        out_specs=(HBM,) * 3,
        scratch_shapes=[
            *[pltpu.VMEM((CHIPS, B, 4 * HEAD), BF16)] * 2,
            *[pltpu.VMEM((L, HEAD), BF16)] * 4,
            pltpu.VMEM((L // B, B, B), F32),
            pltpu.VMEM((L // B, B, B), BF16),
            *[pltpu.VMEM((HEAD, L), F32)] * 2,
            *[pltpu.VMEM((B, 128), F32)] * 2,
            *[pltpu.VMEM((B, HEAD), F32)] * 2,
            *[pltpu.SemaphoreType.DMA((CHIPS,))] * 4,
            *[pltpu.SemaphoreType.DMA((28,))] * 2,
            pltpu.SemaphoreType.DMA((4,)),
        ],
        compiler_params=pltpu.CompilerParams(
            collective_id=1, has_side_effects=True, vmem_limit_bytes=56 * MIB
        ),
    )(packed, wh, wo)


ORDERS = ("yzx", "zxy", "xyz")
LEADS = ((2, 4), (2, 4), (4, 2))


def from_input(n, ref, t, h):
    if n == 0:
        return ref.at[t, h]
    if n == 1:
        return ref.at[pl.ds(2 * h, 2), t % 2, t // 2]
    return ref.at[:, h, :, t]


def from_own(n, stage, own, t, h, where):
    y, zl, zh, px = where
    if stage == 1:
        if n == 0:
            return own.at[t % 2, t // 2, pl.ds(2 * h, 2)]
        if n == 1:
            return own.at[h, :, t]
        return own.at[h, t]
    half = own.shape[-1] // 2
    columns = pl.ds(h * half, half)
    if n == 0:
        return own.at[zl, zh, t, :, columns]
    if n == 1:
        return own.at[t // 2, t % 2, px, :, columns]
    return own.at[t % 2, y, t // 2, :, columns]


def add_into(dst, terms):
    lead = tuple(dst.shape[:-2])

    def body(k, _):
        at = []
        for extent in reversed(lead):
            at.insert(0, k % extent)
            k = k // extent
        at = (*at, slice(None), slice(None))
        total = dst[at].astype(F32)
        for t in terms:
            total = total + t[at].astype(F32)
        dst[at] = total.astype(BF16)
        return 0

    lax.fori_loop(0, math.prod(lead), body, 0)


def reduce_kernel(*refs):
    ins, small, outs, small_out = refs[0:3], refs[3], refs[4:7], refs[7]
    scratch = refs[8:]
    bufs = [scratch[9 * n : 9 * n + 9] for n in range(3)]
    (sm_a, sm_b, send, recv, local_sem, sm_send, sm_recv) = scratch[27:]
    f, s, (y, zl, px, zh, core) = place()
    z = zh * 2 + zl
    coordinate = {"y": y, "z": z, "x": px}
    where = (y, zl, zh, px)

    def along(axis, step):
        t = dict(coordinate)
        t[axis] = (t[axis] + step) % 4
        return device(t["y"], t["z"], t["x"], core)

    plus = {a: along(a, 1) for a in "yzx"}
    minus = {a: along(a, 3) for a in "yzx"}
    same_seq = [{"fsdp": (f + k) % 8, "seq": s} for k in range(1, 8)]
    same_fsdp = [{"fsdp": f, "seq": (s + k) % 16} for k in range(1, 16)]
    zother = device(y, 2 * (1 - zh) + 1 - zl, px, core)
    sibling = device(y, z, px, 1 - core)
    barrier(same_seq + same_fsdp + [zother])
    sends = []

    def started(src, dst, k, target):
        copy = remote(src, dst, send.at[k], recv.at[k], target)
        copy.start()
        sends.append(copy)

    def arrived(ref, k):
        remote(ref, ref, send.at[k], recv.at[k], sibling).wait_recv()

    def small_sent(src, dst, k, target):
        copy = remote(src, dst, sm_send.at[k], sm_recv.at[k], target)
        copy.start()
        sends.append(copy)

    def small_arrived(ref, k):
        remote(ref, ref, sm_send.at[k], sm_recv.at[k], sibling).wait_recv()

    for k in range(1, 8):
        small_sent(small.at[(f + k) % 8], sm_a.at[k], k, same_seq[k - 1])

    keeps = []
    for n in range(3):
        axis = ORDERS[n][0]
        p = coordinate[axis]
        src = ins[n]
        opp, fin, mid, own = bufs[n][0:4]
        b = 26 * n
        started(from_input(n, src, (p + 2) % 4, 0), opp.at[0], b, plus[axis])
        started(from_input(n, src, (p + 2) % 4, 1), opp.at[1], b + 1, minus[axis])
        pairs = [
            (from_input(n, src, (p + 1) % 4, 0), mid.at[0]),
            (from_input(n, src, (p + 3) % 4, 1), mid.at[1]),
            (from_input(n, src, p, 0), own.at[0]),
            (from_input(n, src, p, 1), own.at[1]),
        ]
        for k, (a, dst) in enumerate(pairs):
            copy = pltpu.make_async_copy(a, dst, local_sem.at[4 * n + k])
            copy.start()
            keeps.append(copy)
        started(from_input(n, src, (p + 1) % 4, 1), fin.at[0, 1], b + 2, plus[axis])
        started(from_input(n, src, (p + 3) % 4, 0), fin.at[1, 0], b + 3, minus[axis])

    def buffers(n, stage):
        if stage == 0:
            return bufs[n][0], bufs[n][1]
        return bufs[n][2 + 2 * stage], bufs[n][3 + 2 * stage]

    def begin(n, stage):
        axis = ORDERS[n][stage]
        p = coordinate[axis]
        own = bufs[n][3]
        opp, fin = buffers(n, stage)
        b = 26 * n + 6 * stage

        def view(t, h):
            return from_own(n, stage, own, t % 4, h, where)

        started(view(p + 2, 0), opp.at[0], b, plus[axis])
        started(view(p + 2, 1), opp.at[1], b + 1, minus[axis])
        started(view(p + 1, 1), fin.at[0, 1], b + 2, plus[axis])
        started(view(p + 3, 0), fin.at[1, 0], b + 3, minus[axis])

    def relay(n, stage):
        axis = ORDERS[n][stage]
        p = coordinate[axis]
        opp, fin = buffers(n, stage)
        b = 26 * n + 6 * stage
        if stage == 0:
            mids = bufs[n][2].at[0], bufs[n][2].at[1]
        else:
            own = bufs[n][3]
            mids = (
                from_own(n, stage, own, (p + 1) % 4, 0, where),
                from_own(n, stage, own, (p + 3) % 4, 1, where),
            )
        arrived(opp.at[0], b)
        add_into(mids[0], [opp.at[0]])
        started(mids[0], fin.at[0, 0], b + 4, plus[axis])
        arrived(opp.at[1], b + 1)
        add_into(mids[1], [opp.at[1]])
        started(mids[1], fin.at[1, 1], b + 5, minus[axis])

    def finish(n, stage):
        p = coordinate[ORDERS[n][stage]]
        own = bufs[n][3]
        _, fin = buffers(n, stage)
        b = 26 * n + 6 * stage
        arrived(fin.at[0, 1], b + 2)
        arrived(fin.at[1, 0], b + 3)
        arrived(fin.at[0, 0], b + 4)
        arrived(fin.at[1, 1], b + 5)
        for h in range(2):
            mine = own.at[h] if stage == 0 else from_own(n, stage, own, p, h, where)
            add_into(mine, [fin.at[0, h], fin.at[1, h]])

    for n in range(3):
        keeps[4 * n].wait()
        keeps[4 * n + 1].wait()
        relay(n, 0)

    for k in range(1, 8):
        small_arrived(sm_a.at[k], k)
    total = small[f]
    for k in range(1, 8):
        total = total + sm_a[k]
    sm_b[0] = total
    for k in range(1, 16):
        small_sent(sm_b.at[0], sm_b.at[k], 7 + k, same_fsdp[k - 1])

    for n in range(3):
        keeps[4 * n + 2].wait()
        keeps[4 * n + 3].wait()
        finish(n, 0)
        begin(n, 1)
    for n in range(3):
        relay(n, 1)
    for n in range(3):
        finish(n, 1)
        begin(n, 2)
    for n in range(3):
        relay(n, 2)

    chip = px * 2 + zh
    mine = zh * 4 + px
    gathers = []
    for n in range(3):
        finish(n, 2)
        own, out = bufs[n][3], outs[n]
        done = [own.at[zl, zh, px], own.at[y // 2, y % 2, px], own.at[zl, y, zh]][n]
        keep = pltpu.make_async_copy(done, out.at[core, mine], local_sem.at[12 + n])
        keep.start()
        gathers.append(keep)
        for k in range(1, 8):
            j = (chip + k) % 8
            started(done, out.at[core, mine], 26 * n + 17 + k, {"fsdp": f, "seq": j * 2 + core})
    for n in range(3):
        out = outs[n]
        for k in range(1, 8):
            j = (chip + 8 - k) % 8
            arrived(out.at[core, (j % 2) * 4 + j // 2], 26 * n + 17 + k)
        gathers[n].wait()
        started(out.at[core], out.at[core], 26 * n + 25, sibling)
    for k in range(1, 16):
        small_arrived(sm_b.at[k], 7 + k)
    total = sm_b[0]
    for k in range(1, 16):
        total = total + sm_b[k]
    small_out[...] = total
    for n in range(3):
        arrived(outs[n].at[1 - core], 26 * n + 25)
    for copy in sends:
        copy.wait_send()


def reduce_all(parts, small, collective_id):
    scratch = []
    for part, lead in zip(parts, LEADS):
        R, C = part.shape[-2:]
        for dims in (
            (2, *lead, R, C),
            (2, 2, *lead, R, C),
            (2, *lead, R, C),
            (2, *lead, R, C),
            (2, 2, R, C),
            (2, 2, 2, R, C),
            (2, R, C // 2),
            (2, 2, R, C // 2),
        ):
            scratch.append(pltpu.VMEM(dims, BF16))
        scratch.append(pltpu.SemaphoreType.DMA)
    outs = [jax.ShapeDtypeStruct((2, 8, *p.shape[-2:]), BF16) for p in parts]
    return pl.pallas_call(
        reduce_kernel,
        out_shape=(*outs, jax.ShapeDtypeStruct((16, 128), F32)),
        in_specs=[HBM, HBM, HBM, VMEM],
        out_specs=(HBM, HBM, HBM, VMEM),
        scratch_shapes=[
            *scratch,
            pltpu.VMEM((8, 16, 128), F32),
            pltpu.VMEM((16, 16, 128), F32),
            pltpu.SemaphoreType.DMA((78,)),
            pltpu.SemaphoreType.DMA((78,)),
            pltpu.SemaphoreType.DMA((15,)),
            pltpu.SemaphoreType.DMA((23,)),
            pltpu.SemaphoreType.DMA((23,)),
        ],
        compiler_params=pltpu.CompilerParams(
            collective_id=collective_id, has_side_effects=True, vmem_limit_bytes=48 * MIB
        ),
    )(*parts, small)


def turn(values, tables, sign):
    cosine, ahead, behind = tables
    moved = pltpu.roll(values, 120, 1) * ahead + pltpu.roll(values, 8, 1) * behind
    return values * cosine + sign * moved


def front_kernel(x, ct, wq, wd, vectors, bias, tables, packed, attn_out, mlp_out):
    values = x[...].astype(F32)
    centered = values - jnp.mean(values, axis=-1, keepdims=True)
    variance = jnp.mean(centered * centered, axis=-1, keepdims=True)
    normed = centered * lax.rsqrt(variance + epsilon)
    attn_out[...] = (normed * vectors[0:1, :] + vectors[1:2, :]).astype(BF16)
    mlp_out[...] = (normed * vectors[2:3, :] + vectors[3:4, :]).astype(BF16)
    low = lax.broadcasted_iota(jnp.int32, (CHIP_TOKENS, 128), 1) < HEAD
    rotary = (tables[0], tables[1], tables[2])
    for pair in range(4):
        a = attn_out[...]
        qk = slice(pair * 256, pair * 256 + 256)
        vs = slice(1024 + pair * 128, 1024 + pair * 128 + 128)
        projected = jnp.dot(a, wq[:, qk], preferred_element_type=F32) + bias[0:1, qk]
        for j in range(2):
            turned = turn(projected[:, j * 128 : j * 128 + 128], rotary, 1.0)
            packed[2 * pair + j, :, 0:128] = turned.astype(BF16)
        v = jnp.dot(a, wq[:, vs], preferred_element_type=F32) + bias[0:1, vs]
        rows = slice(pair * 128, pair * 128 + 128)
        d = lax.dot_general(ct[...], wd[rows, :], NT, preferred_element_type=F32)
        packed[2 * pair, :, 128:256] = jnp.where(low, v, pltpu.roll(d, 64, 1)).astype(BF16)
        packed[2 * pair + 1, :, 128:256] = jnp.where(low, pltpu.roll(v, 64, 1), d).astype(BF16)


def front(x, ct, wq, wd, vectors, bias, tables):
    T = CHIP_TOKENS
    return pl.pallas_call(
        front_kernel,
        out_shape=(
            jax.ShapeDtypeStruct((8, T, 256), BF16),
            jax.ShapeDtypeStruct((T, D), BF16),
            jax.ShapeDtypeStruct((T, D), BF16),
        ),
        in_specs=[VMEM] * 7,
        out_specs=(VMEM,) * 3,
        compiler_params=pltpu.CompilerParams(vmem_limit_bytes=48 * MIB),
    )(x, ct, wq, wd, vectors, bias, tables)


def back_kernel(packed, tables, grad, attended, bias):
    low = lax.broadcasted_iota(jnp.int32, (CHIP_TOKENS, 128), 1) < HEAD
    rotary = (tables[0], tables[1], tables[2])
    for pair in range(4):
        for j in range(2):
            at = slice((2 * pair + j) * 128, (2 * pair + j) * 128 + 128)
            turned = turn(packed[2 * pair + j, :, 0:128].astype(F32), rotary, -1.0).astype(BF16)
            grad[:, at] = turned
            bias[0:1, at] = jnp.sum(turned.astype(F32), axis=0, keepdims=True)
        a = packed[2 * pair, :, 128:256].astype(F32)
        b = packed[2 * pair + 1, :, 128:256].astype(F32)
        at = slice(1024 + pair * 128, 1024 + pair * 128 + 128)
        v = jnp.where(low, a, pltpu.roll(b, 64, 1))
        grad[:, at] = v.astype(BF16)
        bias[0:1, at] = jnp.sum(v, axis=0, keepdims=True)
        o = jnp.where(low, pltpu.roll(a, 64, 1), b)
        attended[:, pair * 128 : pair * 128 + 128] = o.astype(BF16)


def back(packed, tables):
    T = CHIP_TOKENS
    return pl.pallas_call(
        back_kernel,
        out_shape=(
            jax.ShapeDtypeStruct((T, 1536), BF16),
            jax.ShapeDtypeStruct((T, 512), BF16),
            jax.ShapeDtypeStruct((1, 1536), F32),
        ),
        in_specs=[VMEM] * 2,
        out_specs=(VMEM,) * 3,
        compiler_params=pltpu.CompilerParams(vmem_limit_bytes=48 * MIB),
    )(packed, tables)


def rotary_tables(first_position):
    half = ROT // 2
    frequency = 10000.0 ** (-2.0 * jnp.arange(half, dtype=F32) / ROT)
    positions = first_position + jnp.arange(CHIP_TOKENS, dtype=jnp.int32)
    angles = positions.astype(F32)[:, None] * frequency[None, :]
    cosine, sine = jnp.cos(angles), jnp.sin(angles)
    rest = HEAD - ROT
    one = jnp.ones((CHIP_TOKENS, rest), F32)
    zero = jnp.zeros((CHIP_TOKENS, rest), F32)
    none = jnp.zeros((CHIP_TOKENS, half), F32)
    rows = [
        jnp.concatenate([cosine, cosine, one] * 2, axis=1),
        jnp.concatenate([-sine, none, zero] * 2, axis=1),
        jnp.concatenate([none, sine, zero] * 2, axis=1),
    ]
    return jnp.stack(rows)


def gelu_and_slope(h):
    below = 0.5 * lax.erfc(-h * math.sqrt(0.5))
    density = jnp.exp(-0.5 * h * h) * (1.0 / math.sqrt(2.0 * math.pi))
    return h * below, below + h * density


def local(
    inputs,
    cotangent,
    ln_attn_gain,
    ln_attn_bias,
    ln_mlp_gain,
    ln_mlp_bias,
    qkv_weight,
    qkv_bias,
    dense_weight,
    dense_bias,
    hidden_weight,
    hidden_bias,
    output_weight,
    output_bias,
):
    seq = lax.axis_index("seq")
    core = seq % 2
    small = jnp.concatenate(
        [
            ln_attn_gain.reshape(1, 128),
            ln_attn_bias.reshape(1, 128),
            ln_mlp_gain.reshape(1, 128),
            ln_mlp_bias.reshape(1, 128),
            qkv_bias.reshape(3, 128),
            dense_bias.reshape(1, 128),
            hidden_bias.reshape(4, 128),
            output_bias.reshape(1, 128),
            jnp.zeros((3, 128), BF16),
        ]
    )
    own_qkv = lax.dynamic_index_in_dim(
        qkv_weight.reshape(128, 8, 2, 192), core, axis=2, keepdims=False
    )
    own_qkv = jnp.concatenate(
        [own_qkv[:, :, :128].reshape(128, 1024), own_qkv[:, :, 128:].reshape(128, 512)], axis=1
    )
    own_hidden = lax.dynamic_index_in_dim(
        hidden_weight.reshape(128, 8, 2, 256), core, axis=2, keepdims=False
    ).reshape(128, 2048)
    wq, wd, vectors, x, ct = gather(own_qkv, dense_weight, small, inputs, cotangent)
    wq = wq.reshape(D, 1536)
    wd = wd.reshape(512, D)
    x = x.reshape(CHIP_TOKENS, D)
    ct = ct.reshape(CHIP_TOKENS, D)
    vectors = vectors.astype(F32)
    norms = vectors[:, 0:4].transpose(1, 0, 2).reshape(4, D)
    head_bias = lax.dynamic_index_in_dim(
        vectors[:, 4:7].reshape(8, 2, 192), core, axis=1, keepdims=False
    )
    head_bias = jnp.concatenate(
        [head_bias[:, :128].reshape(1, 1024), head_bias[:, 128:].reshape(1, 512)], axis=1
    )
    out_bias = (vectors[:, 7] + vectors[:, 12]).reshape(1, D)
    unit_bias = lax.dynamic_index_in_dim(
        vectors[:, 8:12].reshape(8, 2, 256), core, axis=1, keepdims=False
    ).reshape(1, 2048)

    tables = rotary_tables((seq // 2) * CHIP_TOKENS)
    packed, attn_normed, mlp_normed = front(x, ct, wq, wd, norms, head_bias, tables)
    tokens, wh, wo = attention(packed, own_hidden, output_weight)
    wh = wh.reshape(D, 2048)
    wo = wo.reshape(2048, D)
    projected_grad, attended, head_bias_grad = back(tokens, tables)

    hidden = jnp.dot(mlp_normed, wh, preferred_element_type=F32) + unit_bias
    active, slope = gelu_and_slope(hidden)
    active = active.astype(BF16)
    active_grad = lax.dot_general(ct, wo, NT, preferred_element_type=F32)
    hidden_grad = (active_grad * slope).astype(BF16)
    output_weight_grad = lax.dot_general(active, ct, TN, preferred_element_type=F32)
    hidden_weight_grad = lax.dot_general(mlp_normed, hidden_grad, TN, preferred_element_type=F32)
    mlp_norm_grad = lax.dot_general(hidden_grad, wh, NT, preferred_element_type=F32)
    hidden_bias_grad = jnp.sum(hidden_grad.astype(F32), axis=0)

    branches = jnp.dot(attended, wd, preferred_element_type=F32) + jnp.dot(
        active, wo, preferred_element_type=F32
    )
    attn_norm_grad = lax.dot_general(projected_grad, wq, NT, preferred_element_type=F32)
    weighted = attn_norm_grad * norms[0:1] + mlp_norm_grad * norms[2:3]
    qkv_weight_grad = lax.dot_general(attn_normed, projected_grad, TN, preferred_element_type=F32)
    dense_weight_grad = lax.dot_general(attended, ct, TN, preferred_element_type=F32)

    values = x.astype(F32)
    centered = values - jnp.mean(values, axis=-1, keepdims=True)
    variance = jnp.mean(centered * centered, axis=-1, keepdims=True)
    scale = lax.rsqrt(variance + epsilon)
    normed = centered * scale
    attn_gain_grad = jnp.sum(attn_norm_grad * normed, axis=0)
    attn_bias_grad = jnp.sum(attn_norm_grad, axis=0)
    mlp_gain_grad = jnp.sum(mlp_norm_grad * normed, axis=0)
    mlp_bias_grad = jnp.sum(mlp_norm_grad, axis=0)

    def rows(a, c):
        return lax.dynamic_slice_in_dim(a, c * 256, 256, 0)

    swap = [(i, i + 1 - 2 * (i % 2)) for i in range(16)]
    given = jnp.concatenate(
        [rows(branches, 1 - core).astype(BF16), rows(weighted, 1 - core).astype(BF16)]
    )
    taken = lax.ppermute(given, "seq", swap).astype(F32)
    outputs = inputs.astype(F32) + rows(branches, core) + taken[:256] + out_bias
    w = rows(weighted, core) + taken[256:]
    n = rows(normed, core)
    input_grad = cotangent.astype(F32) + rows(scale, core) * (
        w - jnp.mean(w, axis=-1, keepdims=True) - n * jnp.mean(w * n, axis=-1, keepdims=True)
    )

    mine = (jnp.arange(2) == core).astype(F32)
    cotangent_sum = jnp.sum(cotangent.astype(F32), axis=0)
    per_head = jnp.concatenate(
        [head_bias_grad[0, :1024].reshape(8, 128), head_bias_grad[0, 1024:].reshape(8, 64)], axis=1
    )
    small_grads = jnp.concatenate(
        [
            attn_gain_grad.reshape(8, 1, 128),
            attn_bias_grad.reshape(8, 1, 128),
            mlp_gain_grad.reshape(8, 1, 128),
            mlp_bias_grad.reshape(8, 1, 128),
            (per_head[:, None, :] * mine[None, :, None]).reshape(8, 3, 128),
            cotangent_sum.reshape(8, 1, 128),
            (hidden_bias_grad.reshape(8, 1, 256) * mine[None, :, None]).reshape(8, 4, 128),
            jnp.zeros((8, 4, 128), F32),
        ],
        axis=1,
    )
    dense_part = dense_weight_grad.astype(BF16).reshape(8, 64, 2, 512).transpose(0, 2, 1, 3)
    heads_part = jnp.concatenate(
        [qkv_weight_grad.astype(BF16).reshape(8, 128, 1536), dense_part.reshape(8, 128, 512)],
        axis=2,
    )
    hidden_sum, output_sum, heads_sum, small_sum = reduce_all(
        (
            hidden_weight_grad.astype(BF16).reshape(4, 2, 2, 4, 16, 2048),
            output_weight_grad.astype(BF16).reshape(4, 2, 2, 4, 32, 1024),
            heads_part.reshape(4, 2, 2, 4, 16, 2048),
        ),
        small_grads,
        3,
    )
    hidden_total = (
        hidden_sum.reshape(2, 128, 8, 256).transpose(1, 2, 0, 3).reshape(128, FF).astype(F32)
    )
    output_total = output_sum.reshape(512, D).astype(F32)
    heads_sum = heads_sum.reshape(2, 128, 2048)
    qkv_total = jnp.concatenate(
        [
            heads_sum[:, :, :1024].reshape(2, 128, 8, 128),
            heads_sum[:, :, 1024:1536].reshape(2, 128, 8, 64),
        ],
        axis=3,
    )
    qkv_total = qkv_total.transpose(1, 2, 0, 3).reshape(128, 3 * D).astype(F32)
    dense_total = heads_sum[:, :, 1536:].reshape(2, 2, 64, 512).transpose(0, 2, 1, 3)
    dense_total = dense_total.reshape(128, D).astype(F32)
    return (
        outputs.astype(BF16),
        input_grad,
        small_sum[0],
        small_sum[1],
        small_sum[2],
        small_sum[3],
        qkv_total,
        small_sum[4:7].reshape(384),
        dense_total,
        small_sum[7],
        hidden_total,
        small_sum[8:12].reshape(512),
        output_total,
        small_sum[7],
    )


def solution(mesh):
    rows = P(("fsdp", "seq"), None)
    vector = P("fsdp")
    matrix = P("fsdp", None)
    shared = (vector,) * 4 + (matrix, vector) * 4
    return jax.shard_map(
        local,
        mesh=mesh,
        in_specs=(rows, rows, *shared),
        out_specs=(rows, rows, *shared),
        check_vma=False,
    )
```

profile of v0, /device:TPU:1, one launch (start us, length us, event | category | flops | bytes accessed | tf_op | source)
XLA Modules:
  0.0 370.3 jit_solution(9889748722408172700)
XLA Ops:
  0.7 1.5 copy.55
  2.7 0.8 pad_maximum_fusion.3.wq
  3.5 1.2 concatenate.39.small
  4.7 54.7 %shard_map.245 = (bf16[8,128,1536]{2,1,0:T(8,128)(2,1)}, bf16[8,64,1024]{2,1,0:T(8,128)(2,1)}, bf16[8,16,128]{2,1,0:T(8,128)(2,1)}, bf16[2,256,1024]{2,1,0:T(8,128)(2,1)}, bf16[2,256,1024]{2,1,0:T(8,128)(2,1)}) custom-call(bf16[128,1536]{1,0:T(8,128)(2,1)} %pad_maximum_fusion.3.wq, bf16[128,1024]{1,0:T(8,128)(2,1)} %wd.1, ...), custom_call_target="tpu_custom_call" | custom-call | tf_op jit(solution)/shard_map/pallas_call | solution.py:162
  59.4 0.8 convert_element_type.104
  61.1 0.7 slice.109
  61.8 1.4 convert_reduce_fusion.1
  63.2 1.6 fusion.15
  65.0 1.0 multiply_cosine_fusion
  66.1 1.1 concatenate.43
  67.2 1.1 concatenate.42
  68.3 3.0 reshape.281
  71.2 4.3 %dynamic-slice_reduce_fusion = bf16[128,8,256]{2,1,0:T(8,128)(2,1)S(1)} fusion(bf16[128,8,2,256]{3,2,1,0:T(2,128)(2,1)} %reshape.281, s32[]{:T(128)S(6)} %select_n.32), kind=kLoop, calls=%fused_computation.53 | loop fusion | bytes 1048580 | tf_op jit(solution)/shard_map/jit(dynamic_index_in_dim)/dynamic_slice | solution.py:765
  75.6 0.9 copy.72
  77.2 2.2 concatenate.41
  79.4 1.2 pad_maximum_fusion.2.tables
  80.6 7.2 %shard_map.246 = (bf16[8,512,256]{2,1,0:T(8,128)(2,1)}, bf16[512,1024]{1,0:T(8,128)(2,1)S(1)}, bf16[512,1024]{1,0:T(8,128)(2,1)S(1)}) custom-call(bf16[512,1024]{1,0:T(8,128)(2,1)S(1)} %bitcast.125, bf16[512,1024]{1,0:T(8,128)(2,1)S(1)} %bitcast.128, bf16[1024,1536]{1,0:T(8,128)(2,1)} %bitcast.140, bf16[512,1024]{1,0:T(8,128)(2,1)S(1)} %bitcast.126, ...), custom_call_target="tpu_custom_call" | custom-call | tf_op jit(solution)/shard_map/pallas_call | solution.py:657
  87.8 110.8 %shard_map.247 = (bf16[8,512,256]{2,1,0:T(8,128)(2,1)}, bf16[8,128,2048]{2,1,0:T(8,128)(2,1)}, bf16[8,256,1024]{2,1,0:T(8,128)(2,1)}) custom-call(bf16[8,512,256]{2,1,0:T(8,128)(2,1)} %get-tuple-element.37.packed, bf16[128,2048]{1,0:T(8,128)(2,1)} %bitcast.143, bf16[512,1024]{1,0:T(8,128)(2,1)} %wo.1), custom_call_target="tpu_custom_call" | custom-call | tf_op jit(solution)/shard_map/pallas_call | solution.py:336
  198.7 1.6 copy-done.2
  200.2 1.5 shard_map.248
  201.8 0.8 copy-done.4
  202.5 1.1 copy-done.6
  203.7 5.0 %fusion.29 = f32[512,1024]{1,0:T(8,128)} fusion(bf16[512,1536]{1,0:T(8,128)(2,1)S(1)} %get-tuple-element.43, bf16[1024,1536]{1,0:T(8,128)(2,1)} %bitcast.141), kind=kOutput, calls=%fused_computation.95 | convolution fusion | flops 1610612736 | bytes 6815744 | tf_op jit(solution)/shard_map/dot_general | solution.py:806
  208.8 13.6 %multiply_convert_fusion = (bf16[512,2048]{1,0:T(8,128)(2,1)S(1)}, f32[512,2048]{1,0:T(8,128)S(1)}, f32[512,2048]{1,0:T(8,128)S(1)}) fusion(f32[2048]{0:T(1024)S(1)} %bitcast.162, bf16[512,1024]{1,0:T(8,128)(2,1)} %copy-done.8, bf16[1024,2048]{1,0:T(8,128)(2,1)} %bitcast.182), kind=kOutput, calls=%fused_computation.12 | convolution fusion | flops 2216689664 | bytes 15736832 | tf_op jit(solution)/shard_map/dot_general | solution.py:793
  222.4 3.7 fusion.28
  226.1 4.4 %convert_reduce_fusion = (f32[2048]{0:T(1024)S(1)}, bf16[512,2048]{1,0:T(8,128)(2,1)}) fusion(f32[512,2048]{1,0:T(8,128)S(1)} %get-tuple-element.99, f32[512,2048]{1,0:T(8,128)S(1)} %get-tuple-element.125, f32[2048]{0:T(1024)S(1)} %bitcast.163, bf16[512,1024]{1,0:T(8,128)(2,1)S(1)} %bitcast.129, bf16[2048,1024]{1,0:T(8,128)(2,1)S(1)} %bitcast.185), kind=kOutput, calls=%fused_computation.11 | convolution fusion | flops 2157967360 | bytes 15745024 | tf_op jit(solution)/shard_map/dot_general | solution.py:796
  230.4 2.6 convolution_add_fusion
  233.4 6.8 %fusion.23 = (f32[1024]{0:T(1024)S(1)}, f32[1024]{0:T(1024)S(1)}, f32[512,1024]{1,0:T(8,128)S(1)}, f32[1024]{0:T(1024)S(1)}, f32[1024]{0:T(1024)S(1)}, /*index=5*/f32[512,1024]{1,0:T(8,128)}) fusion(f32[512]{0:T(512)S(1)} %bitcast.172, f32[512]{0:T(512)S(1)} %bitcast.173, bf16[2,256,1024]{2,1,0:T(8,128)(2,1)S(1)} %copy-done, f32[1024]{0:T(1024)S(1)} %bitcast.171, ...), kind=kOutput, calls=%fused_computation.90 | convolution fusion | flops 2153771008 | bytes 13660160 | tf_op jit(solution)/shard_map/dot_general | solution.py:800
  240.4 1.1 copy-done.13
  241.5 1.1 pad_maximum_fusion.1
  242.6 2.7 collective-permute-start
  245.4 1.7 convolution_convert_fusion.3
  247.1 2.8 reshape.288
  249.9 2.5 copy.60
  252.4 4.7 %convolution_convert_fusion = bf16[1024,1536]{1,0:T(8,128)(2,1)} fusion(bf16[512,1024]{1,0:T(8,128)(2,1)} %copy-done.10, bf16[512,1536]{1,0:T(8,128)(2,1)S(1)} %copy-done.7), kind=kOutput, calls=%fused_computation.27 | convolution fusion | flops 1612185600 | bytes 5767168 | tf_op jit(solution)/shard_map/dot_general | solution.py:808
  257.7 5.0 %pad_maximum_fusion.refs_2_ = bf16[4,2,2,4,16,2048]{5,4,3,2,1,0:T(8,128)(2,1)} fusion(bf16[4,2,2,4,16,512]{5,4,3,2,1,0:T(8,128)(2,1)} %bitcast.139, bf16[4,2,2,4,16,1536]{5,4,3,2,1,0:T(8,128)(2,1)} %bitcast.142), kind=kLoop, calls=%fused_computation.10 | loop fusion | flops 8388608 | bytes 8388608 | tf_op jit(solution)/shard_map/concatenate | solution.py:855
  262.8 4.4 %convolution_convert_fusion.2 = bf16[1024,2048]{1,0:T(8,128)(2,1)} fusion(bf16[512,1024]{1,0:T(8,128)(2,1)S(1)} %copy-done.9, bf16[512,2048]{1,0:T(8,128)(2,1)S(1)} %copy-done.30), kind=kOutput, calls=%fused_computation.29 | convolution fusion | flops 2149580800 | bytes 7340032 | tf_op jit(solution)/shard_map/dot_general | solution.py:799
  267.2 4.4 %convolution_convert_fusion.1 = bf16[2048,1024]{1,0:T(8,128)(2,1)} fusion(bf16[512,2048]{1,0:T(8,128)(2,1)S(1)} %copy-done.32, bf16[512,1024]{1,0:T(8,128)(2,1)S(1)} %bitcast.131), kind=kOutput, calls=%fused_computation.28 | convolution fusion | flops 2149580800 | bytes 7340032 | tf_op jit(solution)/shard_map/dot_general | solution.py:798
  271.5 1.6 convert_element_type.110
  273.7 1.7 convert_add_fusion
  275.4 79.2 %shard_map.249 = (bf16[2,8,16,2048]{3,2,1,0:T(8,128)(2,1)S(1)}, bf16[2,8,32,1024]{3,2,1,0:T(8,128)(2,1)S(1)}, bf16[2,8,16,2048]{3,2,1,0:T(8,128)(2,1)S(1)}, f32[16,128]{1,0:T(8,128)S(1)}) custom-call(bf16[4,2,2,4,16,2048]{5,4,3,2,1,0:T(8,128)(2,1)} %bitcast.137, bf16[4,2,2,4,32,1024]{5,4,3,2,1,0:T(8,128)(2,1)} %bitcast.138, ...), custom_call_target="tpu_custom_call" | custom-call | tf_op jit(solution)/shard_map/pallas_call | solution.py:604
  354.6 0.8 fusion.26
  357.7 1.3 copy.63
  359.0 3.0 copy.66
  362.3 0.9 copy.76
  363.6 1.6 copy.65
  365.2 2.7 reshape.301
  367.9 1.6 bitcast_convert_fusion
  (126 shorter events, 7.4 us)
Async XLA Ops:
  0.6 2.8 copy-start.21
  0.7 2.8 copy-start.22
  0.7 2.8 copy-start.23
  0.7 2.8 copy-start.24
  0.7 2.8 copy-start.19
  0.7 2.8 copy-start.25
  0.7 2.8 copy-start.20
  0.7 2.8 copy-start.26
  68.3 12.3 %copy-start = (bf16[2,256,1024]{2,1,0:T(8,128)(2,1)S(1)}, bf16[2,256,1024]{2,1,0:T(8,128)(2,1)}, u32[]{:S(2)}) copy-start(bf16[2,256,1024]{2,1,0:T(8,128)(2,1)} %get-tuple-element.32) | copy-start | bytes 3145732
  68.3 12.3 %copy-start.1 = (bf16[8,64,1024]{2,1,0:T(8,128)(2,1)S(1)}, bf16[8,64,1024]{2,1,0:T(8,128)(2,1)}, u32[]{:S(2)}) copy-start(bf16[8,64,1024]{2,1,0:T(8,128)(2,1)} %get-tuple-element.35) | copy-start | bytes 3145732
  68.3 12.3 %copy-start.3 = (bf16[2,256,1024]{2,1,0:T(8,128)(2,1)S(1)}, bf16[2,256,1024]{2,1,0:T(8,128)(2,1)}, u32[]{:S(2)}) copy-start(bf16[2,256,1024]{2,1,0:T(8,128)(2,1)} %get-tuple-element.33) | copy-start | bytes 3145732
  87.8 110.8 %copy-start.8 = (bf16[512,1024]{1,0:T(8,128)(2,1)}, bf16[512,1024]{1,0:T(8,128)(2,1)S(1)}, u32[]{:S(2)}) copy-start(bf16[512,1024]{1,0:T(8,128)(2,1)S(1)} %get-tuple-element.40) | copy-start | bytes 3145732
  87.8 110.8 %copy-start.10 = (bf16[512,1024]{1,0:T(8,128)(2,1)}, bf16[512,1024]{1,0:T(8,128)(2,1)S(1)}, u32[]{:S(2)}) copy-start(bf16[512,1024]{1,0:T(8,128)(2,1)S(1)} %get-tuple-element.44) | copy-start | bytes 3145732
  198.7 1.6 copy-start.2
  201.7 0.8 copy-start.4
  202.5 1.1 copy-start.6
  208.8 13.6 %copy-start.29 = (bf16[8,256,1024]{2,1,0:T(8,128)(2,1)S(1)}, bf16[8,256,1024]{2,1,0:T(8,128)(2,1)}, u32[]{:S(2)}) copy-start(bf16[8,256,1024]{2,1,0:T(8,128)(2,1)} %get-tuple-element.42) | copy-start | bytes 12582916
  222.3 3.7 %copy-start.31 = (bf16[512,2048]{1,0:T(8,128)(2,1)}, bf16[512,2048]{1,0:T(8,128)(2,1)S(1)}, u32[]{:S(2)}) copy-start(bf16[512,2048]{1,0:T(8,128)(2,1)S(1)} %get-tuple-element.98) | copy-start | bytes 6291460
  230.4 3.0 copy-start.28
  233.1 7.2 %copy-start.11 = (f32[512,1024]{1,0:T(8,128)}, f32[512,1024]{1,0:T(8,128)S(1)}, u32[]{:S(2)}) copy-start(f32[512,1024]{1,0:T(8,128)S(1)} %convolution_add_fusion) | copy-start | bytes 6291460
  240.2 1.3 copy-start.13
  240.2 5.1 %copy-start.5 = (bf16[512,512]{1,0:T(8,128)(2,1)S(1)}, bf16[512,512]{1,0:T(8,128)(2,1)}, u32[]{:S(2)}) copy-start(bf16[512,512]{1,0:T(8,128)(2,1)} %copy-done.4) | copy-start | bytes 1572868
  241.5 10.9 %copy-start.7 = (bf16[512,1536]{1,0:T(8,128)(2,1)S(1)}, bf16[512,1536]{1,0:T(8,128)(2,1)}, u32[]{:S(2)}) copy-start(bf16[512,1536]{1,0:T(8,128)(2,1)} %copy-done.6) | copy-start | bytes 4718596
  242.6 28.9 %collective-permute-start = (bf16[512,1024]{1,0:T(8,128)(2,1)}, bf16[512,1024]{1,0:T(8,128)(2,1)}, u32[]{:S(2)}, u32[]{:S(2)}) collective-permute-start(bf16[512,1024]{1,0:T(8,128)(2,1)} %pad_maximum_fusion.1), channel_id=1, source_target_pairs={{0,1},{1,0},{2,3},{3,2},{4,5},{5,4},{6,7},{7,6},{8,9},{9,8},{10,11... | collective-permute-start | bytes 3145736 | tf_op jit(solution)/shard_map/ppermute | solution.py:828
  257.7 5.1 %copy-start.9 = (bf16[512,1024]{1,0:T(8,128)(2,1)S(1)}, bf16[512,1024]{1,0:T(8,128)(2,1)}, u32[]{:S(2)}) copy-start(bf16[512,1024]{1,0:T(8,128)(2,1)} %copy-done.8) | copy-start | bytes 3145732
  257.7 5.1 %copy-start.30 = (bf16[512,2048]{1,0:T(8,128)(2,1)S(1)}, bf16[512,2048]{1,0:T(8,128)(2,1)}, u32[]{:S(2)}) copy-start(bf16[512,2048]{1,0:T(8,128)(2,1)} %get-tuple-element.127) | copy-start | bytes 6291460
  262.8 4.4 %copy-start.32 = (bf16[512,2048]{1,0:T(8,128)(2,1)S(1)}, bf16[512,2048]{1,0:T(8,128)(2,1)}, u32[]{:S(2)}) copy-start(bf16[512,2048]{1,0:T(8,128)(2,1)} %copy-done.31) | copy-start | bytes 6291460
  267.2 6.0 %copy-start.14 = (f32[512,1024]{1,0:T(8,128)S(1)}, f32[512,1024]{1,0:T(8,128)}, u32[]{:S(2)}) copy-start(f32[512,1024]{1,0:T(8,128)} %copy-done.13) | copy-start | bytes 6291460
  267.2 6.0 %copy-start.15 = (f32[512,1024]{1,0:T(8,128)S(1)}, f32[512,1024]{1,0:T(8,128)}, u32[]{:S(2)}) copy-start(f32[512,1024]{1,0:T(8,128)} %get-tuple-element.105) | copy-start | bytes 6291460
  271.5 2.0 copy-start.12
  271.5 2.0 copy-start.16
  271.5 2.1 copy-start.17
  356.0 13.6 %copy-start.27 = (f32[128]{0:T(128)}, f32[128]{0:T(128)S(1)}, u32[]{:S(2)}) copy-start(f32[128]{0:T(128)S(1)} %get-tuple-element.157) | copy-start | bytes 1540
  357.6 4.4 %copy-start.18 = (bf16[2,128,512]{2,1,0:T(8,128)(2,1)S(1)}, bf16[2,128,512]{2,1,0:T(8,128)(2,1)}, u32[]{:S(2)}) copy-start(bf16[2,128,512]{2,1,0:T(8,128)(2,1)} %get-tuple-element.106) | copy-start | bytes 786436
where the time goes:
time: 377 us; the launch traced here: 370 us
  Pallas kernels  253 us (67%)
  matrix products  51.3 us (14%)
  local copies, waits for them, and re-layouts  43 us (11%)
  other arithmetic  18.3 us (5%)
    pallas_call x1, Pallas kernels, attention(): pl.pallas_call(attention_kernel, out_shape=(jax.ShapeDtypeStruct((CHIPS,...  111 us
    pallas_call x1, Pallas kernels, reduce_all(): pl.pallas_call(reduce_kernel, out_shape=(*outs, jax.ShapeDtypeStruct((16,...  79.2 us
    pallas_call x1, Pallas kernels, gather(): pl.pallas_call(gather_kernel, out_shape=(shape(8, 128, 1536), shape(8, 64...  54.7 us
    dot_general x1, matrix products, local(): hidden = jnp.dot(mlp_normed, wh, preferred_element_type=F32) + unit_bias  13.6 us
    unnamed x78, local copies, waits for them, and re-layouts  12.8 us
  transfers between devices with their start and end apart: 1, of which 0 were waited for; matrix products, arithmetic and copies ran while one was open for 7% of the time, Pallas kernels for 0%

commit v1 on v0

--- a/solution.py
+++ b/solution.py
@@ -362,31 +362,31 @@
 
 ORDERS = ("yzx", "zxy", "xyz")
 LEADS = ((2, 4), (2, 4), (4, 2))
-
-
-def from_input(n, ref, t, h):
-    if n == 0:
-        return ref.at[t, h]
-    if n == 1:
-        return ref.at[pl.ds(2 * h, 2), t % 2, t // 2]
-    return ref.at[:, h, :, t]
-
-
-def from_own(n, stage, own, t, h, where):
+ROWS = (16, 32, 16)
+COLUMNS = (2048, 1024, 2048)
+
+
+def chunk(n, stage, g, t, h, where):
     y, zl, zh, px = where
+    if stage == 0:
+        if n == 0:
+            return g.at[t, h]
+        if n == 1:
+            return g.at[pl.ds(2 * h, 2), t % 2, t // 2]
+        return g.at[:, h, :, t]
     if stage == 1:
         if n == 0:
-            return own.at[t % 2, t // 2, pl.ds(2 * h, 2)]
+            return g.at[y, t % 2, t // 2, pl.ds(2 * h, 2)]
         if n == 1:
-            return own.at[h, :, t]
-        return own.at[h, t]
-    half = own.shape[-1] // 2
+            return g.at[pl.ds(2 * h, 2), zl, zh, t]
+        return g.at[t, h, :, px]
+    half = g.shape[-1] // 2
     columns = pl.ds(h * half, half)
     if n == 0:
-        return own.at[zl, zh, t, :, columns]
+        return g.at[y, zl, zh, t, :, columns]
     if n == 1:
-        return own.at[t // 2, t % 2, px, :, columns]
-    return own.at[t % 2, y, t // 2, :, columns]
+        return g.at[t, zl, zh, px, :, columns]
+    return g.at[y, t % 2, t // 2, px, :, columns]
 
 
 def add_into(dst, terms):
@@ -407,15 +407,28 @@
     lax.fori_loop(0, math.prod(lead), body, 0)
 
 
-def reduce_kernel(*refs):
-    ins, small, outs, small_out = refs[0:3], refs[3], refs[4:7], refs[7]
-    scratch = refs[8:]
-    bufs = [scratch[9 * n : 9 * n + 9] for n in range(3)]
-    (sm_a, sm_b, send, recv, local_sem, sm_send, sm_recv) = scratch[27:]
+def normalised(values):
+    values = values.astype(F32)
+    centered = values - jnp.mean(values, axis=-1, keepdims=True)
+    variance = jnp.mean(centered * centered, axis=-1, keepdims=True)
+    scale = lax.rsqrt(variance + epsilon)
+    return centered * scale, scale
+
+
+def rest_kernel(
+    tokens, x, ct, an, mn, wq, wd, wh, wo, norms, unit_bias, out_bias, tables,
+    outputs, input_grad, hidden_out, output_out, qkv_out, dense_out, small_out,
+    x_v, ct_v, an_v, mn_v, branches, weighted, sums, small, sm_a, sm_b, pair_send, pair_recv,
+    g0, g1, g2, *rest,
+):
+    grads = (g0, g1, g2)
+    bufs = [rest[7 * n : 7 * n + 7] for n in range(3)]
+    send, recv, local_sem, sm_send, sm_recv = rest[21:]
     f, s, (y, zl, px, zh, core) = place()
     z = zh * 2 + zl
     coordinate = {"y": y, "z": z, "x": px}
     where = (y, zl, zh, px)
+    T = CHIP_TOKENS
 
     def along(axis, step):
         t = dict(coordinate)
@@ -428,8 +441,12 @@
     same_fsdp = [{"fsdp": f, "seq": (s + k) % 16} for k in range(1, 16)]
     zother = device(y, 2 * (1 - zh) + 1 - zl, px, core)
     sibling = device(y, z, px, 1 - core)
-    barrier(same_seq + same_fsdp + [zother])
     sends = []
+
+    def load(src, dst, k):
+        copy = pltpu.make_async_copy(src, dst, local_sem.at[k])
+        copy.start()
+        return copy
 
     def started(src, dst, k, target):
         copy = remote(src, dst, send.at[k], recv.at[k], target)
@@ -447,74 +464,49 @@
     def small_arrived(ref, k):
         remote(ref, ref, sm_send.at[k], sm_recv.at[k], sibling).wait_recv()
 
-    for k in range(1, 8):
-        small_sent(small.at[(f + k) % 8], sm_a.at[k], k, same_seq[k - 1])
-
-    keeps = []
-    for n in range(3):
-        axis = ORDERS[n][0]
-        p = coordinate[axis]
-        src = ins[n]
-        opp, fin, mid, own = bufs[n][0:4]
-        b = 26 * n
-        started(from_input(n, src, (p + 2) % 4, 0), opp.at[0], b, plus[axis])
-        started(from_input(n, src, (p + 2) % 4, 1), opp.at[1], b + 1, minus[axis])
-        pairs = [
-            (from_input(n, src, (p + 1) % 4, 0), mid.at[0]),
-            (from_input(n, src, (p + 3) % 4, 1), mid.at[1]),
-            (from_input(n, src, p, 0), own.at[0]),
-            (from_input(n, src, p, 1), own.at[1]),
-        ]
-        for k, (a, dst) in enumerate(pairs):
-            copy = pltpu.make_async_copy(a, dst, local_sem.at[4 * n + k])
-            copy.start()
-            keeps.append(copy)
-        started(from_input(n, src, (p + 1) % 4, 1), fin.at[0, 1], b + 2, plus[axis])
-        started(from_input(n, src, (p + 3) % 4, 0), fin.at[1, 0], b + 3, minus[axis])
-
     def buffers(n, stage):
-        if stage == 0:
-            return bufs[n][0], bufs[n][1]
-        return bufs[n][2 + 2 * stage], bufs[n][3 + 2 * stage]
-
-    def begin(n, stage):
-        axis = ORDERS[n][stage]
-        p = coordinate[axis]
-        own = bufs[n][3]
-        opp, fin = buffers(n, stage)
-        b = 26 * n + 6 * stage
-
-        def view(t, h):
-            return from_own(n, stage, own, t % 4, h, where)
-
-        started(view(p + 2, 0), opp.at[0], b, plus[axis])
-        started(view(p + 2, 1), opp.at[1], b + 1, minus[axis])
-        started(view(p + 1, 1), fin.at[0, 1], b + 2, plus[axis])
-        started(view(p + 3, 0), fin.at[1, 0], b + 3, minus[axis])
-
-    def relay(n, stage):
+        return bufs[n][2 * stage], bufs[n][2 * stage + 1]
+
+    def raw_copies(n, stage):
         axis = ORDERS[n][stage]
         p = coordinate[axis]
         opp, fin = buffers(n, stage)
         b = 26 * n + 6 * stage
-        if stage == 0:
-            mids = bufs[n][2].at[0], bufs[n][2].at[1]
-        else:
-            own = bufs[n][3]
-            mids = (
-                from_own(n, stage, own, (p + 1) % 4, 0, where),
-                from_own(n, stage, own, (p + 3) % 4, 1, where),
-            )
-        arrived(opp.at[0], b)
-        add_into(mids[0], [opp.at[0]])
-        started(mids[0], fin.at[0, 0], b + 4, plus[axis])
-        arrived(opp.at[1], b + 1)
-        add_into(mids[1], [opp.at[1]])
-        started(mids[1], fin.at[1, 1], b + 5, minus[axis])
+
+        def copy(t, h, dst, k, target):
+            src = chunk(n, stage, grads[n], t % 4, h, where)
+            return remote(src, dst, send.at[k], recv.at[k], target)
+
+        return [
+            copy(p + 2, 0, opp.at[0], b, plus[axis]),
+            copy(p + 2, 1, opp.at[1], b + 1, minus[axis]),
+            copy(p + 1, 1, fin.at[0, 1], b + 2, plus[axis]),
+            copy(p + 3, 0, fin.at[1, 0], b + 3, minus[axis]),
+        ]
+
+    def relay_copy(n, stage, h):
+        axis = ORDERS[n][stage]
+        _, fin = buffers(n, stage)
+        k = 26 * n + 6 * stage + 4 + h
+        t = coordinate[axis] + 1 + 2 * h
+        src = chunk(n, stage, grads[n], t % 4, h, where)
+        target = (plus, minus)[h][axis]
+        return src, remote(src, fin.at[h, h], send.at[k], recv.at[k], target)
+
+    def begin(n, stage):
+        for copy in raw_copies(n, stage):
+            copy.start()
+
+    def relay(n, stage):
+        opp, _ = buffers(n, stage)
+        for h in range(2):
+            mid, copy = relay_copy(n, stage, h)
+            arrived(opp.at[h], 26 * n + 6 * stage + h)
+            add_into(mid, [opp.at[h]])
+            copy.start()
 
     def finish(n, stage):
         p = coordinate[ORDERS[n][stage]]
-        own = bufs[n][3]
         _, fin = buffers(n, stage)
         b = 26 * n + 6 * stage
         arrived(fin.at[0, 1], b + 2)
@@ -522,14 +514,159 @@
         arrived(fin.at[0, 0], b + 4)
         arrived(fin.at[1, 1], b + 5)
         for h in range(2):
-            mine = own.at[h] if stage == 0 else from_own(n, stage, own, p, h, where)
-            add_into(mine, [fin.at[0, h], fin.at[1, h]])
-
-    for n in range(3):
-        keeps[4 * n].wait()
-        keeps[4 * n + 1].wait()
-        relay(n, 0)
-
+            add_into(chunk(n, stage, grads[n], p, h, where), [fin.at[0, h], fin.at[1, h]])
+
+    keeps = [load(a, b, k) for k, (a, b) in enumerate([(x, x_v), (ct, ct_v), (an, an_v), (mn, mn_v)])]
+    barrier(same_seq + same_fsdp + [zother])
+    small[...] = jnp.zeros_like(small)
+
+    def attention_part(wq_v, wd_v, tk_v, pg_v, at_v, turned_v):
+        loads = [load(a, b, 4 + k) for k, (a, b) in enumerate([(tokens, tk_v), (wq, wq_v), (wd, wd_v)])]
+        for copy in keeps:
+            copy.wait()
+        loads[0].wait()
+        low = lax.broadcasted_iota(jnp.int32, (T, 128), 1) < HEAD
+        first = lax.broadcasted_iota(jnp.int32, (1, 128), 1) < HEAD
+        rotary = (tables[0], tables[1], tables[2])
+        for pair in range(4):
+            for j in range(2):
+                r = 2 * pair + j
+                at = slice(r * 128, r * 128 + 128)
+                turned = turn(tk_v[r, :, 0:128].astype(F32), rotary, -1.0).astype(BF16)
+                pg_v[:, at] = turned
+                small[r, pl.ds(4 + core, 1), :] = jnp.sum(turned.astype(F32), axis=0, keepdims=True)
+            a = tk_v[2 * pair, :, 128:256].astype(F32)
+            b = tk_v[2 * pair + 1, :, 128:256].astype(F32)
+            v = jnp.where(low, a, pltpu.roll(b, 64, 1))
+            pg_v[:, 1024 + pair * 128 : 1152 + pair * 128] = v.astype(BF16)
+            total = jnp.sum(v, axis=0, keepdims=True)
+            moved = jnp.sum(jnp.where(low, pltpu.roll(v, 64, 1), pltpu.roll(v, 64, 1)), axis=0, keepdims=True)
+            zero = jnp.zeros_like(total)
+            at_low = (jnp.where(first, total, zero), jnp.where(first, moved, zero))
+            at_high = (jnp.where(first, zero, moved), jnp.where(first, zero, total))
+            for j in range(2):
+                small[2 * pair + j, 6:7, :] = jnp.where(core == 0, at_low[j], at_high[j])
+            o = jnp.where(low, pltpu.roll(a, 64, 1), b)
+            at_v[:, pair * 128 : pair * 128 + 128] = o.astype(BF16)
+
+        turned_v[...] = an_v[...].T
+
+        def qkv_columns(k, _):
+            at = pl.ds(pl.multiple_of(k * 512, 512), 512)
+            part = jnp.dot(turned_v[...], pg_v[:, at], preferred_element_type=F32)
+            g2[:, :, :, :, :, at] = part.astype(BF16).reshape(4, 2, 2, 4, 16, 512)
+            return 0
+
+        lax.fori_loop(0, 3, qkv_columns, 0)
+        turned_v[0:512, :] = at_v[...].T
+        for k in range(2):
+            part = jnp.dot(
+                turned_v[0:512, :], ct_v[:, k * 512 : k * 512 + 512], preferred_element_type=F32
+            )
+            g2[:, :, k, :, :, 1536:2048] = part.astype(BF16).reshape(4, 2, 4, 16, 512)
+        begin(2, 0)
+        loads[1].wait()
+        loads[2].wait()
+        grad = lax.dot_general(pg_v[...], wq_v[...], NT, preferred_element_type=F32)
+        normed, _ = normalised(x_v[...])
+        sums[0:1, :] = jnp.sum(grad * normed, axis=0, keepdims=True)
+        sums[1:2, :] = jnp.sum(grad, axis=0, keepdims=True)
+        weighted[...] = grad * norms[0:1, :]
+        branches[...] = jnp.dot(at_v[...], wd_v[...], preferred_element_type=F32)
+
+    pl.run_scoped(
+        attention_part,
+        pltpu.VMEM((D, 1536), BF16),
+        pltpu.VMEM((512, D), BF16),
+        pltpu.VMEM((8, T, 256), BF16),
+        pltpu.VMEM((T, 1536), BF16),
+        pltpu.VMEM((T, 512), BF16),
+        pltpu.VMEM((D, T), BF16),
+    )
+
+    def unit_part(wh_v, wo_v, act_v, hg_v, turned_v):
+        loads = [load(a, b, 7 + k) for k, (a, b) in enumerate([(wh, wh_v), (wo, wo_v)])]
+        loads[0].wait()
+        loads[1].wait()
+
+        def units(r, _):
+            at = pl.ds(pl.multiple_of(r * 256, 256), 256)
+            h = jnp.dot(mn_v[...], wh_v[:, at], preferred_element_type=F32) + unit_bias[0:1, at]
+            below = 0.5 + 0.5 * lax.erf(h * math.sqrt(0.5))
+            density = jnp.exp(-0.5 * h * h) * (1.0 / math.sqrt(2.0 * math.pi))
+            act_v[:, at] = (h * below).astype(BF16)
+            up = lax.dot_general(ct_v[...], wo_v[at, :], NT, preferred_element_type=F32)
+            grad = (up * (below + h * density)).astype(BF16)
+            hg_v[:, at] = grad
+            total = jnp.sum(grad.astype(F32), axis=0, keepdims=True)
+            small[r, pl.ds(8 + 2 * core, 1), :] = total[:, 0:128]
+            small[r, pl.ds(9 + 2 * core, 1), :] = total[:, 128:256]
+            return 0
+
+        lax.fori_loop(0, 8, units, 0)
+        turned_v[...] = act_v[...].T
+
+        def output_rows(k, _):
+            at = pl.ds(pl.multiple_of(k * 512, 512), 512)
+            part = jnp.dot(turned_v[at, :], ct_v[...], preferred_element_type=F32)
+            g1[k] = part.astype(BF16).reshape(2, 2, 4, 32, 1024)
+            return 0
+
+        lax.fori_loop(0, 4, output_rows, 0)
+        begin(1, 0)
+        turned_v[0:D, :] = mn_v[...].T
+
+        def hidden_columns(k, _):
+            at = pl.ds(pl.multiple_of(k * 512, 512), 512)
+            part = jnp.dot(turned_v[0:D, :], hg_v[:, at], preferred_element_type=F32)
+            g0[:, :, :, :, :, at] = part.astype(BF16).reshape(4, 2, 2, 4, 16, 512)
+            return 0
+
+        lax.fori_loop(0, 4, hidden_columns, 0)
+        begin(0, 0)
+        relay(2, 0)
+        grad = lax.dot_general(hg_v[...], wh_v[...], NT, preferred_element_type=F32)
+        normed, _ = normalised(x_v[...])
+        sums[2:3, :] = jnp.sum(grad * normed, axis=0, keepdims=True)
+        sums[3:4, :] = jnp.sum(grad, axis=0, keepdims=True)
+        weighted[...] += grad * norms[2:3, :]
+        branches[...] += jnp.dot(act_v[...], wo_v[...], preferred_element_type=F32)
+
+    pl.run_scoped(
+        unit_part,
+        pltpu.VMEM((D, 2048), BF16),
+        pltpu.VMEM((2048, D), BF16),
+        pltpu.VMEM((T, 2048), BF16),
+        pltpu.VMEM((T, 2048), BF16),
+        pltpu.VMEM((2048, T), BF16),
+    )
+
+    other = pl.ds(pl.multiple_of((1 - core) * 256, 256), 256)
+    mine = pl.ds(pl.multiple_of(core * 256, 256), 256)
+    pair_send[0] = branches[other, :].astype(BF16)
+    pair_send[1] = weighted[other, :].astype(BF16)
+    started(pair_send, pair_recv, 78, sibling)
+    sums[4:5, :] = jnp.sum(ct_v[mine, :].astype(F32), axis=0, keepdims=True)
+    for r in range(8):
+        at = slice(r * 128, r * 128 + 128)
+        small[r, 0:4, :] = sums[0:4, at]
+        small[r, 7:8, :] = sums[4:5, at]
+    for k in range(1, 8):
+        small_sent(small.at[(f + k) % 8], sm_a.at[k], k, same_seq[k - 1])
+    relay(1, 0)
+    relay(0, 0)
+    arrived(pair_recv, 78)
+    normed, scale = normalised(x_v[mine, :])
+    total = x_v[mine, :].astype(F32) + branches[mine, :] + pair_recv[0].astype(F32) + out_bias[...]
+    outputs[...] = total.astype(BF16)
+    w = weighted[mine, :] + pair_recv[1].astype(F32)
+    input_grad[...] = ct_v[mine, :].astype(F32) + scale * (
+        w
+        - jnp.mean(w, axis=-1, keepdims=True)
+        - normed * jnp.mean(w * normed, axis=-1, keepdims=True)
+    )
+    finish(2, 0)
+    begin(2, 1)
     for k in range(1, 8):
         small_arrived(sm_a.at[k], k)
     total = small[f]
@@ -538,88 +675,175 @@
     sm_b[0] = total
     for k in range(1, 16):
         small_sent(sm_b.at[0], sm_b.at[k], 7 + k, same_fsdp[k - 1])
-
-    for n in range(3):
-        keeps[4 * n + 2].wait()
-        keeps[4 * n + 3].wait()
-        finish(n, 0)
-        begin(n, 1)
-    for n in range(3):
+    finish(1, 0)
+    begin(1, 1)
+    finish(0, 0)
+    begin(0, 1)
+
+    across = device(y, (z + 2) % 4, px, core)
+    xp, xm = plus["x"], minus["x"]
+
+    def at_chip(n, zz, xx):
+        return bufs[n][6].at[core, zz * 4 + xx % 4]
+
+    def spread(n):
+        b = 26 * n + 18
+        done = grads[n].at[y, zl, zh, px]
+        place_ = at_chip(n, zh, px)
+        keep = pltpu.make_async_copy(done, place_, local_sem.at[9 + n])
+        keep.start()
+        started(done, place_, b, across)
+        started(done, place_, b + 1, xp)
+        started(done, place_, b + 2, xm)
+        return keep
+
+    def spread_on(n):
+        b = 26 * n + 18
+        theirs = at_chip(n, 1 - zh, px)
+        arrived(theirs, b)
+        started(theirs, theirs, b + 3, xp)
+        started(theirs, theirs, b + 4, xm)
+        left, right = at_chip(n, zh, px + 3), at_chip(n, 1 - zh, px + 1)
+        arrived(left, b + 1)
+        started(left, left, b + 5, xp)
+        arrived(right, b + 4)
+        started(right, right, b + 6, xm)
+
+    def spread_end(n, keep):
+        b = 26 * n + 18
+        arrived(at_chip(n, zh, px + 1), b + 2)
+        arrived(at_chip(n, 1 - zh, px + 3), b + 3)
+        arrived(at_chip(n, zh, px + 2), b + 5)
+        arrived(at_chip(n, 1 - zh, px + 2), b + 6)
+        keep.wait()
+        whole = bufs[n][6].at[core]
+        started(whole, whole, b + 7, sibling)
+
+    order = (2, 1, 0)
+    for n in order:
         relay(n, 1)
-    for n in range(3):
+    for n in order:
         finish(n, 1)
         begin(n, 2)
-    for n in range(3):
+    for n in order:
         relay(n, 2)
-
-    chip = px * 2 + zh
-    mine = zh * 4 + px
-    gathers = []
-    for n in range(3):
+    copies = {}
+    for n in order:
         finish(n, 2)
-        own, out = bufs[n][3], outs[n]
-        done = [own.at[zl, zh, px], own.at[y // 2, y % 2, px], own.at[zl, y, zh]][n]
-        keep = pltpu.make_async_copy(done, out.at[core, mine], local_sem.at[12 + n])
-        keep.start()
-        gathers.append(keep)
-        for k in range(1, 8):
-            j = (chip + k) % 8
-            started(done, out.at[core, mine], 26 * n + 17 + k, {"fsdp": f, "seq": j * 2 + core})
-    for n in range(3):
-        out = outs[n]
-        for k in range(1, 8):
-            j = (chip + 8 - k) % 8
-            arrived(out.at[core, (j % 2) * 4 + j // 2], 26 * n + 17 + k)
-        gathers[n].wait()
-        started(out.at[core], out.at[core], 26 * n + 25, sibling)
+        copies[n] = spread(n)
+    for n in order:
+        spread_on(n)
+    for n in order:
+        spread_end(n, copies[n])
     for k in range(1, 16):
         small_arrived(sm_b.at[k], 7 + k)
     total = sm_b[0]
     for k in range(1, 16):
         total = total + sm_b[k]
     small_out[...] = total
-    for n in range(3):
-        arrived(outs[n].at[1 - core], 26 * n + 25)
+
+    def finals(hidden_v, output_v, qkv_v, dense_v):
+        ends = []
+        a = bufs[2][6]
+        arrived(a.at[1 - core], 26 * 2 + 25)
+        low = lax.broadcasted_iota(jnp.int32, (128, 128), 1) < HEAD
+        for pair in range(4):
+            v0 = a[0, :, :, 1024 + pair * 128 : 1152 + pair * 128].reshape(128, 128).astype(F32)
+            v1 = a[1, :, :, 1024 + pair * 128 : 1152 + pair * 128].reshape(128, 128).astype(F32)
+            for j in range(2):
+                r = 2 * pair + j
+                q0 = a[0, :, :, r * 128 : r * 128 + 128].reshape(128, 128).astype(F32)
+                q1 = a[1, :, :, r * 128 : r * 128 + 128].reshape(128, 128).astype(F32)
+                q1 = pltpu.roll(q1, 64, 1)
+                left = v0 if j == 0 else pltpu.roll(v0, 64, 1)
+                right = pltpu.roll(v1, 64, 1) if j == 0 else v1
+                qkv_v[:, r * 384 : r * 384 + 128] = q0
+                qkv_v[:, r * 384 + 128 : r * 384 + 256] = jnp.where(low, left, q1)
+                qkv_v[:, r * 384 + 256 : r * 384 + 384] = jnp.where(low, q1, right)
+        for c in range(2):
+            for k in range(2):
+                piece = a[c, k * 4 : k * 4 + 4, :, 1536:2048].reshape(64, 512)
+                dense_v[c * 64 : c * 64 + 64, k * 512 : k * 512 + 512] = piece.astype(F32)
+        ends.append(load(qkv_v, qkv_out, 12))
+        ends.append(load(dense_v, dense_out, 13))
+        a1 = bufs[1][6]
+        arrived(a1.at[1 - core], 26 + 25)
+        output_v[...] = a1[...].reshape(512, D).astype(F32)
+        ends.append(load(output_v, output_out, 14))
+        a0 = bufs[0][6]
+        arrived(a0.at[1 - core], 25)
+        for c in range(2):
+            for r in range(8):
+                piece = a0[c, :, :, r * 256 : r * 256 + 256].reshape(128, 256)
+                hidden_v[:, r * 512 + c * 256 : r * 512 + c * 256 + 256] = piece.astype(F32)
+        ends.append(load(hidden_v, hidden_out, 15))
+        for copy in ends:
+            copy.wait()
+
+    pl.run_scoped(
+        finals,
+        pltpu.VMEM((128, FF), F32),
+        pltpu.VMEM((512, D), F32),
+        pltpu.VMEM((128, 3 * D), F32),
+        pltpu.VMEM((128, D), F32),
+    )
     for copy in sends:
         copy.wait_send()
-
-
-def reduce_all(parts, small, collective_id):
+    for n in range(3):
+        for stage in range(3):
+            for copy in raw_copies(n, stage):
+                copy.wait_send()
+            for h in range(2):
+                relay_copy(n, stage, h)[1].wait_send()
+
+
+def rest_of_block(*args):
     scratch = []
-    for part, lead in zip(parts, LEADS):
-        R, C = part.shape[-2:]
+    for lead, R, C in zip(LEADS, ROWS, COLUMNS):
         for dims in (
             (2, *lead, R, C),
             (2, 2, *lead, R, C),
-            (2, *lead, R, C),
-            (2, *lead, R, C),
             (2, 2, R, C),
             (2, 2, 2, R, C),
             (2, R, C // 2),
             (2, 2, R, C // 2),
+            (2, 8, R, C),
         ):
             scratch.append(pltpu.VMEM(dims, BF16))
-        scratch.append(pltpu.SemaphoreType.DMA)
-    outs = [jax.ShapeDtypeStruct((2, 8, *p.shape[-2:]), BF16) for p in parts]
+    T = CHIP_TOKENS
     return pl.pallas_call(
-        reduce_kernel,
-        out_shape=(*outs, jax.ShapeDtypeStruct((16, 128), F32)),
-        in_specs=[HBM, HBM, HBM, VMEM],
-        out_specs=(HBM, HBM, HBM, VMEM),
+        rest_kernel,
+        out_shape=(
+            jax.ShapeDtypeStruct((256, D), BF16),
+            jax.ShapeDtypeStruct((256, D), F32),
+            jax.ShapeDtypeStruct((128, FF), F32),
+            jax.ShapeDtypeStruct((512, D), F32),
+            jax.ShapeDtypeStruct((128, 3 * D), F32),
+            jax.ShapeDtypeStruct((128, D), F32),
+            jax.ShapeDtypeStruct((16, 128), F32),
+        ),
+        in_specs=[HBM] * 9 + [VMEM] * 4,
+        out_specs=(VMEM, VMEM, HBM, HBM, HBM, HBM, VMEM),
         scratch_shapes=[
-            *scratch,
+            *[pltpu.VMEM((T, D), BF16)] * 4,
+            *[pltpu.VMEM((T, D), F32)] * 2,
+            pltpu.VMEM((8, D), F32),
+            pltpu.VMEM((8, 16, 128), F32),
             pltpu.VMEM((8, 16, 128), F32),
             pltpu.VMEM((16, 16, 128), F32),
-            pltpu.SemaphoreType.DMA((78,)),
-            pltpu.SemaphoreType.DMA((78,)),
-            pltpu.SemaphoreType.DMA((15,)),
+            *[pltpu.VMEM((2, 256, D), BF16)] * 2,
+            *[pltpu.VMEM((4, 2, 2, 4, R, C), BF16) for R, C in zip(ROWS, COLUMNS)],
+            *scratch,
+            pltpu.SemaphoreType.DMA((79,)),
+            pltpu.SemaphoreType.DMA((79,)),
+            pltpu.SemaphoreType.DMA((16,)),
             pltpu.SemaphoreType.DMA((23,)),
             pltpu.SemaphoreType.DMA((23,)),
         ],
         compiler_params=pltpu.CompilerParams(
-            collective_id=collective_id, has_side_effects=True, vmem_limit_bytes=48 * MIB
+            collective_id=2, has_side_effects=True, vmem_limit_bytes=62 * MIB
         ),
-    )(*parts, small)
+    )(*args)
 
 
 def turn(values, tables, sign):
@@ -667,40 +891,6 @@
     )(x, ct, wq, wd, vectors, bias, tables)
 
 
-def back_kernel(packed, tables, grad, attended, bias):
-    low = lax.broadcasted_iota(jnp.int32, (CHIP_TOKENS, 128), 1) < HEAD
-    rotary = (tables[0], tables[1], tables[2])
-    for pair in range(4):
-        for j in range(2):
-            at = slice((2 * pair + j) * 128, (2 * pair + j) * 128 + 128)
-            turned = turn(packed[2 * pair + j, :, 0:128].astype(F32), rotary, -1.0).astype(BF16)
-            grad[:, at] = turned
-            bias[0:1, at] = jnp.sum(turned.astype(F32), axis=0, keepdims=True)
-        a = packed[2 * pair, :, 128:256].astype(F32)
-        b = packed[2 * pair + 1, :, 128:256].astype(F32)
-        at = slice(1024 + pair * 128, 1024 + pair * 128 + 128)
-        v = jnp.where(low, a, pltpu.roll(b, 64, 1))
-        grad[:, at] = v.astype(BF16)
-        bias[0:1, at] = jnp.sum(v, axis=0, keepdims=True)
-        o = jnp.where(low, pltpu.roll(a, 64, 1), b)
-        attended[:, pair * 128 : pair * 128 + 128] = o.astype(BF16)
-
-
-def back(packed, tables):
-    T = CHIP_TOKENS
-    return pl.pallas_call(
-        back_kernel,
-        out_shape=(
-            jax.ShapeDtypeStruct((T, 1536), BF16),
-            jax.ShapeDtypeStruct((T, 512), BF16),
-            jax.ShapeDtypeStruct((1, 1536), F32),
-        ),
-        in_specs=[VMEM] * 2,
-        out_specs=(VMEM,) * 3,
-        compiler_params=pltpu.CompilerParams(vmem_limit_bytes=48 * MIB),
-    )(packed, tables)
-
-
 def rotary_tables(first_position):
     half = ROT // 2
     frequency = 10000.0 ** (-2.0 * jnp.arange(half, dtype=F32) / ROT)
@@ -717,12 +907,6 @@
         jnp.concatenate([none, sine, zero] * 2, axis=1),
     ]
     return jnp.stack(rows)
-
-
-def gelu_and_slope(h):
-    below = 0.5 * lax.erfc(-h * math.sqrt(0.5))
-    density = jnp.exp(-0.5 * h * h) * (1.0 / math.sqrt(2.0 * math.pi))
-    return h * below, below + h * density
 
 
 def local(
@@ -788,113 +972,25 @@
     tokens, wh, wo = attention(packed, own_hidden, output_weight)
     wh = wh.reshape(D, 2048)
     wo = wo.reshape(2048, D)
-    projected_grad, attended, head_bias_grad = back(tokens, tables)
-
-    hidden = jnp.dot(mlp_normed, wh, preferred_element_type=F32) + unit_bias
-    active, slope = gelu_and_slope(hidden)
-    active = active.astype(BF16)
-    active_grad = lax.dot_general(ct, wo, NT, preferred_element_type=F32)
-    hidden_grad = (active_grad * slope).astype(BF16)
-    output_weight_grad = lax.dot_general(active, ct, TN, preferred_element_type=F32)
-    hidden_weight_grad = lax.dot_general(mlp_normed, hidden_grad, TN, preferred_element_type=F32)
-    mlp_norm_grad = lax.dot_general(hidden_grad, wh, NT, preferred_element_type=F32)
-    hidden_bias_grad = jnp.sum(hidden_grad.astype(F32), axis=0)
-
-    branches = jnp.dot(attended, wd, preferred_element_type=F32) + jnp.dot(
-        active, wo, preferred_element_type=F32
-    )
-    attn_norm_grad = lax.dot_general(projected_grad, wq, NT, preferred_element_type=F32)
-    weighted = attn_norm_grad * norms[0:1] + mlp_norm_grad * norms[2:3]
-    qkv_weight_grad = lax.dot_general(attn_normed, projected_grad, TN, preferred_element_type=F32)
-    dense_weight_grad = lax.dot_general(attended, ct, TN, preferred_element_type=F32)
-
-    values = x.astype(F32)
-    centered = values - jnp.mean(values, axis=-1, keepdims=True)
-    variance = jnp.mean(centered * centered, axis=-1, keepdims=True)
-    scale = lax.rsqrt(variance + epsilon)
-    normed = centered * scale
-    attn_gain_grad = jnp.sum(attn_norm_grad * normed, axis=0)
-    attn_bias_grad = jnp.sum(attn_norm_grad, axis=0)
-    mlp_gain_grad = jnp.sum(mlp_norm_grad * normed, axis=0)
-    mlp_bias_grad = jnp.sum(mlp_norm_grad, axis=0)
-
-    def rows(a, c):
-        return lax.dynamic_slice_in_dim(a, c * 256, 256, 0)
-
-    swap = [(i, i + 1 - 2 * (i % 2)) for i in range(16)]
-    given = jnp.concatenate(
-        [rows(branches, 1 - core).astype(BF16), rows(weighted, 1 - core).astype(BF16)]
-    )
-    taken = lax.ppermute(given, "seq", swap).astype(F32)
-    outputs = inputs.astype(F32) + rows(branches, core) + taken[:256] + out_bias
-    w = rows(weighted, core) + taken[256:]
-    n = rows(normed, core)
-    input_grad = cotangent.astype(F32) + rows(scale, core) * (
-        w - jnp.mean(w, axis=-1, keepdims=True) - n * jnp.mean(w * n, axis=-1, keepdims=True)
-    )
-
-    mine = (jnp.arange(2) == core).astype(F32)
-    cotangent_sum = jnp.sum(cotangent.astype(F32), axis=0)
-    per_head = jnp.concatenate(
-        [head_bias_grad[0, :1024].reshape(8, 128), head_bias_grad[0, 1024:].reshape(8, 64)], axis=1
-    )
-    small_grads = jnp.concatenate(
-        [
-            attn_gain_grad.reshape(8, 1, 128),
-            attn_bias_grad.reshape(8, 1, 128),
-            mlp_gain_grad.reshape(8, 1, 128),
-            mlp_bias_grad.reshape(8, 1, 128),
-            (per_head[:, None, :] * mine[None, :, None]).reshape(8, 3, 128),
-            cotangent_sum.reshape(8, 1, 128),
-            (hidden_bias_grad.reshape(8, 1, 256) * mine[None, :, None]).reshape(8, 4, 128),
-            jnp.zeros((8, 4, 128), F32),
-        ],
-        axis=1,
-    )
-    dense_part = dense_weight_grad.astype(BF16).reshape(8, 64, 2, 512).transpose(0, 2, 1, 3)
-    heads_part = jnp.concatenate(
-        [qkv_weight_grad.astype(BF16).reshape(8, 128, 1536), dense_part.reshape(8, 128, 512)],
-        axis=2,
-    )
-    hidden_sum, output_sum, heads_sum, small_sum = reduce_all(
-        (
-            hidden_weight_grad.astype(BF16).reshape(4, 2, 2, 4, 16, 2048),
-            output_weight_grad.astype(BF16).reshape(4, 2, 2, 4, 32, 1024),
-            heads_part.reshape(4, 2, 2, 4, 16, 2048),
-        ),
-        small_grads,
-        3,
-    )
-    hidden_total = (
-        hidden_sum.reshape(2, 128, 8, 256).transpose(1, 2, 0, 3).reshape(128, FF).astype(F32)
-    )
-    output_total = output_sum.reshape(512, D).astype(F32)
-    heads_sum = heads_sum.reshape(2, 128, 2048)
-    qkv_total = jnp.concatenate(
-        [
-            heads_sum[:, :, :1024].reshape(2, 128, 8, 128),
-            heads_sum[:, :, 1024:1536].reshape(2, 128, 8, 64),
-        ],
-        axis=3,
-    )
-    qkv_total = qkv_total.transpose(1, 2, 0, 3).reshape(128, 3 * D).astype(F32)
-    dense_total = heads_sum[:, :, 1536:].reshape(2, 2, 64, 512).transpose(0, 2, 1, 3)
-    dense_total = dense_total.reshape(128, D).astype(F32)
+    outputs, input_grad, hidden_total, output_total, qkv_total, dense_total, sums = rest_of_block(
+        tokens, x, ct, attn_normed, mlp_normed, wq, wd, wh, wo, norms, unit_bias, out_bias, tables
+    )
+    head_bias_total = jnp.concatenate([sums[4], sums[6, :64], sums[5], sums[6, 64:]])
     return (
-        outputs.astype(BF16),
+        outputs,
         input_grad,
-        small_sum[0],
-        small_sum[1],
-        small_sum[2],
-        small_sum[3],
+        sums[0],
+        sums[1],
+        sums[2],
+        sums[3],
         qkv_total,
-        small_sum[4:7].reshape(384),
+        head_bias_total,
         dense_total,
-        small_sum[7],
+        sums[7],
         hidden_total,
-        small_sum[8:12].reshape(512),
+        sums[8:12].reshape(512),
         output_total,
-        small_sum[7],
+        sums[7],
     )
 
 

time: 377 us -> 323 us (0.86); the launches traced: 370 us -> 322 us
  matrix products: 51.3 us -> 0 us
  Pallas kernels: 253 us -> 285 us
  other arithmetic: 18.3 us -> 3.86 us
  local copies, waits for them, and re-layouts: 43 us -> 32.2 us
    dot_general x10 -> x0, matrix products: 51.3 us -> none  [the longest x1 13.6 us: local(): hidden = jnp.dot(mlp_normed, wh, preferred_element_type=F32) + unit_bias]
    pallas_call x2 -> x1, Pallas kernels: 80.7 us -> 113 us  [rest_of_block(): pl.pallas_call(rest_kernel, out_shape=(jax.ShapeDtypeStruct((256, D), BF1...]
    convert_element_type x6 -> x0, local copies, waits for them, and re-layouts: 6.14 us -> none  [the longest x3 4.46 us: local(): hidden_sum.reshape(2, 128, 8, 256).transpose(1, 2, 0, 3).reshape(128, FF)]
    concatenate x3 -> x1, other arithmetic: 6.06 us -> 0.65 us  [local(): jnp.concatenate([sums[4], sums[6, :64], sums[5], sums[6, 64:]])]
    unnamed x78 -> x38, local copies, waits for them, and re-layouts: 12.8 us -> 18.2 us
    reshape x4 -> x2, local copies, waits for them, and re-layouts: 6.43 us -> 1.26 us  [the longest x1 1.26 us: local(): sums[8:12].reshape(512)]
  transfers between devices with their start and end apart: 1 -> 0, of which waited for: 0 -> 0; matrix products, arithmetic and copies ran while one was open for 7% -> 0% of each run, Pallas kernels for 0% -> 0%
where the time goes in v1:
time: 323 us; the launch traced here: 322 us
  Pallas kernels  285 us (88%)
  local copies, waits for them, and re-layouts  32.2 us (10%)
  other arithmetic  3.86 us (1%)
    pallas_call x1, Pallas kernels, rest_of_block(): pl.pallas_call(rest_kernel, out_shape=(jax.ShapeDtypeStruct((256, D), BF1...  113 us
    pallas_call x1, Pallas kernels, attention(): pl.pallas_call(attention_kernel, out_shape=(jax.ShapeDtypeStruct((CHIPS,...  111 us
    pallas_call x1, Pallas kernels, gather(): pl.pallas_call(gather_kernel, out_shape=(shape(8, 128, 1536), shape(8, 64...  54.7 us
    unnamed x38, local copies, waits for them, and re-layouts  18.2 us
    pallas_call x1, Pallas kernels, front(): pl.pallas_call(front_kernel, out_shape=(jax.ShapeDtypeStruct((8, T, 256),...  7.32 us

profile of v1, /device:TPU:1, one launch (start us, length us, event | category | flops | bytes accessed | tf_op | source)
XLA Modules:
  0.0 322.4 jit_solution(3996967151351040590)
XLA Ops:
  0.7 2.6 concatenate.22.small
  3.3 1.0 multiply_cosine_fusion
  4.4 0.4 concatenate.24
  4.8 0.4 concatenate.25
  5.3 0.0 copy-start.11
  5.3 0.4 concatenate.26
  5.7 0.1 pad_maximum_fusion.tables
  5.8 0.6 copy-done.11
  6.4 0.4 copy.35
  6.9 0.1 copy.41
  7.0 0.1 copy.37
  7.2 0.8 pad_maximum_fusion.1.wq
  7.9 0.0 copy-done.10
  7.9 0.8 reshape.156
  8.7 3.1 dynamic-slice_reduce_fusion
  11.8 0.9 copy.45
  12.7 54.7 %shard_map.245 = (bf16[8,128,1536]{2,1,0:T(8,128)(2,1)}, bf16[8,64,1024]{2,1,0:T(8,128)(2,1)}, bf16[8,16,128]{2,1,0:T(8,128)(2,1)}, bf16[2,256,1024]{2,1,0:T(8,128)(2,1)}, bf16[2,256,1024]{2,1,0:T(8,128)(2,1)}) custom-call(bf16[128,1536]{1,0:T(8,128)(2,1)} %pad_maximum_fusion.1.wq, bf16[128,1024]{1,0:T(8,128)(2,1)} %wd.1, ...), custom_call_target="tpu_custom_call" | custom-call | tf_op jit(solution)/shard_map/pallas_call | solution.py:162
  67.4 0.7 slice.83
  68.2 0.6 constant_dynamic-slice_fusion
  68.8 0.7 slice.80
  69.5 0.1 reshape.153
  69.6 0.1 reshape.155
  69.7 0.8 convert_element_type.10
  70.5 0.6 fusion.1.out_bias
  71.1 0.0 copy-done
  71.1 1.2 copy-done.1
  72.3 1.2 copy-done.2
  73.6 1.2 copy-done.3
  74.8 7.3 %shard_map.246 = (bf16[8,512,256]{2,1,0:T(8,128)(2,1)}, bf16[512,1024]{1,0:T(8,128)(2,1)S(1)}, bf16[512,1024]{1,0:T(8,128)(2,1)S(1)}) custom-call(bf16[512,1024]{1,0:T(8,128)(2,1)S(1)} %bitcast.58, bf16[512,1024]{1,0:T(8,128)(2,1)S(1)} %bitcast.60, bf16[1024,1536]{1,0:T(8,128)(2,1)} %bitcast.61, bf16[512,1024]{1,0:T(8,128)(2,1)S(1)} %bitcast.56, ...), custom_call_target="tpu_custom_call" | custom-call | tf_op jit(solution)/shard_map/pallas_call | solution.py:881
  82.1 0.0 copy-done.6
  82.1 1.0 copy-done.4
  83.1 1.0 copy-done.5
  84.0 110.7 %shard_map.247 = (bf16[8,512,256]{2,1,0:T(8,128)(2,1)}, bf16[8,128,2048]{2,1,0:T(8,128)(2,1)}, bf16[8,256,1024]{2,1,0:T(8,128)(2,1)}) custom-call(bf16[8,512,256]{2,1,0:T(8,128)(2,1)} %get-tuple-element.37.packed, bf16[128,2048]{1,0:T(8,128)(2,1)} %bitcast.65, bf16[512,1024]{1,0:T(8,128)(2,1)} %wo.1), custom_call_target="tpu_custom_call" | custom-call | tf_op jit(solution)/shard_map/pallas_call | solution.py:336
  194.8 112.7 %shard_map.248 = (bf16[256,1024]{1,0:T(8,128)(2,1)}, f32[256,1024]{1,0:T(8,128)}, f32[128,4096]{1,0:T(8,128)}, f32[512,1024]{1,0:T(8,128)}, f32[128,3072]{1,0:T(...) custom-call(bf16[8,512,256]{2,1,0:T(8,128)(2,1)} %get-tuple-element.38.tokens, bf16[512,1024]{1,0:T(8,128)(2,1)} %bitcast.57, ...), custom_call_target="tpu_custom_call" | custom-call | tf_op jit(solution)/shard_map/pallas_call | solution.py:814
  307.5 0.9 slice_bitcast_fusion.5
  308.3 1.3 slice_bitcast_fusion.1
  309.6 1.5 slice_bitcast_fusion.2
  311.1 0.7 pad_maximum_fusion.3
  311.7 0.5 copy.55
  312.2 1.9 copy.56
  314.1 2.3 copy.57
  316.4 1.1 copy.58
  317.5 0.2 copy-done.12
  317.8 0.8 copy.59
  318.6 0.2 copy-done.8
  318.7 1.3 copy.60
  320.1 1.0 copy-done.7
  321.1 1.3 copy.61
  (31 shorter events, 0.2 us)
Async XLA Ops:
  5.3 1.1 copy-start.11
  6.4 64.7 %copy-start = (f32[3,512,128]{2,1,0:T(8,128)}, f32[3,512,128]{2,1,0:T(8,128)S(1)}, u32[]{:S(2)}) copy-start(f32[3,512,128]{2,1,0:T(8,128)S(1)} %pad_maximum_fusion.tables) | copy-start | bytes 2359300
  6.4 1.5 copy-start.10
  71.1 1.2 copy-start.1
  72.3 1.2 copy-start.2
  73.6 1.2 copy-start.3
  74.8 7.3 %copy-start.6 = (f32[4,1024]{1,0:T(4,128)}, f32[4,1024]{1,0:T(4,128)S(1)}, u32[]{:S(2)}) copy-start(f32[4,1024]{1,0:T(4,128)S(1)} %slice_bitcast_fusion.vectors.norms) | copy-start | bytes 49156
  82.1 1.0 copy-start.4
  83.1 1.0 copy-start.5
  307.5 8.9 %copy-start.9 = (f32[128,3072]{1,0:T(8,128)S(1)}, f32[128,3072]{1,0:T(8,128)}, u32[]{:S(2)}) copy-start(f32[128,3072]{1,0:T(8,128)} %get-tuple-element.110) | copy-start | bytes 4718596
  311.1 6.5 %copy-start.13 = (f32[128]{0:T(128)}, f32[128]{0:T(128)S(1)}, u32[]{:S(2)}) copy-start(f32[128]{0:T(128)S(1)} %get-tuple-element.113) | copy-start | bytes 1540
  316.4 1.4 copy-start.12
  316.4 2.3 copy-start.8
  318.7 2.3 copy-start.7

commit v2 on v1

--- a/solution.py
+++ b/solution.py
@@ -3,6 +3,7 @@
 
 import jax
 import jax.numpy as jnp
+import numpy as np
 from jax import lax
 from jax.experimental import pallas as pl
 from jax.experimental.pallas import tpu as pltpu
@@ -102,10 +103,16 @@
         for kk, target in targets:
             self.started(ref, ref, 14 * n + kk, target)
 
-    def near(self):
+    def near_y(self):
         for n in range(len(self.full)):
-            self.pass_on(n, 0, self.slots[1], 0, [(4, self.yp), (7, self.zp)])
-            self.pass_on(n, 3, self.slots[2], 1, [(5, self.ym), (12, self.zm)])
+            self.pass_on(n, 0, self.slots[1], 0, [(4, self.yp)])
+            self.pass_on(n, 3, self.slots[2], 1, [(5, self.ym)])
+
+    def near_z(self):
+        for n, g in enumerate(self.full):
+            for k, slot, h, target in ((7, 1, 0, self.zp), (12, 2, 1, self.zm)):
+                ref = self.part(g.at[self.slots[slot]], h)
+                self.started(ref, ref, 14 * n + k, target)
             self.pass_on(n, 2, self.slots[2], 0, [(8, self.zp)])
             self.pass_on(n, 1, self.slots[1], 1, [(11, self.zm)])
 
@@ -123,62 +130,6 @@
             copy.wait_send()
 
 
-def gather_kernel(wq, wd, small, x, ct, gq, gd, gs, gx, gc, send, recv, local_sem):
-    f, s, (y, zl, px, zh, core) = place()
-    sibling = device(y, zh * 2 + zl, px, 1 - core)
-    others = [{"fsdp": (f + k) % 8, "seq": s} for k in range(1, 8)]
-    zother = device(y, 2 * (1 - zh) + 1 - zl, px, core)
-    own = [wq, wd.at[pl.ds(pl.multiple_of(core * 64, 64), 64)]]
-    weights = Gather(own, [gq, gd], send, recv)
-    barrier(others + [sibling, zother])
-    base = 28
-    weights.own_y()
-    weights.started(x, gx.at[core], base, sibling)
-    weights.started(ct, gc.at[core], base + 1, sibling)
-    for k in range(1, 8):
-        weights.started(small, gs.at[f], base + 1 + k, others[k - 1])
-    weights.own_z()
-    pairs = [(gx.at[core], x), (gc.at[core], ct), (gs.at[f], small), (gq.at[f], own[0]), (gd.at[f], own[1])]
-    keeps = []
-    for k, (b, a) in enumerate(pairs):
-        copy = pltpu.make_async_copy(a, b, local_sem.at[k])
-        copy.start()
-        keeps.append(copy)
-    weights.near()
-    weights.opposite()
-    weights.arrived(gx.at[1 - core], base)
-    weights.arrived(gc.at[1 - core], base + 1)
-    for k in range(1, 8):
-        weights.arrived(gs.at[(f + 8 - k) % 8], base + 1 + k)
-    weights.finish()
-    for copy in keeps:
-        copy.wait()
-
-
-def gather(wq, wd, small, x, ct):
-    def shape(*dims):
-        return jax.ShapeDtypeStruct(dims, BF16)
-
-    return pl.pallas_call(
-        gather_kernel,
-        out_shape=(
-            shape(8, 128, 1536),
-            shape(8, 64, 1024),
-            shape(8, 16, 128),
-            shape(2, 256, 1024),
-            shape(2, 256, 1024),
-        ),
-        in_specs=[HBM] * 5,
-        out_specs=(HBM,) * 5,
-        scratch_shapes=[
-            pltpu.SemaphoreType.DMA((37,)),
-            pltpu.SemaphoreType.DMA((37,)),
-            pltpu.SemaphoreType.DMA((5,)),
-        ],
-        compiler_params=pltpu.CompilerParams(collective_id=0, has_side_effects=True),
-    )(wq, wd, small, x, ct)
-
-
 def fold(op, a):
     result = a[:, :128]
     for j in range(128, a.shape[1], 128):
@@ -187,39 +138,163 @@
 
 
 def attention_kernel(
-    packed, wh, wo, result, gh, go,
+    qkv_w, dense_w, hidden_w, output_w, small, x, ct, cosine, sine,
+    result, gh, go, wq_out, wd_out, x_out, ct_out, an_out, mn_out, vectors,
+    raw_q, own_q, own_h, own_o, wq, wd, x_v, ct_v, an, mn, vec, norms, bias, tables, packed,
     hd, out, q_s, k_s, v_s, d_s, s_s, p_s, dk_s, dv_s, mx_s, l_s, o_s, dq_s,
-    in_send, in_recv, out_send, out_recv, g_send, g_recv, local_sem,
+    in_send, in_recv, out_send, out_recv, a_send, a_recv, g_send, g_recv, local_sem,
 ):
     f, s, (y, zl, px, zh, core) = place()
     me = s // 2
     B = CHIP_TOKENS
     n = CHIPS
     scale = 1.0 / math.sqrt(HEAD)
-    own = [wh, wo.at[pl.ds(pl.multiple_of(core * 256, 256), 256)]]
-    weights = Gather(own, [gh, go], g_send, g_recv)
+    sibling = device(y, zh * 2 + zl, px, 1 - core)
+    others = [{"fsdp": (f + k) % 8, "seq": s} for k in range(1, 8)]
+    zother = device(y, 2 * (1 - zh) + 1 - zl, px, core)
 
     def chip(j):
         return {"fsdp": f, "seq": j * 2 + core}
 
-    barrier([chip((me + k) % n) for k in range(1, n)] + weights.neighbours())
-    given = []
+    greeted = others + [sibling, zother] + [chip((me + k) % n) for k in range(1, n)]
+    entered = pltpu.get_barrier_semaphore()
+    for d in greeted:
+        pl.semaphore_signal(entered, inc=1, device_id=d, device_id_type=pl.DeviceIdType.MESH)
+
+    def load(src, dst, k):
+        copy = pltpu.make_async_copy(src, dst, local_sem.at[k])
+        copy.start()
+        return copy
+
+    own_d = dense_w.at[pl.ds(pl.multiple_of(core * 64, 64), 64)]
+    here = pl.ds(pl.multiple_of(me * B, B), B)
+    load_q = load(qkv_w, raw_q, 0)
+    loads = [
+        load(own_d, wd.at[f], 1),
+        load(x, x_v.at[core], 2),
+        load(ct, ct_v.at[core], 3),
+        load(small, vec.at[f], 4),
+        load(cosine.at[here], tables.at[0], 5),
+        load(sine.at[here], tables.at[1], 6),
+    ]
+    load_o = load(output_w.at[pl.ds(pl.multiple_of(core * 256, 256), 256)], own_o, 7)
+    load_h = [
+        load(
+            hidden_w.at[:, pl.ds(pl.multiple_of(r * 512 + core * 256, 256), 256)],
+            own_h.at[:, pl.ds(r * 256, 256)],
+            8 + r,
+        )
+        for r in range(8)
+    ]
+    load_q.wait()
+    low = lax.broadcasted_iota(jnp.int32, (128, 128), 1) < HEAD
+    even = core == 0
+    held = None
+    for r in range(8):
+        t0, t1, t2 = [raw_q[:, r * 384 + j * 128 : r * 384 + j * 128 + 128].astype(F32) for j in range(3)]
+        t2 = pltpu.roll(t2, 64, 1)
+        qk = jnp.where(even, t0, jnp.where(low, pltpu.roll(t1, 64, 1), t2))
+        v = jnp.where(even, t1, t2)
+        own_q[:, r * 128 : r * 128 + 128] = qk.astype(BF16)
+        if r % 2 == 0:
+            held = v
+        else:
+            at = 1024 + r // 2 * 128
+            own_q[:, at : at + 128] = jnp.where(low, held, pltpu.roll(v, 64, 1)).astype(BF16)
+    pl.semaphore_wait(entered, len(greeted))
+
+    heads = Gather([own_q, own_d], [wq, wd], a_send, a_recv)
+    units = Gather([own_h, own_o], [gh, go], g_send, g_recv)
+    heads.own_y()
+    heads.started(x, x_v.at[core], 28, sibling)
+    heads.started(ct, ct_v.at[core], 29, sibling)
+    for k in range(1, 8):
+        heads.started(small, vec.at[f], 29 + k, others[k - 1])
+    heads.own_z()
+    wq[f] = own_q[...]
+
+    for copy in loads:
+        copy.wait()
+    heads.arrived(x_v.at[1 - core], 28)
+    for k in range(1, 8):
+        heads.arrived(vec.at[(f + 8 - k) % 8], 29 + k)
+    heads.near_y()
+    for r in range(8):
+        at = slice(r * 128, r * 128 + 128)
+        norms[0:4, at] = vec[r, 0:4, :]
+        bias[0:1, at] = vec[r, pl.ds(4 + core, 1), :]
+    first = low[0:1, :]
+    for pair in range(4):
+        a, b = vec[2 * pair, 6:7, :], vec[2 * pair + 1, 6:7, :]
+        v_even = jnp.where(first, a, pltpu.roll(b, 64, 1))
+        v_odd = jnp.where(first, pltpu.roll(a, 64, 1), b)
+        at = slice(1024 + pair * 128, 1152 + pair * 128)
+        bias[0:1, at] = jnp.where(even, v_even, v_odd)
+    for c in range(2):
+        rows = slice(c * 256, c * 256 + 256)
+        normed, _ = normalised(x_v[c])
+        an[rows, :] = (normed * norms[0:1, :] + norms[1:2, :]).astype(BF16)
+        mn[rows, :] = (normed * norms[2:3, :] + norms[3:4, :]).astype(BF16)
+        if c == 0:
+            heads.near_z()
+    heads.opposite()
+    heads.arrived(ct_v.at[1 - core], 29)
+    load_o.wait()
+    for copy in load_h:
+        copy.wait()
+    units.own_y()
+    heads.finish()
+
+    def given(j):
+        return remote(packed.at[j], hd.at[me], in_send.at[j], in_recv.at[me], chip(j))
+
+    wide = lax.broadcasted_iota(jnp.int32, (B, 128), 1) < HEAD
+    rotary = (tables[0], tables[1])
+    tokens = ct_v[...].reshape(B, D)
+    for pair in range(4):
+        a = an[...]
+        qk = slice(pair * 256, pair * 256 + 256)
+        vs = slice(1024 + pair * 128, 1024 + pair * 128 + 128)
+        weight = wq[:, :, qk].reshape(D, 256)
+        projected = jnp.dot(a, weight, preferred_element_type=F32) + bias[0:1, qk]
+        for j in range(2):
+            turned = turn(projected[:, j * 128 : j * 128 + 128], rotary, 1.0)
+            packed[2 * pair + j, :, 0:128] = turned.astype(BF16)
+        weight = wq[:, :, vs].reshape(D, 128)
+        v = jnp.dot(a, weight, preferred_element_type=F32) + bias[0:1, vs]
+        weight = wd[2 * pair : 2 * pair + 2].reshape(128, D)
+        d = lax.dot_general(tokens, weight, NT, preferred_element_type=F32)
+        packed[2 * pair, :, 128:256] = jnp.where(wide, v, pltpu.roll(d, 64, 1)).astype(BF16)
+        packed[2 * pair + 1, :, 128:256] = jnp.where(wide, pltpu.roll(v, 64, 1), d).astype(BF16)
+        for j in (2 * pair, 2 * pair + 1):
+
+            @pl.when(me != j)
+            def _():
+                given(j).start()
+
+    hd[me] = packed[me]
+    units.near_y()
+    saves = [
+        load(a, b, 16 + k)
+        for k, (a, b) in enumerate(
+            [
+                (own_h, gh.at[f]),
+                (own_o, go.at[f]),
+                (wq, wq_out),
+                (wd, wd_out),
+                (x_v, x_out),
+                (ct_v, ct_out),
+                (an, an_out),
+                (mn, mn_out),
+                (vec, vectors),
+            ]
+        )
+    ]
     for k in range(1, n):
-        j = (me + k) % n
-        copy = remote(packed.at[j], hd.at[me], in_send.at[k], in_recv.at[k], chip(j))
-        copy.start()
-        given.append(copy)
-    weights.own_y()
-    keeps = []
-    for k, (a, b) in enumerate([(packed.at[me], hd.at[me]), (own[0], gh.at[f]), (own[1], go.at[f])]):
-        copy = pltpu.make_async_copy(a, b, local_sem.at[k])
-        copy.start()
-        keeps.append(copy)
-    keeps[0].wait()
-    for k in range(1, n):
-        ref = hd.at[(me + n - k) % n]
-        remote(ref, ref, in_send.at[k], in_recv.at[k], chip(me)).wait_recv()
-    weights.own_z()
+        j = (me + n - k) % n
+        remote(hd.at[j], hd.at[j], in_send.at[j], in_recv.at[j], chip(j)).wait_recv()
+    units.own_z()
+    units.near_z()
 
     def block(i):
         return pl.ds(pl.multiple_of(i * B, B), B)
@@ -306,44 +381,65 @@
 
         @pl.when(i == me)
         def _():
-            pltpu.make_async_copy(out.at[i], result.at[i], local_sem.at[3]).start()
+            pltpu.make_async_copy(out.at[i], result.at[i], local_sem.at[25]).start()
 
         return 0
 
     lax.fori_loop(0, 1, query_block, 0)
-    weights.near()
-    lax.fori_loop(1, 2, query_block, 0)
-    weights.opposite()
-    lax.fori_loop(2, n, query_block, 0)
-
-    for copy in given:
-        copy.wait_send()
-    keeps[1].wait()
-    keeps[2].wait()
-    weights.finish()
+    units.opposite()
+    lax.fori_loop(1, n, query_block, 0)
+
+    for k in range(1, n):
+        given((me + k) % n).wait_send()
+    for copy in saves:
+        copy.wait()
+    units.finish()
     for k in range(1, n):
         back_to((me + k) % n).wait_send()
-    pltpu.make_async_copy(out.at[me], result.at[me], local_sem.at[3]).wait()
+    pltpu.make_async_copy(out.at[me], result.at[me], local_sem.at[25]).wait()
     for k in range(1, n):
         j = (me + k) % n
         ref = result.at[j]
         remote(ref, ref, out_send.at[j], out_recv.at[j], chip(me)).wait_recv()
 
 
-def attention(packed, wh, wo):
+def attention(*args):
     B = CHIP_TOKENS
     L = CHIPS * B
+
+    def shape(*dims):
+        return jax.ShapeDtypeStruct(dims, BF16)
+
     return pl.pallas_call(
         attention_kernel,
         out_shape=(
-            jax.ShapeDtypeStruct((CHIPS, B, 4 * HEAD), BF16),
-            jax.ShapeDtypeStruct((8, 128, 2048), BF16),
-            jax.ShapeDtypeStruct((8, 256, 1024), BF16),
+            shape(CHIPS, B, 4 * HEAD),
+            shape(8, 128, 2048),
+            shape(8, 256, 1024),
+            shape(8, 128, 1536),
+            shape(8, 64, 1024),
+            shape(2, 256, D),
+            shape(2, 256, D),
+            shape(B, D),
+            shape(B, D),
+            jax.ShapeDtypeStruct((8, 16, 128), F32),
         ),
-        in_specs=[HBM] * 3,
-        out_specs=(HBM,) * 3,
+        in_specs=[HBM] * 9,
+        out_specs=(HBM,) * 10,
         scratch_shapes=[
-            *[pltpu.VMEM((CHIPS, B, 4 * HEAD), BF16)] * 2,
+            pltpu.VMEM((128, 3072), BF16),
+            pltpu.VMEM((128, 1536), BF16),
+            pltpu.VMEM((128, 2048), BF16),
+            pltpu.VMEM((256, 1024), BF16),
+            pltpu.VMEM((8, 128, 1536), BF16),
+            pltpu.VMEM((8, 64, 1024), BF16),
+            *[pltpu.VMEM((2, 256, D), BF16)] * 2,
+            *[pltpu.VMEM((B, D), BF16)] * 2,
+            pltpu.VMEM((8, 16, 128), F32),
+            pltpu.VMEM((8, D), F32),
+            pltpu.VMEM((8, 1536), F32),
+            pltpu.VMEM((2, B, 128), F32),
+            *[pltpu.VMEM((CHIPS, B, 4 * HEAD), BF16)] * 3,
             *[pltpu.VMEM((L, HEAD), BF16)] * 4,
             pltpu.VMEM((L // B, B, B), F32),
             pltpu.VMEM((L // B, B, B), BF16),
@@ -351,13 +447,14 @@
             *[pltpu.VMEM((B, 128), F32)] * 2,
             *[pltpu.VMEM((B, HEAD), F32)] * 2,
             *[pltpu.SemaphoreType.DMA((CHIPS,))] * 4,
+            *[pltpu.SemaphoreType.DMA((37,))] * 2,
             *[pltpu.SemaphoreType.DMA((28,))] * 2,
-            pltpu.SemaphoreType.DMA((4,)),
+            pltpu.SemaphoreType.DMA((26,)),
         ],
         compiler_params=pltpu.CompilerParams(
-            collective_id=1, has_side_effects=True, vmem_limit_bytes=56 * MIB
+            collective_id=1, has_side_effects=True, vmem_limit_bytes=60 * MIB
         ),
-    )(packed, wh, wo)
+    )(*args)
 
 
 ORDERS = ("yzx", "zxy", "xyz")
@@ -416,14 +513,15 @@
 
 
 def rest_kernel(
-    tokens, x, ct, an, mn, wq, wd, wh, wo, norms, unit_bias, out_bias, tables,
-    outputs, input_grad, hidden_out, output_out, qkv_out, dense_out, small_out,
-    x_v, ct_v, an_v, mn_v, branches, weighted, sums, small, sm_a, sm_b, pair_send, pair_recv,
+    tokens, x, ct, an, mn, wq, wd, wh, wo, vec, cosine, sine,
+    outputs, input_grad, gathered0, gathered1, gathered2, small_out,
+    tables, norms, unit_bias, x_v, ct_v, an_v, mn_v, branches, weighted, sums, small, sm_a, sm_b, pair_send, pair_recv,
     g0, g1, g2, *rest,
 ):
     grads = (g0, g1, g2)
-    bufs = [rest[7 * n : 7 * n + 7] for n in range(3)]
-    send, recv, local_sem, sm_send, sm_recv = rest[21:]
+    gathered = (gathered0, gathered1, gathered2)
+    bufs = [(*rest[6 * n : 6 * n + 6], gathered[n]) for n in range(3)]
+    send, recv, local_sem, sm_send, sm_recv = rest[18:]
     f, s, (y, zl, px, zh, core) = place()
     z = zh * 2 + zl
     coordinate = {"y": y, "z": z, "x": px}
@@ -519,6 +617,16 @@
     keeps = [load(a, b, k) for k, (a, b) in enumerate([(x, x_v), (ct, ct_v), (an, an_v), (mn, mn_v)])]
     barrier(same_seq + same_fsdp + [zother])
     small[...] = jnp.zeros_like(small)
+    here = pl.ds(pl.multiple_of((px * 2 + zh) * T, T), T)
+    keeps += [load(cosine.at[here], tables.at[0], 12), load(sine.at[here], tables.at[1], 13)]
+    for r in range(8):
+        at = slice(r * 128, r * 128 + 128)
+        norms[0:4, at] = vec[r, 0:4, :]
+        norms[4:5, at] = vec[r, 7:8, :] + vec[r, 12:13, :]
+        for j in range(2):
+            unit_bias[0:1, r * 256 + j * 128 : r * 256 + j * 128 + 128] = vec[
+                r, pl.ds(8 + 2 * core + j, 1), :
+            ]
 
     def attention_part(wq_v, wd_v, tk_v, pg_v, at_v, turned_v):
         loads = [load(a, b, 4 + k) for k, (a, b) in enumerate([(tokens, tk_v), (wq, wq_v), (wd, wd_v)])]
@@ -527,7 +635,7 @@
         loads[0].wait()
         low = lax.broadcasted_iota(jnp.int32, (T, 128), 1) < HEAD
         first = lax.broadcasted_iota(jnp.int32, (1, 128), 1) < HEAD
-        rotary = (tables[0], tables[1], tables[2])
+        rotary = (tables[0], tables[1])
         for pair in range(4):
             for j in range(2):
                 r = 2 * pair + j
@@ -657,7 +765,7 @@
     relay(0, 0)
     arrived(pair_recv, 78)
     normed, scale = normalised(x_v[mine, :])
-    total = x_v[mine, :].astype(F32) + branches[mine, :] + pair_recv[0].astype(F32) + out_bias[...]
+    total = x_v[mine, :].astype(F32) + branches[mine, :] + pair_recv[0].astype(F32) + norms[4:5, :]
     outputs[...] = total.astype(BF16)
     w = weighted[mine, :] + pair_recv[1].astype(F32)
     input_grad[...] = ct_v[mine, :].astype(F32) + scale * (
@@ -742,51 +850,8 @@
         total = total + sm_b[k]
     small_out[...] = total
 
-    def finals(hidden_v, output_v, qkv_v, dense_v):
-        ends = []
-        a = bufs[2][6]
-        arrived(a.at[1 - core], 26 * 2 + 25)
-        low = lax.broadcasted_iota(jnp.int32, (128, 128), 1) < HEAD
-        for pair in range(4):
-            v0 = a[0, :, :, 1024 + pair * 128 : 1152 + pair * 128].reshape(128, 128).astype(F32)
-            v1 = a[1, :, :, 1024 + pair * 128 : 1152 + pair * 128].reshape(128, 128).astype(F32)
-            for j in range(2):
-                r = 2 * pair + j
-                q0 = a[0, :, :, r * 128 : r * 128 + 128].reshape(128, 128).astype(F32)
-                q1 = a[1, :, :, r * 128 : r * 128 + 128].reshape(128, 128).astype(F32)
-                q1 = pltpu.roll(q1, 64, 1)
-                left = v0 if j == 0 else pltpu.roll(v0, 64, 1)
-                right = pltpu.roll(v1, 64, 1) if j == 0 else v1
-                qkv_v[:, r * 384 : r * 384 + 128] = q0
-                qkv_v[:, r * 384 + 128 : r * 384 + 256] = jnp.where(low, left, q1)
-                qkv_v[:, r * 384 + 256 : r * 384 + 384] = jnp.where(low, q1, right)
-        for c in range(2):
-            for k in range(2):
-                piece = a[c, k * 4 : k * 4 + 4, :, 1536:2048].reshape(64, 512)
-                dense_v[c * 64 : c * 64 + 64, k * 512 : k * 512 + 512] = piece.astype(F32)
-        ends.append(load(qkv_v, qkv_out, 12))
-        ends.append(load(dense_v, dense_out, 13))
-        a1 = bufs[1][6]
-        arrived(a1.at[1 - core], 26 + 25)
-        output_v[...] = a1[...].reshape(512, D).astype(F32)
-        ends.append(load(output_v, output_out, 14))
-        a0 = bufs[0][6]
-        arrived(a0.at[1 - core], 25)
-        for c in range(2):
-            for r in range(8):
-                piece = a0[c, :, :, r * 256 : r * 256 + 256].reshape(128, 256)
-                hidden_v[:, r * 512 + c * 256 : r * 512 + c * 256 + 256] = piece.astype(F32)
-        ends.append(load(hidden_v, hidden_out, 15))
-        for copy in ends:
-            copy.wait()
-
-    pl.run_scoped(
-        finals,
-        pltpu.VMEM((128, FF), F32),
-        pltpu.VMEM((512, D), F32),
-        pltpu.VMEM((128, 3 * D), F32),
-        pltpu.VMEM((128, D), F32),
-    )
+    for n in order:
+        arrived(gathered[n].at[1 - core], 26 * n + 25)
     for copy in sends:
         copy.wait_send()
     for n in range(3):
@@ -807,7 +872,6 @@
             (2, 2, 2, R, C),
             (2, R, C // 2),
             (2, 2, R, C // 2),
-            (2, 8, R, C),
         ):
             scratch.append(pltpu.VMEM(dims, BF16))
     T = CHIP_TOKENS
@@ -816,15 +880,15 @@
         out_shape=(
             jax.ShapeDtypeStruct((256, D), BF16),
             jax.ShapeDtypeStruct((256, D), F32),
-            jax.ShapeDtypeStruct((128, FF), F32),
-            jax.ShapeDtypeStruct((512, D), F32),
-            jax.ShapeDtypeStruct((128, 3 * D), F32),
-            jax.ShapeDtypeStruct((128, D), F32),
+            *[jax.ShapeDtypeStruct((2, 8, R, C), BF16) for R, C in zip(ROWS, COLUMNS)],
             jax.ShapeDtypeStruct((16, 128), F32),
         ),
-        in_specs=[HBM] * 9 + [VMEM] * 4,
-        out_specs=(VMEM, VMEM, HBM, HBM, HBM, HBM, VMEM),
+        in_specs=[HBM] * 9 + [VMEM, HBM, HBM],
+        out_specs=(VMEM, VMEM, HBM, HBM, HBM, VMEM),
         scratch_shapes=[
+            pltpu.VMEM((2, T, 128), F32),
+            pltpu.VMEM((8, D), F32),
+            pltpu.VMEM((8, 2048), F32),
             *[pltpu.VMEM((T, D), BF16)] * 4,
             *[pltpu.VMEM((T, D), F32)] * 2,
             pltpu.VMEM((8, D), F32),
@@ -846,67 +910,77 @@
     )(*args)
 
 
+def position_tables():
+    half = ROT // 2
+    frequency = np.power(10000.0, -2.0 * np.arange(half) / ROT).astype(np.float32)
+    angles = np.arange(CHIPS * CHIP_TOKENS, dtype=np.float32)[:, None] * frequency[None, :]
+    angles = angles.astype(np.float64)
+    cosine = np.ones((CHIPS * CHIP_TOKENS, 2 * HEAD), np.float32)
+    sine = np.zeros((CHIPS * CHIP_TOKENS, 2 * HEAD), np.float32)
+    for at in (0, HEAD):
+        cosine[:, at : at + half] = cosine[:, at + half : at + ROT] = np.cos(angles)
+        sine[:, at : at + half] = -np.sin(angles)
+        sine[:, at + half : at + ROT] = np.sin(angles)
+    return cosine, sine
+
+
 def turn(values, tables, sign):
-    cosine, ahead, behind = tables
-    moved = pltpu.roll(values, 120, 1) * ahead + pltpu.roll(values, 8, 1) * behind
-    return values * cosine + sign * moved
-
-
-def front_kernel(x, ct, wq, wd, vectors, bias, tables, packed, attn_out, mlp_out):
-    values = x[...].astype(F32)
-    centered = values - jnp.mean(values, axis=-1, keepdims=True)
-    variance = jnp.mean(centered * centered, axis=-1, keepdims=True)
-    normed = centered * lax.rsqrt(variance + epsilon)
-    attn_out[...] = (normed * vectors[0:1, :] + vectors[1:2, :]).astype(BF16)
-    mlp_out[...] = (normed * vectors[2:3, :] + vectors[3:4, :]).astype(BF16)
-    low = lax.broadcasted_iota(jnp.int32, (CHIP_TOKENS, 128), 1) < HEAD
-    rotary = (tables[0], tables[1], tables[2])
+    lane = lax.broadcasted_iota(jnp.int32, values.shape, 1) % HEAD
+    moved = jnp.where(lane < ROT // 2, pltpu.roll(values, 120, 1), pltpu.roll(values, 8, 1))
+    return values * tables[0] + sign * (moved * tables[1])
+
+
+def finals_kernel(a0, a1, a2, sums, hidden, output, qkv, dense, *vectors):
+    low = lax.broadcasted_iota(jnp.int32, (128, 128), 1) < HEAD
     for pair in range(4):
-        a = attn_out[...]
-        qk = slice(pair * 256, pair * 256 + 256)
-        vs = slice(1024 + pair * 128, 1024 + pair * 128 + 128)
-        projected = jnp.dot(a, wq[:, qk], preferred_element_type=F32) + bias[0:1, qk]
+        at = slice(1024 + pair * 128, 1152 + pair * 128)
+        v0 = a2[0, :, :, at].reshape(128, 128).astype(F32)
+        v1 = a2[1, :, :, at].reshape(128, 128).astype(F32)
         for j in range(2):
-            turned = turn(projected[:, j * 128 : j * 128 + 128], rotary, 1.0)
-            packed[2 * pair + j, :, 0:128] = turned.astype(BF16)
-        v = jnp.dot(a, wq[:, vs], preferred_element_type=F32) + bias[0:1, vs]
-        rows = slice(pair * 128, pair * 128 + 128)
-        d = lax.dot_general(ct[...], wd[rows, :], NT, preferred_element_type=F32)
-        packed[2 * pair, :, 128:256] = jnp.where(low, v, pltpu.roll(d, 64, 1)).astype(BF16)
-        packed[2 * pair + 1, :, 128:256] = jnp.where(low, pltpu.roll(v, 64, 1), d).astype(BF16)
-
-
-def front(x, ct, wq, wd, vectors, bias, tables):
-    T = CHIP_TOKENS
+            r = 2 * pair + j
+            q0 = a2[0, :, :, r * 128 : r * 128 + 128].reshape(128, 128).astype(F32)
+            q1 = a2[1, :, :, r * 128 : r * 128 + 128].reshape(128, 128).astype(F32)
+            q1 = pltpu.roll(q1, 64, 1)
+            left = v0 if j == 0 else pltpu.roll(v0, 64, 1)
+            right = pltpu.roll(v1, 64, 1) if j == 0 else v1
+            qkv[:, r * 384 : r * 384 + 128] = q0
+            qkv[:, r * 384 + 128 : r * 384 + 256] = jnp.where(low, left, q1)
+            qkv[:, r * 384 + 256 : r * 384 + 384] = jnp.where(low, q1, right)
+    for c in range(2):
+        for k in range(2):
+            piece = a2[c, k * 4 : k * 4 + 4, :, 1536:2048].reshape(64, 512)
+            dense[c * 64 : c * 64 + 64, k * 512 : k * 512 + 512] = piece.astype(F32)
+        for r in range(8):
+            piece = a0[c, :, :, r * 256 : r * 256 + 256].reshape(128, 256)
+            hidden[:, r * 512 + c * 256 : r * 512 + c * 256 + 256] = piece.astype(F32)
+    output[...] = a1[...].reshape(512, D).astype(F32)
+    for k in range(4):
+        vectors[k][...] = sums[k : k + 1, :]
+    first = lax.broadcasted_iota(jnp.int32, (1, 128), 1) < HEAD
+    q1 = pltpu.roll(sums[5:6, :], 64, 1)
+    vectors[4][:, 0:128] = sums[4:5, :]
+    vectors[4][:, 128:256] = jnp.where(first, sums[6:7, :], q1)
+    vectors[4][:, 256:384] = jnp.where(first, q1, sums[6:7, :])
+    vectors[5][...] = sums[7:8, :]
+    for k in range(4):
+        vectors[6][:, k * 128 : k * 128 + 128] = sums[8 + k : 9 + k, :]
+
+
+def finals(a0, a1, a2, sums):
+    widths = (128, 128, 128, 128, 384, 128, 512)
     return pl.pallas_call(
-        front_kernel,
+        finals_kernel,
         out_shape=(
-            jax.ShapeDtypeStruct((8, T, 256), BF16),
-            jax.ShapeDtypeStruct((T, D), BF16),
-            jax.ShapeDtypeStruct((T, D), BF16),
+            jax.ShapeDtypeStruct((128, FF), F32),
+            jax.ShapeDtypeStruct((512, D), F32),
+            jax.ShapeDtypeStruct((128, 3 * D), F32),
+            jax.ShapeDtypeStruct((128, D), F32),
+            *[jax.ShapeDtypeStruct((1, w), F32) for w in widths],
         ),
-        in_specs=[VMEM] * 7,
-        out_specs=(VMEM,) * 3,
+        in_specs=[VMEM] * 4,
+        out_specs=(VMEM,) * 11,
         compiler_params=pltpu.CompilerParams(vmem_limit_bytes=48 * MIB),
-    )(x, ct, wq, wd, vectors, bias, tables)
-
-
-def rotary_tables(first_position):
-    half = ROT // 2
-    frequency = 10000.0 ** (-2.0 * jnp.arange(half, dtype=F32) / ROT)
-    positions = first_position + jnp.arange(CHIP_TOKENS, dtype=jnp.int32)
-    angles = positions.astype(F32)[:, None] * frequency[None, :]
-    cosine, sine = jnp.cos(angles), jnp.sin(angles)
-    rest = HEAD - ROT
-    one = jnp.ones((CHIP_TOKENS, rest), F32)
-    zero = jnp.zeros((CHIP_TOKENS, rest), F32)
-    none = jnp.zeros((CHIP_TOKENS, half), F32)
-    rows = [
-        jnp.concatenate([cosine, cosine, one] * 2, axis=1),
-        jnp.concatenate([-sine, none, zero] * 2, axis=1),
-        jnp.concatenate([none, sine, zero] * 2, axis=1),
-    ]
-    return jnp.stack(rows)
+    )(a0, a1, a2, sums)
 
 
 def local(
@@ -925,73 +999,50 @@
     output_weight,
     output_bias,
 ):
-    seq = lax.axis_index("seq")
-    core = seq % 2
+    bias = qkv_bias.reshape(2, 192)
     small = jnp.concatenate(
         [
-            ln_attn_gain.reshape(1, 128),
-            ln_attn_bias.reshape(1, 128),
-            ln_mlp_gain.reshape(1, 128),
-            ln_mlp_bias.reshape(1, 128),
-            qkv_bias.reshape(3, 128),
-            dense_bias.reshape(1, 128),
-            hidden_bias.reshape(4, 128),
-            output_bias.reshape(1, 128),
-            jnp.zeros((3, 128), BF16),
+            ln_attn_gain,
+            ln_attn_bias,
+            ln_mlp_gain,
+            ln_mlp_bias,
+            bias[:, :128].reshape(256),
+            bias[:, 128:].reshape(128),
+            dense_bias,
+            hidden_bias,
+            output_bias,
+            jnp.zeros((3 * 128,), BF16),
         ]
+    ).reshape(16, 128)
+    cosine, sine = (jnp.asarray(t) for t in position_tables())
+    tokens, wh, wo, wq, wd, x, ct, attn_normed, mlp_normed, vectors = attention(
+        qkv_weight,
+        dense_weight,
+        hidden_weight,
+        output_weight,
+        small.astype(F32),
+        inputs,
+        cotangent,
+        cosine,
+        sine,
     )
-    own_qkv = lax.dynamic_index_in_dim(
-        qkv_weight.reshape(128, 8, 2, 192), core, axis=2, keepdims=False
+    outputs, input_grad, *gathered, sums = rest_of_block(
+        tokens,
+        x.reshape(CHIP_TOKENS, D),
+        ct.reshape(CHIP_TOKENS, D),
+        attn_normed,
+        mlp_normed,
+        wq.reshape(D, 1536),
+        wd.reshape(512, D),
+        wh.reshape(D, 2048),
+        wo.reshape(2048, D),
+        vectors,
+        cosine,
+        sine,
     )
-    own_qkv = jnp.concatenate(
-        [own_qkv[:, :, :128].reshape(128, 1024), own_qkv[:, :, 128:].reshape(128, 512)], axis=1
-    )
-    own_hidden = lax.dynamic_index_in_dim(
-        hidden_weight.reshape(128, 8, 2, 256), core, axis=2, keepdims=False
-    ).reshape(128, 2048)
-    wq, wd, vectors, x, ct = gather(own_qkv, dense_weight, small, inputs, cotangent)
-    wq = wq.reshape(D, 1536)
-    wd = wd.reshape(512, D)
-    x = x.reshape(CHIP_TOKENS, D)
-    ct = ct.reshape(CHIP_TOKENS, D)
-    vectors = vectors.astype(F32)
-    norms = vectors[:, 0:4].transpose(1, 0, 2).reshape(4, D)
-    head_bias = lax.dynamic_index_in_dim(
-        vectors[:, 4:7].reshape(8, 2, 192), core, axis=1, keepdims=False
-    )
-    head_bias = jnp.concatenate(
-        [head_bias[:, :128].reshape(1, 1024), head_bias[:, 128:].reshape(1, 512)], axis=1
-    )
-    out_bias = (vectors[:, 7] + vectors[:, 12]).reshape(1, D)
-    unit_bias = lax.dynamic_index_in_dim(
-        vectors[:, 8:12].reshape(8, 2, 256), core, axis=1, keepdims=False
-    ).reshape(1, 2048)
-
-    tables = rotary_tables((seq // 2) * CHIP_TOKENS)
-    packed, attn_normed, mlp_normed = front(x, ct, wq, wd, norms, head_bias, tables)
-    tokens, wh, wo = attention(packed, own_hidden, output_weight)
-    wh = wh.reshape(D, 2048)
-    wo = wo.reshape(2048, D)
-    outputs, input_grad, hidden_total, output_total, qkv_total, dense_total, sums = rest_of_block(
-        tokens, x, ct, attn_normed, mlp_normed, wq, wd, wh, wo, norms, unit_bias, out_bias, tables
-    )
-    head_bias_total = jnp.concatenate([sums[4], sums[6, :64], sums[5], sums[6, 64:]])
-    return (
-        outputs,
-        input_grad,
-        sums[0],
-        sums[1],
-        sums[2],
-        sums[3],
-        qkv_total,
-        head_bias_total,
-        dense_total,
-        sums[7],
-        hidden_total,
-        sums[8:12].reshape(512),
-        output_total,
-        sums[7],
-    )
+    hidden, output, qkv, dense, *vectors = finals(*gathered, sums)
+    ag, ab, mg, mb, qb, db, hb = (v.reshape(v.shape[1]) for v in vectors)
+    return (outputs, input_grad, ag, ab, mg, mb, qkv, qb, dense, db, hidden, hb, output, db)
 
 
 def solution(mesh):

time: 323 us -> 277 us (0.86)
  Pallas kernels: 285 us -> 260 us
  local copies, waits for them, and re-layouts: 32.2 us -> 14.6 us
    pallas_call x3 -> x2, Pallas kernels: 173 us -> 147 us  [the longest x1 144 us: attention(): pl.pallas_call(attention_kernel, out_shape=(shape(CHIPS, B, 4 * HEAD), sh...]
    unnamed x38 -> x24, local copies, waits for them, and re-layouts: 18.2 us -> 13.6 us
    concatenate x4 -> x1, local copies, waits for them, and re-layouts: 3.91 us -> 0.21 us  [local(): jnp.concatenate([ln_attn_gain, ln_attn_bias, ln_mlp_gain, ln_mlp_bias, bi...]
    dynamic_slice x3 -> x0, local copies, waits for them, and re-layouts: 3.69 us -> none  [the longest x1 3.07 us: local(): lax.dynamic_index_in_dim(hidden_weight.reshape(128, 8, 2, 256), core, axi...]
where the time goes in v2:
time: 277 us; the launch traced here: 276 us
  Pallas kernels  260 us (94%)
  local copies, waits for them, and re-layouts  14.6 us (5%)
    pallas_call x1, Pallas kernels, attention(): pl.pallas_call(attention_kernel, out_shape=(shape(CHIPS, B, 4 * HEAD), sh...  144 us
    pallas_call x1, Pallas kernels, rest_of_block(): pl.pallas_call(rest_kernel, out_shape=(jax.ShapeDtypeStruct((256, D), BF1...  113 us
    unnamed x24, local copies, waits for them, and re-layouts  13.6 us

profile of v2, /device:TPU:1, one launch (start us, length us, event | category | flops | bytes accessed | tf_op | source)
XLA Modules:
  0.0 276.5 jit_solution(377663859611241284)
XLA Ops:
  0.6 0.8 reshape.79
  1.4 0.1 reshape.81
  1.5 0.8 dynamic-update-slice
  2.3 0.8 dynamic-update-slice.1
  3.2 0.8 dynamic-update-slice.2
  4.0 0.8 dynamic-update-slice.3
  4.8 0.2 dynamic-update-slice.4
  5.0 0.2 dynamic-update-slice.5
  5.2 0.8 dynamic-update-slice.6
  6.1 0.9 dynamic-update-slice.7
  6.9 0.8 dynamic-update-slice.8
  7.8 0.2 dynamic-update-slice.9
  8.0 0.6 bitcast_convert_fusion.small
  8.6 144.2 %shard_map.263 = (bf16[8,512,256]{2,1,0:T(8,128)(2,1)}, bf16[8,128,2048]{2,1,0:T(8,128)(2,1)}, bf16[8,256,1024]{2,1,0:T(8,128)(2,1)}, bf16[8,128,1536]{2,1,0:T(8...) custom-call(bf16[128,3072]{1,0:T(8,128)(2,1)} %qkv_w.1, ...), custom_call_target="tpu_custom_call" | custom-call | tf_op jit(solution)/shard_map/pallas_call | solution.py:413
  152.8 112.7 %shard_map.264 = (bf16[256,1024]{1,0:T(8,128)(2,1)}, f32[256,1024]{1,0:T(8,128)}, bf16[2,8,16,2048]{3,2,1,0:T(8,128)(2,1)}, bf16[2,8,32,1024]{3,2,1,0:T(8,128)(2...) custom-call(bf16[8,512,256]{2,1,0:T(8,128)(2,1)} %get-tuple-element.41.tokens, bf16[512,1024]{1,0:T(8,128)(2,1)} %bitcast.21, ...), custom_call_target="tpu_custom_call" | custom-call | tf_op jit(solution)/shard_map/pallas_call | solution.py:878
  265.5 0.0 copy-start
  265.5 1.2 copy-done
  266.7 0.0 copy-start.1
  266.7 1.2 copy-done.1
  267.9 0.0 copy-start.2
  267.9 1.2 copy-done.2
  269.2 0.0 copy-start.3
  269.2 0.7 copy-done.3
  269.9 0.0 copy-start.5
  269.9 0.0 copy-start.4
  269.9 3.1 %shard_map.265 = (f32[128,4096]{1,0:T(8,128)}, f32[512,1024]{1,0:T(8,128)}, f32[128,3072]{1,0:T(8,128)}, f32[128,1024]{1,0:T(8,128)}, f32[1,128]{1,0:T(1,128)}, ...) custom-call(bf16[2,8,16,2048]{3,2,1,0:T(8,128)(2,1)S(1)} %copy-done,, ...), custom_call_target="tpu_custom_call" | custom-call | tf_op jit(solution)/shard_map/pallas_call | solution.py:971
  272.9 0.6 reduce
  273.5 1.2 copy.43
  274.7 0.0 copy-done.5
  274.7 0.8 copy.44
  275.5 0.0 copy-done.4
  275.5 1.0 copy.45
  (4 shorter events, 0.0 us)
Async XLA Ops:
  265.5 1.2 copy-start
  266.7 1.2 copy-start.1
  267.9 1.2 copy-start.2
  269.2 0.7 copy-start.3
  269.9 4.8 %copy-start.5 = (bf16[256,1024]{1,0:T(8,128)(2,1)S(1)}, bf16[256,1024]{1,0:T(8,128)(2,1)}, u32[]{:S(2)}) copy-start(bf16[256,1024]{1,0:T(8,128)(2,1)} %get-tuple-element.110) | copy-start | bytes 1572868
  269.9 5.6 %copy-start.4 = (f32[256,1024]{1,0:T(8,128)S(1)}, f32[256,1024]{1,0:T(8,128)}, u32[]{:S(2)}) copy-start(f32[256,1024]{1,0:T(8,128)} %get-tuple-element.111) | copy-start | bytes 3145732

commit v3 on v2

--- a/solution.py
+++ b/solution.py
@@ -116,6 +116,42 @@
             self.pass_on(n, 2, self.slots[2], 0, [(8, self.zp)])
             self.pass_on(n, 1, self.slots[1], 1, [(11, self.zm)])
 
+    def opposite_y(self):
+        for n, g in enumerate(self.full):
+            self.arrived(self.part(g.at[self.slots[3]], 0), 14 * n + 4)
+            self.arrived(self.part(g.at[self.slots[3]], 1), 14 * n + 5)
+
+    def ends_z(self):
+        for k, slot in ((0, self.f), (3, self.slots[3])):
+            for n, g in enumerate(self.full):
+                a, b = self.part(g.at[slot], 0), self.part(g.at[slot], 1)
+                if k == 0:
+                    a, b = self.part(self.own[n], 0), self.part(self.own[n], 1)
+                at = g.at[slot]
+                self.started(a, self.part(at, 0), 14 * n + 6 + k, self.zp)
+                self.started(b, self.part(at, 1), 14 * n + 10 + k, self.zm)
+
+    def sides_y(self):
+        for n in range(len(self.full)):
+            self.pass_on(n, 6, self.far[0], 0, [(7, self.yp), (8, self.ym)])
+            self.pass_on(n, 10, self.far[0], 1, [(11, self.yp), (12, self.ym)])
+
+    def finish_mixed(self):
+        for n, g in enumerate(self.full):
+            for k, slot, h in (
+                (1, self.slots[1], 1),
+                (2, self.slots[2], 0),
+                (7, self.far[1], 0),
+                (8, self.far[2], 0),
+                (11, self.far[1], 1),
+                (12, self.far[2], 1),
+                (9, self.far[3], 0),
+                (13, self.far[3], 1),
+            ):
+                self.arrived(self.part(g.at[slot], h), 14 * n + k)
+        for copy in self.sends:
+            copy.wait_send()
+
     def opposite(self):
         for n in range(len(self.full)):
             self.pass_on(n, 4, self.slots[3], 0, [(9, self.zp)])
@@ -139,9 +175,9 @@
 
 def attention_kernel(
     qkv_w, dense_w, hidden_w, output_w, small, x, ct, cosine, sine,
-    result, gh, go, wq_out, wd_out, x_out, ct_out, an_out, mn_out, vectors,
+    result_q, result_k, gh, go, wq_out, wd_out, x_out, ct_out, an_out, mn_out, vectors,
     raw_q, own_q, own_h, own_o, wq, wd, x_v, ct_v, an, mn, vec, norms, bias, tables, packed,
-    hd, out, q_s, k_s, v_s, d_s, s_s, p_s, dk_s, dv_s, mx_s, l_s, o_s, dq_s,
+    hd, out_q, out_k, q_s, k_s, v_s, d_s, s_s, p_s, dk_s, dv_s, mx_s, l_s, o_s, dq_s,
     in_send, in_recv, out_send, out_recv, a_send, a_recv, g_send, g_recv, local_sem,
 ):
     f, s, (y, zl, px, zh, core) = place()
@@ -251,10 +287,12 @@
     wide = lax.broadcasted_iota(jnp.int32, (B, 128), 1) < HEAD
     rotary = (tables[0], tables[1])
     tokens = ct_v[...].reshape(B, D)
-    for pair in range(4):
+
+    def project(t, _):
+        pair = (px + 1 + t) % 4
         a = an[...]
-        qk = slice(pair * 256, pair * 256 + 256)
-        vs = slice(1024 + pair * 128, 1024 + pair * 128 + 128)
+        qk = pl.ds(pl.multiple_of(pair * 256, 256), 256)
+        vs = pl.ds(pl.multiple_of(1024 + pair * 128, 128), 128)
         weight = wq[:, :, qk].reshape(D, 256)
         projected = jnp.dot(a, weight, preferred_element_type=F32) + bias[0:1, qk]
         for j in range(2):
@@ -262,16 +300,19 @@
             packed[2 * pair + j, :, 0:128] = turned.astype(BF16)
         weight = wq[:, :, vs].reshape(D, 128)
         v = jnp.dot(a, weight, preferred_element_type=F32) + bias[0:1, vs]
-        weight = wd[2 * pair : 2 * pair + 2].reshape(128, D)
+        weight = wd[pl.ds(2 * pair, 2)].reshape(128, D)
         d = lax.dot_general(tokens, weight, NT, preferred_element_type=F32)
         packed[2 * pair, :, 128:256] = jnp.where(wide, v, pltpu.roll(d, 64, 1)).astype(BF16)
         packed[2 * pair + 1, :, 128:256] = jnp.where(wide, pltpu.roll(v, 64, 1), d).astype(BF16)
-        for j in (2 * pair, 2 * pair + 1):
-
-            @pl.when(me != j)
+        for j in range(2):
+
+            @pl.when(2 * pair + j != me)
             def _():
-                given(j).start()
-
+                given(2 * pair + j).start()
+
+        return 0
+
+    lax.fori_loop(0, 4, project, 0)
     hd[me] = packed[me]
     units.near_y()
     saves = [
@@ -293,8 +334,8 @@
     for k in range(1, n):
         j = (me + n - k) % n
         remote(hd.at[j], hd.at[j], in_send.at[j], in_recv.at[j], chip(j)).wait_recv()
-    units.own_z()
-    units.near_z()
+    units.opposite_y()
+    units.ends_z()
 
     def block(i):
         return pl.ds(pl.multiple_of(i * B, B), B)
@@ -315,11 +356,31 @@
         jnp.int32, (B, B), 0
     )
 
-    def back_to(i):
-        return remote(out.at[i], result.at[me], out_send.at[i], out_recv.at[me], chip(i))
+    def back_to(i, h):
+        src, dst = (out_q, result_q) if h == 0 else (out_k, result_k)
+        return remote(
+            src.at[i], dst.at[me], out_send.at[8 * h + i], out_recv.at[8 * h + me], chip(i)
+        )
+
+    def keep_own(h):
+        src, dst = (out_q, result_q) if h == 0 else (out_k, result_k)
+        return pltpu.make_async_copy(src.at[me], dst.at[me], local_sem.at[25 + h])
+
+    def in_pairs(count, body):
+        def pair(k, _):
+            body(2 * k)
+            body(2 * k + 1)
+            return 0
+
+        def single(k, _):
+            body(k)
+            return 0
+
+        lax.fori_loop(0, count // 2, pair, 0)
+        lax.fori_loop(count // 2 * 2, count, single, 0)
 
     def query_block(t, _):
-        i = n - 1 - t
+        i = (me + 1 + t) % n
         rows = block(i)
         qi = q_s[rows, :]
         mx_s[...] = jnp.full(mx_s.shape, -1e30, F32)
@@ -327,13 +388,12 @@
         def score(kb):
             return lax.dot_general(qi, k_s[block(kb), :], NT, preferred_element_type=F32)
 
-        def first(kb, _):
+        def first(kb):
             scores = score(kb)
             s_s[kb] = scores
             mx_s[...] = jnp.maximum(mx_s[...], fold(jnp.maximum, scores))
-            return 0
-
-        lax.fori_loop(0, i, first, 0)
+
+        in_pairs(i, first)
         scores = jnp.where(keep, score(i), -1e30)
         s_s[i] = scores
         row_max = jnp.max(
@@ -343,15 +403,14 @@
         o_s[...] = jnp.zeros_like(o_s)
         dq_s[...] = jnp.zeros_like(dq_s)
 
-        def second(kb, _):
+        def second(kb):
             p = jnp.exp(s_s[kb] - row_max)
             l_s[...] += fold(jnp.add, p)
             pb = p.astype(BF16)
             p_s[kb] = pb
             o_s[...] += jnp.dot(pb, v_s[block(kb), :], preferred_element_type=F32)
-            return 0
-
-        lax.fori_loop(0, i + 1, second, 0)
+
+        in_pairs(i + 1, second)
         inverse = 1.0 / jnp.sum(l_s[...], axis=1, keepdims=True)
         o = o_s[...] * inverse
         d = (d_s[rows, :].astype(F32) * inverse).astype(BF16)
@@ -359,7 +418,7 @@
         q_t = qi.T
         d_t = d.T
 
-        def third(kb, _):
+        def third(kb):
             cols = block(kb)
             pb = p_s[kb]
             dp = lax.dot_general(d, v_s[cols, :], NT, preferred_element_type=F32)
@@ -367,40 +426,50 @@
             dq_s[...] += jnp.dot(ds, k_s[cols, :], preferred_element_type=F32)
             dk_s[:, cols] += jnp.dot(q_t, ds, preferred_element_type=F32)
             dv_s[:, cols] += jnp.dot(d_t, pb, preferred_element_type=F32)
-            return 0
-
-        lax.fori_loop(0, i + 1, third, 0)
-        out[i, :, 0:64] = (dq_s[...] * scale).astype(BF16)
-        out[i, :, 64:128] = dk_s[:, rows].T.astype(BF16)
-        out[i, :, 128:192] = dv_s[:, rows].T.astype(BF16)
-        out[i, :, 192:256] = o.astype(BF16)
+
+        in_pairs(i + 1, third)
+        out_q[i, :, 0:64] = (dq_s[...] * scale).astype(BF16)
+        out_q[i, :, 64:128] = o.astype(BF16)
 
         @pl.when(i != me)
         def _():
-            back_to(i).start()
-
-        @pl.when(i == me)
+            back_to(i, 0).start()
+
+        return 0
+
+    def key_block(t, _):
+        i = (me + 1 + t) % n
+        rows = block(i)
+        out_k[i, :, 0:64] = dv_s[:, rows].T.astype(BF16)
+        out_k[i, :, 64:128] = dk_s[:, rows].T.astype(BF16)
+
+        @pl.when(i != me)
         def _():
-            pltpu.make_async_copy(out.at[i], result.at[i], local_sem.at[25]).start()
+            back_to(i, 1).start()
 
         return 0
 
     lax.fori_loop(0, 1, query_block, 0)
-    units.opposite()
+    units.sides_y()
     lax.fori_loop(1, n, query_block, 0)
+
+    lax.fori_loop(0, n, key_block, 0)
+    keep_own(0).start()
+    keep_own(1).start()
 
     for k in range(1, n):
         given((me + k) % n).wait_send()
     for copy in saves:
         copy.wait()
-    units.finish()
-    for k in range(1, n):
-        back_to((me + k) % n).wait_send()
-    pltpu.make_async_copy(out.at[me], result.at[me], local_sem.at[25]).wait()
-    for k in range(1, n):
-        j = (me + k) % n
-        ref = result.at[j]
-        remote(ref, ref, out_send.at[j], out_recv.at[j], chip(me)).wait_recv()
+    units.finish_mixed()
+    for h, result in enumerate((result_q, result_k)):
+        for k in range(1, n):
+            back_to((me + k) % n, h).wait_send()
+        keep_own(h).wait()
+        for k in range(1, n):
+            j = (me + k) % n
+            ref = result.at[j]
+            remote(ref, ref, out_send.at[8 * h + j], out_recv.at[8 * h + j], chip(me)).wait_recv()
 
 
 def attention(*args):
@@ -413,7 +482,8 @@
     return pl.pallas_call(
         attention_kernel,
         out_shape=(
-            shape(CHIPS, B, 4 * HEAD),
+            shape(CHIPS, B, 2 * HEAD),
+            shape(CHIPS, B, 2 * HEAD),
             shape(8, 128, 2048),
             shape(8, 256, 1024),
             shape(8, 128, 1536),
@@ -425,7 +495,7 @@
             jax.ShapeDtypeStruct((8, 16, 128), F32),
         ),
         in_specs=[HBM] * 9,
-        out_specs=(HBM,) * 10,
+        out_specs=(HBM,) * 11,
         scratch_shapes=[
             pltpu.VMEM((128, 3072), BF16),
             pltpu.VMEM((128, 1536), BF16),
@@ -439,17 +509,19 @@
             pltpu.VMEM((8, D), F32),
             pltpu.VMEM((8, 1536), F32),
             pltpu.VMEM((2, B, 128), F32),
-            *[pltpu.VMEM((CHIPS, B, 4 * HEAD), BF16)] * 3,
+            *[pltpu.VMEM((CHIPS, B, 4 * HEAD), BF16)] * 2,
+            *[pltpu.VMEM((CHIPS, B, 2 * HEAD), BF16)] * 2,
             *[pltpu.VMEM((L, HEAD), BF16)] * 4,
             pltpu.VMEM((L // B, B, B), F32),
             pltpu.VMEM((L // B, B, B), BF16),
             *[pltpu.VMEM((HEAD, L), F32)] * 2,
             *[pltpu.VMEM((B, 128), F32)] * 2,
             *[pltpu.VMEM((B, HEAD), F32)] * 2,
-            *[pltpu.SemaphoreType.DMA((CHIPS,))] * 4,
+            *[pltpu.SemaphoreType.DMA((CHIPS,))] * 2,
+            *[pltpu.SemaphoreType.DMA((2 * CHIPS,))] * 2,
             *[pltpu.SemaphoreType.DMA((37,))] * 2,
             *[pltpu.SemaphoreType.DMA((28,))] * 2,
-            pltpu.SemaphoreType.DMA((26,)),
+            pltpu.SemaphoreType.DMA((27,)),
         ],
         compiler_params=pltpu.CompilerParams(
             collective_id=1, has_side_effects=True, vmem_limit_bytes=60 * MIB
@@ -513,7 +585,7 @@
 
 
 def rest_kernel(
-    tokens, x, ct, an, mn, wq, wd, wh, wo, vec, cosine, sine,
+    tokens_q, tokens_k, x, ct, an, mn, wq, wd, wh, wo, vec, cosine, sine,
     outputs, input_grad, gathered0, gathered1, gathered2, small_out,
     tables, norms, unit_bias, x_v, ct_v, an_v, mn_v, branches, weighted, sums, small, sm_a, sm_b, pair_send, pair_recv,
     g0, g1, g2, *rest,
@@ -628,11 +700,13 @@
                 r, pl.ds(8 + 2 * core + j, 1), :
             ]
 
-    def attention_part(wq_v, wd_v, tk_v, pg_v, at_v, turned_v):
-        loads = [load(a, b, 4 + k) for k, (a, b) in enumerate([(tokens, tk_v), (wq, wq_v), (wd, wd_v)])]
+    def attention_part(wq_v, wd_v, tq_v, tk_v, pg_v, at_v, turned_v):
+        loads = [load(a, b, 4 + k) for k, (a, b) in enumerate([(tokens_q, tq_v), (wq, wq_v), (wd, wd_v)])]
+        load_k = load(tokens_k, tk_v, 14)
         for copy in keeps:
             copy.wait()
         loads[0].wait()
+        load_k.wait()
         low = lax.broadcasted_iota(jnp.int32, (T, 128), 1) < HEAD
         first = lax.broadcasted_iota(jnp.int32, (1, 128), 1) < HEAD
         rotary = (tables[0], tables[1])
@@ -640,15 +714,18 @@
             for j in range(2):
                 r = 2 * pair + j
                 at = slice(r * 128, r * 128 + 128)
-                turned = turn(tk_v[r, :, 0:128].astype(F32), rotary, -1.0).astype(BF16)
+                qk = jnp.where(low, tq_v[r].astype(F32), tk_v[r].astype(F32))
+                turned = turn(qk, rotary, -1.0).astype(BF16)
                 pg_v[:, at] = turned
                 small[r, pl.ds(4 + core, 1), :] = jnp.sum(turned.astype(F32), axis=0, keepdims=True)
-            a = tk_v[2 * pair, :, 128:256].astype(F32)
-            b = tk_v[2 * pair + 1, :, 128:256].astype(F32)
+            a, b = [
+                jnp.where(low, tk_v[r].astype(F32), tq_v[r].astype(F32))
+                for r in (2 * pair, 2 * pair + 1)
+            ]
             v = jnp.where(low, a, pltpu.roll(b, 64, 1))
             pg_v[:, 1024 + pair * 128 : 1152 + pair * 128] = v.astype(BF16)
             total = jnp.sum(v, axis=0, keepdims=True)
-            moved = jnp.sum(jnp.where(low, pltpu.roll(v, 64, 1), pltpu.roll(v, 64, 1)), axis=0, keepdims=True)
+            moved = jnp.sum(pltpu.roll(v, 64, 1), axis=0, keepdims=True)
             zero = jnp.zeros_like(total)
             at_low = (jnp.where(first, total, zero), jnp.where(first, moved, zero))
             at_high = (jnp.where(first, zero, moved), jnp.where(first, zero, total))
@@ -686,7 +763,8 @@
         attention_part,
         pltpu.VMEM((D, 1536), BF16),
         pltpu.VMEM((512, D), BF16),
-        pltpu.VMEM((8, T, 256), BF16),
+        pltpu.VMEM((8, T, 128), BF16),
+        pltpu.VMEM((8, T, 128), BF16),
         pltpu.VMEM((T, 1536), BF16),
         pltpu.VMEM((T, 512), BF16),
         pltpu.VMEM((D, T), BF16),
@@ -883,7 +961,7 @@
             *[jax.ShapeDtypeStruct((2, 8, R, C), BF16) for R, C in zip(ROWS, COLUMNS)],
             jax.ShapeDtypeStruct((16, 128), F32),
         ),
-        in_specs=[HBM] * 9 + [VMEM, HBM, HBM],
+        in_specs=[HBM] * 10 + [VMEM, HBM, HBM],
         out_specs=(VMEM, VMEM, HBM, HBM, HBM, VMEM),
         scratch_shapes=[
             pltpu.VMEM((2, T, 128), F32),
@@ -930,7 +1008,19 @@
     return values * tables[0] + sign * (moved * tables[1])
 
 
-def finals_kernel(a0, a1, a2, sums, hidden, output, qkv, dense, *vectors):
+def finals_kernel(
+    h0, h1, h2, out_in, grad_in, sums, hidden, output, qkv, dense, out_ref, grad_ref, *rest
+):
+    vectors, (a0, a1, a2, sem) = rest[:7], rest[7:]
+    loads = [
+        pltpu.make_async_copy(a, b, sem.at[k])
+        for k, (a, b) in enumerate(
+            [(h2, a2), (h0, a0), (h1, a1), (out_in, out_ref), (grad_in, grad_ref)]
+        )
+    ]
+    for copy in loads:
+        copy.start()
+    loads[0].wait()
     low = lax.broadcasted_iota(jnp.int32, (128, 128), 1) < HEAD
     for pair in range(4):
         at = slice(1024 + pair * 128, 1152 + pair * 128)
@@ -950,10 +1040,15 @@
         for k in range(2):
             piece = a2[c, k * 4 : k * 4 + 4, :, 1536:2048].reshape(64, 512)
             dense[c * 64 : c * 64 + 64, k * 512 : k * 512 + 512] = piece.astype(F32)
+    loads[1].wait()
+    for c in range(2):
         for r in range(8):
             piece = a0[c, :, :, r * 256 : r * 256 + 256].reshape(128, 256)
             hidden[:, r * 512 + c * 256 : r * 512 + c * 256 + 256] = piece.astype(F32)
+    loads[2].wait()
     output[...] = a1[...].reshape(512, D).astype(F32)
+    loads[3].wait()
+    loads[4].wait()
     for k in range(4):
         vectors[k][...] = sums[k : k + 1, :]
     first = lax.broadcasted_iota(jnp.int32, (1, 128), 1) < HEAD
@@ -966,7 +1061,7 @@
         vectors[6][:, k * 128 : k * 128 + 128] = sums[8 + k : 9 + k, :]
 
 
-def finals(a0, a1, a2, sums):
+def finals(a0, a1, a2, outputs, input_grad, sums):
     widths = (128, 128, 128, 128, 384, 128, 512)
     return pl.pallas_call(
         finals_kernel,
@@ -975,12 +1070,18 @@
             jax.ShapeDtypeStruct((512, D), F32),
             jax.ShapeDtypeStruct((128, 3 * D), F32),
             jax.ShapeDtypeStruct((128, D), F32),
+            jax.ShapeDtypeStruct((256, D), BF16),
+            jax.ShapeDtypeStruct((256, D), F32),
             *[jax.ShapeDtypeStruct((1, w), F32) for w in widths],
         ),
-        in_specs=[VMEM] * 4,
-        out_specs=(VMEM,) * 11,
-        compiler_params=pltpu.CompilerParams(vmem_limit_bytes=48 * MIB),
-    )(a0, a1, a2, sums)
+        in_specs=[HBM] * 5 + [VMEM],
+        out_specs=(VMEM,) * 13,
+        scratch_shapes=[
+            *[pltpu.VMEM((2, 8, R, C), BF16) for R, C in zip(ROWS, COLUMNS)],
+            pltpu.SemaphoreType.DMA((5,)),
+        ],
+        compiler_params=pltpu.CompilerParams(vmem_limit_bytes=60 * MIB),
+    )(a0, a1, a2, outputs, input_grad, sums)
 
 
 def local(
@@ -1000,34 +1101,35 @@
     output_bias,
 ):
     bias = qkv_bias.reshape(2, 192)
-    small = jnp.concatenate(
-        [
-            ln_attn_gain,
-            ln_attn_bias,
-            ln_mlp_gain,
-            ln_mlp_bias,
-            bias[:, :128].reshape(256),
-            bias[:, 128:].reshape(128),
-            dense_bias,
-            hidden_bias,
-            output_bias,
-            jnp.zeros((3 * 128,), BF16),
-        ]
-    ).reshape(16, 128)
+    small = jnp.zeros((16, 128), F32)
+    for k, rows in (
+        (0, ln_attn_gain),
+        (1, ln_attn_bias),
+        (2, ln_mlp_gain),
+        (3, ln_mlp_bias),
+        (4, bias[:, :128]),
+        (6, bias[:, 128:]),
+        (7, dense_bias),
+        (8, hidden_bias),
+        (12, output_bias),
+    ):
+        rows = rows.reshape(-1, 128).astype(F32)
+        small = small + jnp.pad(rows, ((k, 16 - k - rows.shape[0]), (0, 0)))
     cosine, sine = (jnp.asarray(t) for t in position_tables())
-    tokens, wh, wo, wq, wd, x, ct, attn_normed, mlp_normed, vectors = attention(
+    tokens_q, tokens_k, wh, wo, wq, wd, x, ct, attn_normed, mlp_normed, vectors = attention(
         qkv_weight,
         dense_weight,
         hidden_weight,
         output_weight,
-        small.astype(F32),
+        small,
         inputs,
         cotangent,
         cosine,
         sine,
     )
     outputs, input_grad, *gathered, sums = rest_of_block(
-        tokens,
+        tokens_q,
+        tokens_k,
         x.reshape(CHIP_TOKENS, D),
         ct.reshape(CHIP_TOKENS, D),
         attn_normed,
@@ -1040,7 +1142,9 @@
         cosine,
         sine,
     )
-    hidden, output, qkv, dense, *vectors = finals(*gathered, sums)
+    hidden, output, qkv, dense, outputs, input_grad, *vectors = finals(
+        *gathered, outputs, input_grad, sums
+    )
     ag, ab, mg, mb, qb, db, hb = (v.reshape(v.shape[1]) for v in vectors)
     return (outputs, input_grad, ag, ab, mg, mb, qkv, qb, dense, db, hidden, hb, output, db)
 

time: 277 us -> 262 us (0.946)
  local copies, waits for them, and re-layouts: 14.6 us -> 2.02 us
  Pallas kernels: 260 us -> 257 us
    unnamed x24 -> x1, local copies, waits for them, and re-layouts: 13.6 us -> 1.17 us
    pallas_call x1, Pallas kernels: 144 us -> 133 us  [attention(): pl.pallas_call(attention_kernel, out_shape=(shape(CHIPS, B, 2 * HEAD), sh...]
    pallas_call x1, Pallas kernels: 113 us -> 117 us  [rest_of_block(): pl.pallas_call(rest_kernel, out_shape=(jax.ShapeDtypeStruct((256, D), BF1...]
    pallas_call x1, Pallas kernels: 3.06 us -> 6.26 us  [finals(): pl.pallas_call(finals_kernel, out_shape=(jax.ShapeDtypeStruct((128, FF),...]
where the time goes in v3:
time: 262 us
  Pallas kernels  257 us (98%)
  other arithmetic  2.64 us (1%)
    pallas_call x1, Pallas kernels, attention(): pl.pallas_call(attention_kernel, out_shape=(shape(CHIPS, B, 2 * HEAD), sh...  133 us
    pallas_call x1, Pallas kernels, rest_of_block(): pl.pallas_call(rest_kernel, out_shape=(jax.ShapeDtypeStruct((256, D), BF1...  117 us
    pallas_call x1, Pallas kernels, finals(): pl.pallas_call(finals_kernel, out_shape=(jax.ShapeDtypeStruct((128, FF),...  6.26 us

profile of v3, /device:TPU:1, one launch (start us, length us, event | category | flops | bytes accessed | tf_op | source)
XLA Modules:
  0.0 262.0 jit_solution(771684726575287990)
XLA Ops:
  0.6 0.8 reshape.106
  1.4 0.1 convert_element_type.63
  1.5 1.4 convert_add_fusion.small
  2.9 133.5 %shard_map.263 = (bf16[8,512,128]{2,1,0:T(8,128)(2,1)}, bf16[8,512,128]{2,1,0:T(8,128)(2,1)}, bf16[8,128,2048]{2,1,0:T(8,128)(2,1)}, bf16[8,256,1024]{2,1,0:T(8,...) custom-call(bf16[128,3072]{1,0:T(8,128)(2,1)} %qkv_w.1, ...), custom_call_target="tpu_custom_call" | custom-call | tf_op jit(solution)/shard_map/pallas_call | solution.py:482
  136.3 117.0 %shard_map.264 = (bf16[256,1024]{1,0:T(8,128)(2,1)}, f32[256,1024]{1,0:T(8,128)}, bf16[2,8,16,2048]{3,2,1,0:T(8,128)(2,1)}, bf16[2,8,32,1024]{3,2,1,0:T(8,128)(2...) custom-call(bf16[8,512,128]{2,1,0:T(8,128)(2,1)} %get-tuple-element.44.tokens_q, ...), custom_call_target="tpu_custom_call" | custom-call | tf_op jit(solution)/shard_map/pallas_call | solution.py:956
  253.3 6.3 %shard_map.265 = (f32[128,4096]{1,0:T(8,128)}, f32[512,1024]{1,0:T(8,128)}, f32[128,3072]{1,0:T(8,128)}, f32[128,1024]{1,0:T(8,128)}, bf16[256,1024]{1,0:T(8,128...) custom-call(bf16[2,8,16,2048]{3,2,1,0:T(8,128)(2,1)} %get-tuple-elem, ...), custom_call_target="tpu_custom_call" | custom-call | tf_op jit(solution)/shard_map/pallas_call | solution.py:1066
  259.6 1.3 reduce
  260.8 1.2 copy.31
  (2 shorter events, 0.0 us)

commit v4 on v3

--- a/solution.py
+++ b/solution.py
@@ -449,9 +449,9 @@
 
         return 0
 
-    lax.fori_loop(0, 1, query_block, 0)
+    lax.fori_loop(0, 3, query_block, 0)
     units.sides_y()
-    lax.fori_loop(1, n, query_block, 0)
+    lax.fori_loop(3, n, query_block, 0)
 
     lax.fori_loop(0, n, key_block, 0)
     keep_own(0).start()
@@ -544,18 +544,8 @@
             return g.at[pl.ds(2 * h, 2), t % 2, t // 2]
         return g.at[:, h, :, t]
     if stage == 1:
-        if n == 0:
-            return g.at[y, t % 2, t // 2, pl.ds(2 * h, 2)]
-        if n == 1:
-            return g.at[pl.ds(2 * h, 2), zl, zh, t]
-        return g.at[t, h, :, px]
-    half = g.shape[-1] // 2
-    columns = pl.ds(h * half, half)
-    if n == 0:
-        return g.at[y, zl, zh, t, :, columns]
-    if n == 1:
-        return g.at[t, zl, zh, px, :, columns]
-    return g.at[y, t % 2, t // 2, px, :, columns]
+        return (g.at[y, t % 2, t // 2], g.at[:, zl, zh, t], g.at[t, :, :, px])[n]
+    return (g.at[y, zl, zh, t], g.at[t, zl, zh, px], g.at[y, t % 2, t // 2, px])[n]
 
 
 def add_into(dst, terms):
@@ -587,13 +577,14 @@
 def rest_kernel(
     tokens_q, tokens_k, x, ct, an, mn, wq, wd, wh, wo, vec, cosine, sine,
     outputs, input_grad, gathered0, gathered1, gathered2, small_out,
-    tables, norms, unit_bias, x_v, ct_v, an_v, mn_v, branches, weighted, sums, small, sm_a, sm_b, pair_send, pair_recv,
+    tables, norms, unit_bias, x_v, ct_v, an_v, branches, weighted, sums, small, sm_a, sm_b, pair_send, pair_recv,
     g0, g1, g2, *rest,
 ):
     grads = (g0, g1, g2)
     gathered = (gathered0, gathered1, gathered2)
-    bufs = [(*rest[6 * n : 6 * n + 6], gathered[n]) for n in range(3)]
-    send, recv, local_sem, sm_send, sm_recv = rest[18:]
+    bufs = [(*rest[4 * n : 4 * n + 4], gathered[n]) for n in range(3)]
+    wq_v, wd_v, tq_v, tk_v, pg_v, at_v, wh_v, wo_v, act_v, hg_v, turned_v = rest[12:23]
+    send, recv, local_sem, sm_send, sm_recv = rest[23:]
     f, s, (y, zl, px, zh, core) = place()
     z = zh * 2 + zl
     coordinate = {"y": y, "z": z, "x": px}
@@ -634,19 +625,21 @@
     def small_arrived(ref, k):
         remote(ref, ref, sm_send.at[k], sm_recv.at[k], sibling).wait_recv()
 
-    def buffers(n, stage):
-        return bufs[n][2 * stage], bufs[n][2 * stage + 1]
-
     def raw_copies(n, stage):
         axis = ORDERS[n][stage]
         p = coordinate[axis]
-        opp, fin = buffers(n, stage)
-        b = 26 * n + 6 * stage
 
         def copy(t, h, dst, k, target):
             src = chunk(n, stage, grads[n], t % 4, h, where)
             return remote(src, dst, send.at[k], recv.at[k], target)
 
+        if stage > 0:
+            b, got = 26 * n + 3 + 3 * stage, bufs[n][1 + stage]
+            return [
+                copy(p + k, 0, got.at[k - 1], b + k - 1, along(axis, k)) for k in (2, 1, 3)
+            ]
+        opp, fin = bufs[n][0:2]
+        b = 26 * n
         return [
             copy(p + 2, 0, opp.at[0], b, plus[axis]),
             copy(p + 2, 1, opp.at[1], b + 1, minus[axis]),
@@ -654,43 +647,61 @@
             copy(p + 3, 0, fin.at[1, 0], b + 3, minus[axis]),
         ]
 
-    def relay_copy(n, stage, h):
-        axis = ORDERS[n][stage]
-        _, fin = buffers(n, stage)
-        k = 26 * n + 6 * stage + 4 + h
+    def relay_copy(n, h):
+        axis = ORDERS[n][0]
+        k = 26 * n + 4 + h
         t = coordinate[axis] + 1 + 2 * h
-        src = chunk(n, stage, grads[n], t % 4, h, where)
+        src = chunk(n, 0, grads[n], t % 4, h, where)
         target = (plus, minus)[h][axis]
-        return src, remote(src, fin.at[h, h], send.at[k], recv.at[k], target)
+        return src, remote(src, bufs[n][1].at[h, h], send.at[k], recv.at[k], target)
 
     def begin(n, stage):
         for copy in raw_copies(n, stage):
             copy.start()
 
-    def relay(n, stage):
-        opp, _ = buffers(n, stage)
+    def relay(n):
+        opp = bufs[n][0]
         for h in range(2):
-            mid, copy = relay_copy(n, stage, h)
-            arrived(opp.at[h], 26 * n + 6 * stage + h)
+            mid, copy = relay_copy(n, h)
+            arrived(opp.at[h], 26 * n + h)
             add_into(mid, [opp.at[h]])
             copy.start()
 
     def finish(n, stage):
         p = coordinate[ORDERS[n][stage]]
-        _, fin = buffers(n, stage)
-        b = 26 * n + 6 * stage
+        if stage > 0:
+            b, got = 26 * n + 3 + 3 * stage, bufs[n][1 + stage]
+            for k in range(3):
+                arrived(got.at[k], b + k)
+            mine = chunk(n, stage, grads[n], p, 0, where)
+            add_into(mine, [got.at[k] for k in range(3)])
+            return
+        fin = bufs[n][1]
+        b = 26 * n
         arrived(fin.at[0, 1], b + 2)
         arrived(fin.at[1, 0], b + 3)
         arrived(fin.at[0, 0], b + 4)
         arrived(fin.at[1, 1], b + 5)
         for h in range(2):
-            add_into(chunk(n, stage, grads[n], p, h, where), [fin.at[0, h], fin.at[1, h]])
-
-    keeps = [load(a, b, k) for k, (a, b) in enumerate([(x, x_v), (ct, ct_v), (an, an_v), (mn, mn_v)])]
+            add_into(chunk(n, 0, grads[n], p, h, where), [fin.at[0, h], fin.at[1, h]])
+
+    here = pl.ds(pl.multiple_of((px * 2 + zh) * T, T), T)
+    pairs = [
+        (tokens_q, tq_v),
+        (tokens_k, tk_v),
+        (cosine.at[here], tables.at[0]),
+        (sine.at[here], tables.at[1]),
+        (an, an_v),
+        (ct, ct_v),
+        (wh, wh_v),
+        (wo, wo_v),
+        (x, x_v),
+        (wq, wq_v),
+        (wd, wd_v),
+    ]
+    keeps = [load(a, b, k) for k, (a, b) in enumerate(pairs)]
     barrier(same_seq + same_fsdp + [zother])
     small[...] = jnp.zeros_like(small)
-    here = pl.ds(pl.multiple_of((px * 2 + zh) * T, T), T)
-    keeps += [load(cosine.at[here], tables.at[0], 12), load(sine.at[here], tables.at[1], 13)]
     for r in range(8):
         at = slice(r * 128, r * 128 + 128)
         norms[0:4, at] = vec[r, 0:4, :]
@@ -700,13 +711,9 @@
                 r, pl.ds(8 + 2 * core + j, 1), :
             ]
 
-    def attention_part(wq_v, wd_v, tq_v, tk_v, pg_v, at_v, turned_v):
-        loads = [load(a, b, 4 + k) for k, (a, b) in enumerate([(tokens_q, tq_v), (wq, wq_v), (wd, wd_v)])]
-        load_k = load(tokens_k, tk_v, 14)
-        for copy in keeps:
+    def attention_part():
+        for copy in keeps[0:6]:
             copy.wait()
-        loads[0].wait()
-        load_k.wait()
         low = lax.broadcasted_iota(jnp.int32, (T, 128), 1) < HEAD
         first = lax.broadcasted_iota(jnp.int32, (1, 128), 1) < HEAD
         rotary = (tables[0], tables[1])
@@ -734,11 +741,12 @@
             o = jnp.where(low, pltpu.roll(a, 64, 1), b)
             at_v[:, pair * 128 : pair * 128 + 128] = o.astype(BF16)
 
-        turned_v[...] = an_v[...].T
+        turned_v[0:D, :] = an_v[...].T
+        load_mn = load(mn, an_v, 11)
 
         def qkv_columns(k, _):
             at = pl.ds(pl.multiple_of(k * 512, 512), 512)
-            part = jnp.dot(turned_v[...], pg_v[:, at], preferred_element_type=F32)
+            part = jnp.dot(turned_v[0:D, :], pg_v[:, at], preferred_element_type=F32)
             g2[:, :, :, :, :, at] = part.astype(BF16).reshape(4, 2, 2, 4, 16, 512)
             return 0
 
@@ -750,34 +758,33 @@
             )
             g2[:, :, k, :, :, 1536:2048] = part.astype(BF16).reshape(4, 2, 4, 16, 512)
         begin(2, 0)
-        loads[1].wait()
-        loads[2].wait()
-        grad = lax.dot_general(pg_v[...], wq_v[...], NT, preferred_element_type=F32)
-        normed, _ = normalised(x_v[...])
-        sums[0:1, :] = jnp.sum(grad * normed, axis=0, keepdims=True)
-        sums[1:2, :] = jnp.sum(grad, axis=0, keepdims=True)
-        weighted[...] = grad * norms[0:1, :]
-        branches[...] = jnp.dot(at_v[...], wd_v[...], preferred_element_type=F32)
-
-    pl.run_scoped(
-        attention_part,
-        pltpu.VMEM((D, 1536), BF16),
-        pltpu.VMEM((512, D), BF16),
-        pltpu.VMEM((8, T, 128), BF16),
-        pltpu.VMEM((8, T, 128), BF16),
-        pltpu.VMEM((T, 1536), BF16),
-        pltpu.VMEM((T, 512), BF16),
-        pltpu.VMEM((D, T), BF16),
-    )
-
-    def unit_part(wh_v, wo_v, act_v, hg_v, turned_v):
-        loads = [load(a, b, 7 + k) for k, (a, b) in enumerate([(wh, wh_v), (wo, wo_v)])]
-        loads[0].wait()
-        loads[1].wait()
+        return load_mn
+
+    def attention_rows():
+        for copy in keeps[8:11]:
+            copy.wait()
+        sums[...] = jnp.zeros_like(sums)
+
+        def half(c, _):
+            rows = pl.ds(pl.multiple_of(c * 256, 256), 256)
+            grad = lax.dot_general(pg_v[rows, :], wq_v[...], NT, preferred_element_type=F32)
+            normed, _ = normalised(x_v[rows, :])
+            sums[0:1, :] += jnp.sum(grad * normed, axis=0, keepdims=True)
+            sums[1:2, :] += jnp.sum(grad, axis=0, keepdims=True)
+            weighted[rows, :] = grad * norms[0:1, :]
+            branches[rows, :] = jnp.dot(at_v[rows, :], wd_v[...], preferred_element_type=F32)
+            return 0
+
+        lax.fori_loop(0, 2, half, 0)
+
+    def unit_part(load_mn):
+        load_mn.wait()
+        for copy in keeps[6:8]:
+            copy.wait()
 
         def units(r, _):
             at = pl.ds(pl.multiple_of(r * 256, 256), 256)
-            h = jnp.dot(mn_v[...], wh_v[:, at], preferred_element_type=F32) + unit_bias[0:1, at]
+            h = jnp.dot(an_v[...], wh_v[:, at], preferred_element_type=F32) + unit_bias[0:1, at]
             below = 0.5 + 0.5 * lax.erf(h * math.sqrt(0.5))
             density = jnp.exp(-0.5 * h * h) * (1.0 / math.sqrt(2.0 * math.pi))
             act_v[:, at] = (h * below).astype(BF16)
@@ -800,7 +807,7 @@
 
         lax.fori_loop(0, 4, output_rows, 0)
         begin(1, 0)
-        turned_v[0:D, :] = mn_v[...].T
+        turned_v[0:D, :] = an_v[...].T
 
         def hidden_columns(k, _):
             at = pl.ds(pl.multiple_of(k * 512, 512), 512)
@@ -810,22 +817,24 @@
 
         lax.fori_loop(0, 4, hidden_columns, 0)
         begin(0, 0)
-        relay(2, 0)
-        grad = lax.dot_general(hg_v[...], wh_v[...], NT, preferred_element_type=F32)
-        normed, _ = normalised(x_v[...])
-        sums[2:3, :] = jnp.sum(grad * normed, axis=0, keepdims=True)
-        sums[3:4, :] = jnp.sum(grad, axis=0, keepdims=True)
-        weighted[...] += grad * norms[2:3, :]
-        branches[...] += jnp.dot(act_v[...], wo_v[...], preferred_element_type=F32)
-
-    pl.run_scoped(
-        unit_part,
-        pltpu.VMEM((D, 2048), BF16),
-        pltpu.VMEM((2048, D), BF16),
-        pltpu.VMEM((T, 2048), BF16),
-        pltpu.VMEM((T, 2048), BF16),
-        pltpu.VMEM((2048, T), BF16),
-    )
+
+    def unit_rows():
+        def half(c, _):
+            rows = pl.ds(pl.multiple_of(c * 256, 256), 256)
+            grad = lax.dot_general(hg_v[rows, :], wh_v[...], NT, preferred_element_type=F32)
+            normed, _ = normalised(x_v[rows, :])
+            sums[2:3, :] += jnp.sum(grad * normed, axis=0, keepdims=True)
+            sums[3:4, :] += jnp.sum(grad, axis=0, keepdims=True)
+            weighted[rows, :] += grad * norms[2:3, :]
+            branches[rows, :] += jnp.dot(act_v[rows, :], wo_v[...], preferred_element_type=F32)
+            return 0
+
+        lax.fori_loop(0, 2, half, 0)
+
+    unit_part(attention_part())
+    relay(2)
+    attention_rows()
+    unit_rows()
 
     other = pl.ds(pl.multiple_of((1 - core) * 256, 256), 256)
     mine = pl.ds(pl.multiple_of(core * 256, 256), 256)
@@ -839,8 +848,8 @@
         small[r, 7:8, :] = sums[4:5, at]
     for k in range(1, 8):
         small_sent(small.at[(f + k) % 8], sm_a.at[k], k, same_seq[k - 1])
-    relay(1, 0)
-    relay(0, 0)
+    relay(1)
+    relay(0)
     arrived(pair_recv, 78)
     normed, scale = normalised(x_v[mine, :])
     total = x_v[mine, :].astype(F32) + branches[mine, :] + pair_recv[0].astype(F32) + norms[4:5, :]
@@ -851,8 +860,6 @@
         - jnp.mean(w, axis=-1, keepdims=True)
         - normed * jnp.mean(w * normed, axis=-1, keepdims=True)
     )
-    finish(2, 0)
-    begin(2, 1)
     for k in range(1, 8):
         small_arrived(sm_a.at[k], k)
     total = small[f]
@@ -861,22 +868,18 @@
     sm_b[0] = total
     for k in range(1, 16):
         small_sent(sm_b.at[0], sm_b.at[k], 7 + k, same_fsdp[k - 1])
-    finish(1, 0)
-    begin(1, 1)
-    finish(0, 0)
-    begin(0, 1)
 
     across = device(y, (z + 2) % 4, px, core)
     xp, xm = plus["x"], minus["x"]
 
     def at_chip(n, zz, xx):
-        return bufs[n][6].at[core, zz * 4 + xx % 4]
+        return bufs[n][4].at[core, zz * 4 + xx % 4]
 
     def spread(n):
         b = 26 * n + 18
         done = grads[n].at[y, zl, zh, px]
         place_ = at_chip(n, zh, px)
-        keep = pltpu.make_async_copy(done, place_, local_sem.at[9 + n])
+        keep = pltpu.make_async_copy(done, place_, local_sem.at[12 + n])
         keep.start()
         started(done, place_, b, across)
         started(done, place_, b + 1, xp)
@@ -902,25 +905,33 @@
         arrived(at_chip(n, zh, px + 2), b + 5)
         arrived(at_chip(n, 1 - zh, px + 2), b + 6)
         keep.wait()
-        whole = bufs[n][6].at[core]
+        whole = bufs[n][4].at[core]
         started(whole, whole, b + 7, sibling)
 
-    order = (2, 1, 0)
-    for n in order:
-        relay(n, 1)
-    for n in order:
-        finish(n, 1)
-        begin(n, 2)
-    for n in order:
-        relay(n, 2)
-    copies = {}
-    for n in order:
-        finish(n, 2)
-        copies[n] = spread(n)
-    for n in order:
-        spread_on(n)
-    for n in order:
-        spread_end(n, copies[n])
+    finish(2, 0)
+    begin(2, 1)
+    finish(1, 0)
+    begin(1, 1)
+    finish(0, 0)
+    begin(0, 1)
+    finish(2, 1)
+    begin(2, 2)
+    finish(1, 1)
+    begin(1, 2)
+    finish(0, 1)
+    begin(0, 2)
+    finish(2, 2)
+    keep2 = spread(2)
+    finish(1, 2)
+    keep1 = spread(1)
+    finish(0, 2)
+    keep0 = spread(0)
+    spread_on(2)
+    spread_end(2, keep2)
+    spread_on(1)
+    spread_on(0)
+    spread_end(1, keep1)
+    spread_end(0, keep0)
     for k in range(1, 16):
         small_arrived(sm_b.at[k], 7 + k)
     total = sm_b[0]
@@ -928,7 +939,7 @@
         total = total + sm_b[k]
     small_out[...] = total
 
-    for n in order:
+    for n in (2, 1, 0):
         arrived(gathered[n].at[1 - core], 26 * n + 25)
     for copy in sends:
         copy.wait_send()
@@ -936,8 +947,8 @@
         for stage in range(3):
             for copy in raw_copies(n, stage):
                 copy.wait_send()
-            for h in range(2):
-                relay_copy(n, stage, h)[1].wait_send()
+        for h in range(2):
+            relay_copy(n, h)[1].wait_send()
 
 
 def rest_of_block(*args):
@@ -946,10 +957,8 @@
         for dims in (
             (2, *lead, R, C),
             (2, 2, *lead, R, C),
-            (2, 2, R, C),
-            (2, 2, 2, R, C),
-            (2, R, C // 2),
-            (2, 2, R, C // 2),
+            (3, *((2, 2) if lead == (4, 2) else (4,)), R, C),
+            (3, R, C),
         ):
             scratch.append(pltpu.VMEM(dims, BF16))
     T = CHIP_TOKENS
@@ -967,7 +976,7 @@
             pltpu.VMEM((2, T, 128), F32),
             pltpu.VMEM((8, D), F32),
             pltpu.VMEM((8, 2048), F32),
-            *[pltpu.VMEM((T, D), BF16)] * 4,
+            *[pltpu.VMEM((T, D), BF16)] * 3,
             *[pltpu.VMEM((T, D), F32)] * 2,
             pltpu.VMEM((8, D), F32),
             pltpu.VMEM((8, 16, 128), F32),
@@ -976,9 +985,18 @@
             *[pltpu.VMEM((2, 256, D), BF16)] * 2,
             *[pltpu.VMEM((4, 2, 2, 4, R, C), BF16) for R, C in zip(ROWS, COLUMNS)],
             *scratch,
+            pltpu.VMEM((D, 1536), BF16),
+            pltpu.VMEM((512, D), BF16),
+            *[pltpu.VMEM((8, T, 128), BF16)] * 2,
+            pltpu.VMEM((T, 1536), BF16),
+            pltpu.VMEM((T, 512), BF16),
+            pltpu.VMEM((D, 2048), BF16),
+            pltpu.VMEM((2048, D), BF16),
+            *[pltpu.VMEM((T, 2048), BF16)] * 2,
+            pltpu.VMEM((2048, T), BF16),
             pltpu.SemaphoreType.DMA((79,)),
             pltpu.SemaphoreType.DMA((79,)),
-            pltpu.SemaphoreType.DMA((16,)),
+            pltpu.SemaphoreType.DMA((18,)),
             pltpu.SemaphoreType.DMA((23,)),
             pltpu.SemaphoreType.DMA((23,)),
         ],

time: 262 us -> 253 us (0.966); the launches traced: 262 us -> 248 us
  Pallas kernels: 257 us -> 243 us
    pallas_call x1, Pallas kernels: 133 us -> 124 us  [attention(): pl.pallas_call(attention_kernel, out_shape=(shape(CHIPS, B, 2 * HEAD), sh...]
    pallas_call x1, Pallas kernels: 117 us -> 112 us  [rest_of_block(): pl.pallas_call(rest_kernel, out_shape=(jax.ShapeDtypeStruct((256, D), BF1...]
where the time goes in v4:
time: 253 us; the launch traced here: 248 us
  Pallas kernels  243 us (96%)
  other arithmetic  2.64 us (1%)
    pallas_call x1, Pallas kernels, attention(): pl.pallas_call(attention_kernel, out_shape=(shape(CHIPS, B, 2 * HEAD), sh...  124 us
    pallas_call x1, Pallas kernels, rest_of_block(): pl.pallas_call(rest_kernel, out_shape=(jax.ShapeDtypeStruct((256, D), BF1...  112 us
    pallas_call x1, Pallas kernels, finals(): pl.pallas_call(finals_kernel, out_shape=(jax.ShapeDtypeStruct((128, FF),...  6.26 us

profile of v4, /device:TPU:1, one launch (start us, length us, event | category | flops | bytes accessed | tf_op | source)
XLA Modules:
  0.0 248.3 jit_solution(6176620972282524708)
XLA Ops:
  0.6 0.8 reshape.106
  1.4 0.1 convert_element_type.63
  1.5 1.4 convert_add_fusion.small
  2.9 124.2 %shard_map.263 = (bf16[8,512,128]{2,1,0:T(8,128)(2,1)}, bf16[8,512,128]{2,1,0:T(8,128)(2,1)}, bf16[8,128,2048]{2,1,0:T(8,128)(2,1)}, bf16[8,256,1024]{2,1,0:T(8,...) custom-call(bf16[128,3072]{1,0:T(8,128)(2,1)} %qkv_w.1, ...), custom_call_target="tpu_custom_call" | custom-call | tf_op jit(solution)/shard_map/pallas_call | solution.py:482
  127.1 112.5 %shard_map.264 = (bf16[256,1024]{1,0:T(8,128)(2,1)}, f32[256,1024]{1,0:T(8,128)}, bf16[2,8,16,2048]{3,2,1,0:T(8,128)(2,1)}, bf16[2,8,32,1024]{3,2,1,0:T(8,128)(2...) custom-call(bf16[8,512,128]{2,1,0:T(8,128)(2,1)} %get-tuple-element.44.tokens_q, ...), custom_call_target="tpu_custom_call" | custom-call | tf_op jit(solution)/shard_map/pallas_call | solution.py:965
  239.6 6.3 %shard_map.265 = (f32[128,4096]{1,0:T(8,128)}, f32[512,1024]{1,0:T(8,128)}, f32[128,3072]{1,0:T(8,128)}, f32[128,1024]{1,0:T(8,128)}, bf16[256,1024]{1,0:T(8,128...) custom-call(bf16[2,8,16,2048]{3,2,1,0:T(8,128)(2,1)} %get-tuple-elem, ...), custom_call_target="tpu_custom_call" | custom-call | tf_op jit(solution)/shard_map/pallas_call | solution.py:1084
  245.8 1.3 reduce
  247.1 1.2 copy.31
  (2 shorter events, 0.0 us)

commit v5 on v4

--- a/solution.py
+++ b/solution.py
@@ -1029,7 +1029,7 @@
 def finals_kernel(
     h0, h1, h2, out_in, grad_in, sums, hidden, output, qkv, dense, out_ref, grad_ref, *rest
 ):
-    vectors, (a0, a1, a2, sem) = rest[:7], rest[7:]
+    vectors, (a0, a1, a2, sem) = rest[:8], rest[8:]
     loads = [
         pltpu.make_async_copy(a, b, sem.at[k])
         for k, (a, b) in enumerate(
@@ -1075,12 +1075,13 @@
     vectors[4][:, 128:256] = jnp.where(first, sums[6:7, :], q1)
     vectors[4][:, 256:384] = jnp.where(first, q1, sums[6:7, :])
     vectors[5][...] = sums[7:8, :]
+    vectors[7][...] = sums[7:8, :]
     for k in range(4):
         vectors[6][:, k * 128 : k * 128 + 128] = sums[8 + k : 9 + k, :]
 
 
 def finals(a0, a1, a2, outputs, input_grad, sums):
-    widths = (128, 128, 128, 128, 384, 128, 512)
+    widths = (128, 128, 128, 128, 384, 128, 512, 128)
     return pl.pallas_call(
         finals_kernel,
         out_shape=(
@@ -1093,7 +1094,7 @@
             *[jax.ShapeDtypeStruct((1, w), F32) for w in widths],
         ),
         in_specs=[HBM] * 5 + [VMEM],
-        out_specs=(VMEM,) * 13,
+        out_specs=(VMEM,) * 14,
         scratch_shapes=[
             *[pltpu.VMEM((2, 8, R, C), BF16) for R, C in zip(ROWS, COLUMNS)],
             pltpu.SemaphoreType.DMA((5,)),
@@ -1163,8 +1164,8 @@
     hidden, output, qkv, dense, outputs, input_grad, *vectors = finals(
         *gathered, outputs, input_grad, sums
     )
-    ag, ab, mg, mb, qb, db, hb = (v.reshape(v.shape[1]) for v in vectors)
-    return (outputs, input_grad, ag, ab, mg, mb, qkv, qb, dense, db, hidden, hb, output, db)
+    ag, ab, mg, mb, qb, db, hb, ob = (v.reshape(v.shape[1]) for v in vectors)
+    return (outputs, input_grad, ag, ab, mg, mb, qkv, qb, dense, db, hidden, hb, output, ob)
 
 
 def solution(mesh):

time: 253 us -> 252 us (level)
  no operation moved by 1% of the time
where the time goes in v5:
time: 252 us; the launch traced here: 247 us
  Pallas kernels  243 us (96%)
  other arithmetic  2.64 us (1%)
    pallas_call x1, Pallas kernels, attention(): pl.pallas_call(attention_kernel, out_shape=(shape(CHIPS, B, 2 * HEAD), sh...  124 us
    pallas_call x1, Pallas kernels, rest_of_block(): pl.pallas_call(rest_kernel, out_shape=(jax.ShapeDtypeStruct((256, D), BF1...  112 us
    pallas_call x1, Pallas kernels, finals(): pl.pallas_call(finals_kernel, out_shape=(jax.ShapeDtypeStruct((128, FF),...  6.27 us

profile of v5, /device:TPU:1, one launch (start us, length us, event | category | flops | bytes accessed | tf_op | source)
XLA Modules:
  0.0 247.1 jit_solution(3580795662714347776)
XLA Ops:
  0.6 0.8 reshape.109
  1.4 0.1 convert_element_type.63
  1.5 1.4 convert_add_fusion.small
  2.9 124.2 %shard_map.263 = (bf16[8,512,128]{2,1,0:T(8,128)(2,1)}, bf16[8,512,128]{2,1,0:T(8,128)(2,1)}, bf16[8,128,2048]{2,1,0:T(8,128)(2,1)}, bf16[8,256,1024]{2,1,0:T(8,...) custom-call(bf16[128,3072]{1,0:T(8,128)(2,1)} %qkv_w.1, ...), custom_call_target="tpu_custom_call" | custom-call | tf_op jit(solution)/shard_map/pallas_call | solution.py:482
  127.1 112.5 %shard_map.264 = (bf16[256,1024]{1,0:T(8,128)(2,1)}, f32[256,1024]{1,0:T(8,128)}, bf16[2,8,16,2048]{3,2,1,0:T(8,128)(2,1)}, bf16[2,8,32,1024]{3,2,1,0:T(8,128)(2...) custom-call(bf16[8,512,128]{2,1,0:T(8,128)(2,1)} %get-tuple-element.45.tokens_q, ...), custom_call_target="tpu_custom_call" | custom-call | tf_op jit(solution)/shard_map/pallas_call | solution.py:965
  239.6 6.3 %shard_map.265 = (f32[128,4096]{1,0:T(8,128)}, f32[512,1024]{1,0:T(8,128)}, f32[128,3072]{1,0:T(8,128)}, f32[128,1024]{1,0:T(8,128)}, bf16[256,1024]{1,0:T(8,128...) custom-call(bf16[2,8,16,2048]{3,2,1,0:T(8,128)(2,1)} %get-tuple-elem, ...), custom_call_target="tpu_custom_call" | custom-call | tf_op jit(solution)/shard_map/pallas_call | solution.py:1085
  245.8 1.3 reduce
  (2 shorter events, 0.0 us)
